TPU v7x, 32 devices: a whole 2x2x4 slice. The times are simulated.
32 devices in a mesh: inb: 4 (over y, x), hid: 8 (over z, core).
Axes of the slice: x: 2, y: 2, z: 4, core: 2. Of those that a mesh axis runs over, the one named last changes fastest.
Arguments:
- activations: bfloat16 [2, 512, 4096], P(None, 'hid', 'inb'), may hold values from -40 to 40
- out_grads: bfloat16 [2, 512, 8192], P(None, 'inb', 'hid'), may hold values from -1 to 1
- basis_in: bfloat16 [4096, 1024], P('inb', 'hid'), may hold values from -0.1875 to 0.1875
- basis_out: bfloat16 [8192, 1024], P('hid', 'inb'), may hold values from -0.1875 to 0.1875
Outputs:
- precond: bfloat16 [4096, 8192], P('inb', 'hid')
All inputs are finite; a program needn't handle non-finite values.
Results may differ from a plain program's by a relative error of at most 0.0058.
Values may be sent and summed in bfloat16 or wider, within the bound.
No kernel may reach another device: no remote copies, remote signals or barrier semaphores. Data moves between devices by JAX's collectives and lax.ppermute only.
A program may use at most 64 MiB of HBM per device.

v0:
```python
import jax
import jax.numpy as jnp
from jax import lax
from jax.sharding import PartitionSpec as P

damping = 0.1


def square_round(values):
    widened = values.astype(jnp.float32)
    return (widened * widened).astype(jnp.bfloat16)


def contract_tokens(left_side, right_side):
    return lax.dot_general(
        left_side, right_side, (((0, 1), (0, 1)), ((), ())), preferred_element_type=jnp.float32
    )


def on_device(activations, out_grads, basis_in, basis_out):
    width_block = basis_in.shape[0]
    grads_flat = out_grads.reshape(-1, width_block)
    grads_rot = (
        jnp.dot(
            grads_flat,
            lax.all_gather(basis_out, "inb", axis=1, tiled=True),
            preferred_element_type=jnp.float32,
        )
        .astype(jnp.bfloat16)
        .reshape(out_grads.shape)
    )
    basis_whole = lax.all_gather(basis_in, "hid", axis=1, tiled=True)
    grads_full = lax.all_gather(grads_rot, "inb", axis=1, tiled=True)
    grads_squared = square_round(grads_full)
    plain_rows = lax.all_gather(activations, "hid", axis=1, tiled=True)
    rotated = (
        jnp.dot(
            plain_rows.reshape(-1, width_block), basis_whole, preferred_element_type=jnp.float32
        )
        .astype(jnp.bfloat16)
        .reshape(plain_rows.shape)
    )
    grad_sum = contract_tokens(rotated, grads_full)
    fisher_sum = contract_tokens(square_round(rotated), grads_squared)
    return (grad_sum / (fisher_sum + damping)).astype(jnp.bfloat16)


def solution(mesh):
    return jax.shard_map(
        on_device,
        mesh=mesh,
        in_specs=(P(None, "hid", "inb"), P(None, "inb", "hid"), P("inb", "hid"), P("hid", "inb")),
        out_specs=P("inb", "hid"),
        check_vma=False,
    )
```

profile of v0, /device:TPU:0, one launch (start us, length us, event | category | flops | bytes accessed | tf_op | source)
XLA Modules:
  0.0 160.3 jit_solution(2904652703219293035)
XLA Ops:
  6.5 0.0 copy-start
  6.5 0.0 all-gather.9.cloned.1.call-start
  6.5 0.7 all-gather.9.cloned.1.call-update
  7.3 0.0 all-gather.5.cloned.1.call-start
  7.3 0.7 all-gather.5.cloned.1.call-update
  8.0 0.0 all-gather.7.cloned.1.call-start
  8.1 0.7 all-gather.7.cloned.1.call-update
  8.7 0.0 all-gather.11.cloned.1.call-start
  8.8 38.3 %all-gather.9.cloned.1.call-done = bf16[1024,1024]{1,0:T(8,128)(2,1)} async-done(((bf16[1024,256]{1,0:T(8,128)(2,1)}), bf16[1024,1024]{1,0:T(8,128)(2,1)}) %all-gather.9.cloned.1.call-update) | async-done | bytes 2097168 | tf_op jit(solution)/shard_map/all_gather | solution.py:26
  47.1 0.0 copy-done
  47.1 3.1 %convolution_convert_fusion.1 = bf16[256,1024]{1,0:T(8,128)(2,1)} fusion(bf16[256,1024]{1,0:T(8,128)(2,1)S(1)} %bitcast.18, bf16[1024,1024]{1,0:T(8,128)(2,1)} %all-gather.9.cloned.1.call-done), kind=kOutput, calls=%fused_computation.6 | convolution fusion | flops 537133056 | bytes 3145728 | tf_op jit(solution)/shard_map/dot_general | solution.py:24
  50.2 0.0 all-gather.11.cloned.1.call-update
  50.2 27.6 %all-gather.5.cloned.1.call-done = bf16[2,512,1024]{2,1,0:T(8,128)(2,1)} async-done(((bf16[2,64,1024]{2,1,0:T(8,128)(2,1)}), bf16[2,512,1024]{2,1,0:T(8,128)(2,1)}) %all-gather.5.cloned.1.call-update) | async-done | bytes 2097168 | tf_op jit(solution)/shard_map/all_gather | solution.py:35
  77.8 32.0 %all-gather.7.cloned.1.call-done = bf16[1024,1024]{1,0:T(8,128)(2,1)} async-done(((bf16[1024,128]{1,0:T(8,128)(2,1)}), bf16[1024,1024]{1,0:T(8,128)(2,1)}) %all-gather.7.cloned.1.call-update) | async-done | bytes 2097168 | tf_op jit(solution)/shard_map/all_gather | solution.py:32
  109.8 4.5 %convolution_convert_fusion = bf16[1024,1024]{1,0:T(8,128)(2,1)S(1)} fusion(bf16[1024,1024]{1,0:T(8,128)(2,1)} %bitcast.22, bf16[1024,1024]{1,0:T(8,128)(2,1)} %all-gather.7.cloned.1.call-done), kind=kOutput, calls=%fused_computation.5 | convolution fusion | flops 2148532224 | bytes 6291456 | tf_op jit(solution)/shard_map/dot_general | solution.py:37
  114.3 2.6 %copy.6 = bf16[2,512,1024]{1,2,0:T(8,128)(2,1)} copy(bf16[2,512,1024]{2,1,0:T(8,128)(2,1)S(1)} %bitcast.19) | data formatting | bytes 4194304 | tf_op jit(solution)/shard_map/reshape | solution.py:41
  116.9 29.0 %all-gather.11.cloned.1.call-done = bf16[2,512,1024]{2,1,0:T(8,128)(2,1)} async-done(((bf16[2,128,1024]{2,1,0:T(8,128)(2,1)}), bf16[2,512,1024]{2,1,0:T(8,128)(2,1)}) %all-gather.11.cloned.1.call-update) | async-done | bytes 2097168 | tf_op jit(solution)/shard_map/all_gather | solution.py:33
  145.9 0.0 copy-start.1
  145.9 0.0 copy-start.2
  145.9 4.1 %fusion.2 = f32[1024,1024,1]{1,0,2:T(8,128)S(1)} fusion(bf16[2,512,1024]{2,1,0:T(8,128)(2,1)S(1)} %bitcast.20, bf16[2,512,1024]{2,1,0:T(8,128)(2,1)} %all-gather.11.cloned.1.call-done), kind=kOutput, calls=%fused_computation.7 | convolution fusion | flops 2147483648 | bytes 8388608 | tf_op jit(solution)/shard_map/dot_general | solution.py:15
  150.0 0.0 copy-done.1
  150.1 0.0 copy-done.2
  150.1 3.8 %fusion.1 = bf16[1024,1024]{1,0:T(8,128)(2,1)} fusion(f32[1024,1024,1]{1,0,2:T(8,128)S(1)} %fusion.2, bf16[2,512,1024]{1,2,0:T(8,128)(2,1)S(1)} %copy-done.1, bf16[2,512,1024]{2,1,0:T(8,128)(2,1)S(1)} %copy-done.2), kind=kOutput, calls=%fused_computation.2 | convolution fusion | flops 2156920832 | bytes 10485760 | tf_op jit(solution)/shard_map/dot_general | solution.py:15
Async XLA Ops:
  6.5 40.6 %copy-start = (bf16[2,128,1024]{2,1,0:T(8,128)(2,1)S(1)}, bf16[2,128,1024]{2,1,0:T(8,128)(2,1)}, u32[]{:S(2)}) copy-start(bf16[2,128,1024]{2,1,0:T(8,128)(2,1)} %param.5) | copy-start | bytes 1572868
  6.5 40.5 %all-gather.9.cloned.1.call-start = ((), (), s32[]{:S(2)}) async-start(), calls=%async_computation.2 | async-start | bytes 2621440 | tf_op jit(solution)/shard_map/all_gather | solution.py:26
  7.3 70.6 %all-gather.5.cloned.1.call-start = ((), (), s32[]{:S(2)}) async-start(), calls=%async_computation | async-start | bytes 2359296 | tf_op jit(solution)/shard_map/all_gather | solution.py:35
  8.0 101.8 %all-gather.7.cloned.1.call-start = ((), (), s32[]{:S(2)}) async-start(), calls=%async_computation.1 | async-start | bytes 2359296 | tf_op jit(solution)/shard_map/all_gather | solution.py:32
  8.7 137.2 %all-gather.11.cloned.1.call-start = ((), (), s32[]{:S(2)}) async-start(), calls=%async_computation.3 | async-start | bytes 2621440 | tf_op jit(solution)/shard_map/all_gather | solution.py:33
  145.9 4.1 %copy-start.1 = (bf16[2,512,1024]{1,2,0:T(8,128)(2,1)S(1)}, bf16[2,512,1024]{1,2,0:T(8,128)(2,1)}, u32[]{:S(2)}) copy-start(bf16[2,512,1024]{1,2,0:T(8,128)(2,1)} %copy.6) | copy-start | bytes 6291460
  145.9 4.1 %copy-start.2 = (bf16[2,512,1024]{2,1,0:T(8,128)(2,1)S(1)}, bf16[2,512,1024]{2,1,0:T(8,128)(2,1)}, u32[]{:S(2)}) copy-start(bf16[2,512,1024]{2,1,0:T(8,128)(2,1)} %all-gather.11.cloned.1.call-done) | copy-start | bytes 6291460
Sparse Core Ops, SparseCore 0:
  9.2 37.8 all-gather.8
  48.7 29.0 all-gather.4
  79.4 30.3 all-gather.6
  111.5 34.3 all-gather.10
where the time goes:
time: 160 us
  waiting for transfers between devices  129 us (81%)
  matrix products  15.5 us (10%)
  between operations  13.2 us (8%)
  local copies, waits for them, and re-layouts  2.57 us (2%)
    all_gather x1, waiting for transfers between devices, on_device(): lax.all_gather(basis_out, 'inb', axis=1, tiled=True)  38.3 us
    all_gather x1, waiting for transfers between devices, on_device(): basis_whole = lax.all_gather(basis_in, 'hid', axis=1, tiled=True)  32 us
    all_gather x1, waiting for transfers between devices, on_device(): grads_full = lax.all_gather(grads_rot, 'inb', axis=1, tiled=True)  29 us
    all_gather x1, waiting for transfers between devices, on_device(): plain_rows = lax.all_gather(activations, 'hid', axis=1, tiled=True)  27.6 us
    dot_general x2, matrix products, contract_tokens(): lax.dot_general(left_side, right_side, (((0, 1), (0, 1)), ((), ())), pref...  7.87 us
    dot_general x1, matrix products, on_device(): jnp.dot(plain_rows.reshape(-1, width_block), basis_whole, preferred_eleme...  4.55 us
  transfers between devices with their start and end apart: 4, of which 4 were waited for; matrix products, arithmetic and copies ran while one was open for 6% of the time, Pallas kernels for 0%

commit v1 on v0

--- a/solution.py
+++ b/solution.py
@@ -1,6 +1,8 @@
 import jax
 import jax.numpy as jnp
 from jax import lax
+from jax.experimental import pallas as pl
+from jax.experimental.pallas import tpu as pltpu
 from jax.sharding import PartitionSpec as P
 
 damping = 0.1
@@ -17,7 +19,7 @@
     )
 
 
-def on_device(activations, out_grads, basis_in, basis_out):
+def gathered(activations, out_grads, basis_in, basis_out):
     width_block = basis_in.shape[0]
     grads_flat = out_grads.reshape(-1, width_block)
     grads_rot = (
@@ -45,9 +47,175 @@
     return (grad_sum / (fisher_sum + damping)).astype(jnp.bfloat16)
 
 
+def swap(values, axis, count, distance):
+    return lax.ppermute(values, axis, [(i, i ^ distance) for i in range(count)])
+
+
+def rows_of(index, size):
+    return pl.ds(pl.multiple_of(index * size, size), size)
+
+
+def rotate_out_kernel(run, own_ref, near_ref, basis_ref, far_ref, tile_ref):
+    index = lax.axis_index("inb")
+    low, high = lax.rem(index, 2), index // 2
+    micro, tokens, depth = own_ref.shape
+    width = basis_ref.shape[1]
+    for grads_ref, place in ((own_ref, low), (near_ref, 1 - low)):
+        grads = grads_ref[...].reshape(micro * tokens, depth)
+        for weights_ref, column in ((basis_ref, high), (far_ref, 1 - high)):
+            part = jnp.dot(grads, weights_ref[...], preferred_element_type=jnp.float32)
+            part = part.astype(jnp.bfloat16)
+            for m in range(micro):
+                for k in range(tokens // run):
+                    here = m * tokens + k * run
+                    row = place * (micro * tokens) + (k * micro + m) * run
+                    tile_ref[
+                        pl.ds(pl.multiple_of(row, run), run), rows_of(column, width)
+                    ] = part[here : here + run]
+
+
+def rotate_in_kernel(own_ref, core_ref, near_ref, near_core_ref, basis_ref, far_ref, tile_ref, weights):
+    index = lax.axis_index("hid")
+    core, low, high = lax.rem(index, 2), lax.rem(index // 2, 2), index // 4
+    micro, tokens, depth = own_ref.shape
+    width = basis_ref.shape[1]
+    weights[:, rows_of(high, width)] = basis_ref[...]
+    weights[:, rows_of(1 - high, width)] = far_ref[...]
+    for acts_ref, place in (
+        (own_ref, 2 * low + core),
+        (core_ref, 2 * low + 1 - core),
+        (near_ref, 2 * (1 - low) + core),
+        (near_core_ref, 2 * (1 - low) + 1 - core),
+    ):
+        acts = acts_ref[...].reshape(micro * tokens, depth)
+        part = jnp.dot(acts, weights[...], preferred_element_type=jnp.float32)
+        tile_ref[:, rows_of(place, micro * tokens)] = part.astype(jnp.bfloat16).T
+
+
+def final_kernel(
+    t0, t1, t2, t3, t4, s0, s1, s2, s3, g0, g1, g2, g3, out_ref, left, right, right_squared
+):
+    @pl.when(pl.program_id(0) == 0)
+    def _():
+        index = lax.axis_index("hid")
+        core, low, high = lax.rem(index, 2), lax.rem(index // 2, 2), index // 4
+        width, span = t0.shape[0] // 2, t0.shape[1]
+        inner = low != high
+        t3_value = jnp.where(inner, t3[...], t4[...])
+        for piece, dl, dh, dc in (
+            (t0[...], 0, 0, 0), (t1[...], 1, 0, 0), (t2[...], 0, 1, 0), (t3_value, 1, 1, 0),
+            (s0[...], 0, 0, 1), (s1[...], 1, 0, 1), (s2[...], 0, 1, 1), (s3[...], 1, 1, 1),
+        ):
+            piece_low = low if dl == 0 else 1 - low
+            piece_high = high if dh == 0 else 1 - high
+            piece_core = core if dc == 0 else 1 - core
+            for k in range(2):
+                row = 4 * k + 2 * piece_low + piece_core
+                left[rows_of(row, width), rows_of(piece_high, span)] = piece[k * width : (k + 1) * width]
+        index = lax.axis_index("inb")
+        low, high = lax.rem(index, 2), index // 2
+        span, width = g0.shape[0], g0.shape[1] // 2
+        for piece, dl, dh in ((g0, 0, 0), (g1, 1, 0), (g2, 0, 1), (g3, 1, 1)):
+            piece_low = low if dl == 0 else 1 - low
+            piece_high = high if dh == 0 else 1 - high
+            for k in range(2):
+                values = piece[:, k * width : (k + 1) * width]
+                at = (rows_of(piece_high, span), rows_of(2 * k + piece_low, width))
+                right[at] = values
+                right_squared[at] = values * values
+
+    block = out_ref.shape[0]
+    rows = left[rows_of(pl.program_id(0), block), :]
+    grad = jnp.dot(rows, right[...], preferred_element_type=jnp.float32)
+    fisher = jnp.dot(rows * rows, right_squared[...], preferred_element_type=jnp.float32)
+    out_ref[...] = (grad / (fisher + damping)).astype(jnp.bfloat16)
+
+
+def paired(n_inb, n_hid, activations, out_grads, basis_in, basis_out):
+    vmem = pl.BlockSpec(memory_space=pltpu.VMEM)
+    params = pltpu.CompilerParams(vmem_limit_bytes=40 * 1024 * 1024)
+    low_in, high_in = n_hid // 4, n_hid // 2
+    low_out, high_out = n_inb // 4, n_inb // 2
+
+    def hid(values, distance):
+        return swap(values, "hid", n_hid, distance)
+
+    def inb(values, distance):
+        return swap(values, "inb", n_inb, distance)
+
+    acts_core = hid(activations, 1)
+    basis_far = hid(basis_in, high_in)
+    acts_near = hid(activations, low_in)
+    grads_near = inb(out_grads, low_out)
+    basis_out_far = inb(basis_out, high_out)
+    acts_near_core = hid(acts_near, 1)
+
+    micro, tin, _ = activations.shape
+    tout = out_grads.shape[1]
+    t0 = pl.pallas_call(
+        rotate_in_kernel,
+        out_shape=jax.ShapeDtypeStruct((2 * basis_in.shape[1], 4 * micro * tin), jnp.bfloat16),
+        in_specs=[vmem] * 6,
+        out_specs=vmem,
+        scratch_shapes=[pltpu.VMEM((basis_in.shape[0], 2 * basis_in.shape[1]), jnp.bfloat16)],
+        compiler_params=params,
+    )(activations, acts_core, acts_near, acts_near_core, basis_in, basis_far)
+    g0 = pl.pallas_call(
+        lambda *refs: rotate_out_kernel(tin, *refs),
+        out_shape=jax.ShapeDtypeStruct((2 * micro * tout, 2 * basis_out.shape[1]), jnp.bfloat16),
+        in_specs=[vmem] * 4,
+        out_specs=vmem,
+        compiler_params=params,
+    )(out_grads, grads_near, basis_out, basis_out_far)
+
+    t2 = hid(t0, high_in)
+    t1 = hid(t0, low_in)
+    g1 = inb(g0, low_out)
+    g2 = inb(g0, high_out)
+    s0 = hid(t0, 1)
+    s1 = hid(t1, 1)
+    s2 = hid(t2, 1)
+    chips = n_hid // 2
+    inner = [(2 * z + c, 2 * (chips - 1 - z) + c) for z in range(1, chips - 1) for c in range(2)]
+    outer = [(2 * z + c, 2 * (z ^ 1) + c) for z in range(1, chips - 1) for c in range(2)]
+    t3 = lax.ppermute(t0, "hid", inner)
+    t4 = lax.ppermute(t2, "hid", outer)
+    core = lax.rem(lax.axis_index("hid"), 2)
+    onward = []
+    for h in range(n_hid):
+        step = high_out if h % 2 == 0 else low_out
+        onward += [(i * n_hid + h, (i ^ step) * n_hid + h) for i in range(n_inb)]
+    g3 = lax.ppermute(jnp.where(core == 0, g1, g2), ("inb", "hid"), onward)
+    zone = lax.axis_index("hid") // 2
+    is_inner = (zone > 0) & (zone < chips - 1)
+    s3 = hid(jnp.where(is_inner, t3, t4), 1)
+
+    rows, columns = activations.shape[2], out_grads.shape[2]
+    steps = 4
+    whole = lambda v: pl.BlockSpec(v.shape, lambda r: (0, 0))
+    pieces = (t0, t1, t2, t3, t4, s0, s1, s2, s3, g0, g1, g2, g3)
+    total = t0.shape[1] * 2
+    return pl.pallas_call(
+        final_kernel,
+        grid=(steps,),
+        out_shape=jax.ShapeDtypeStruct((rows, columns), jnp.bfloat16),
+        in_specs=[vmem for v in pieces],
+        out_specs=pl.BlockSpec((rows // steps, columns), lambda r: (r, 0)),
+        scratch_shapes=[
+            pltpu.VMEM((rows, total), jnp.bfloat16),
+            pltpu.VMEM((total, columns), jnp.bfloat16),
+            pltpu.VMEM((total, columns), jnp.bfloat16),
+        ],
+        compiler_params=params,
+    )(*pieces)
+
+
 def solution(mesh):
+    n_inb, n_hid = mesh.shape["inb"], mesh.shape["hid"]
+    two_by_two = n_inb == 2 * 2 and n_hid == 2 * n_inb
+    body = (lambda *a: paired(n_inb, n_hid, *a)) if two_by_two else gathered
     return jax.shard_map(
-        on_device,
+        body,
         mesh=mesh,
         in_specs=(P(None, "hid", "inb"), P(None, "inb", "hid"), P("inb", "hid"), P("hid", "inb")),
         out_specs=P("inb", "hid"),

time: 160 us -> 55.2 us (0.35)
  waiting for transfers between devices: 129 us -> 24.6 us
  starting transfers between devices: 0.12 us -> 19.3 us
  matrix products: 15.5 us -> 0 us
  between operations: 13.2 us -> 0.11 us
  Pallas kernels: 0 us -> 8.02 us
    all_gather x4 -> x0, waiting for transfers between devices: 127 us -> none  [the longest x1 38.3 us: on_device(): lax.all_gather(basis_out, 'inb', axis=1, tiled=True)]
    ppermute x0 -> x17, waiting for transfers between devices: none -> 24.6 us  [the longest x14 17.8 us: swap(): return lax.ppermute(values, axis, [(i, i ^ distance) for i in range(count)])]
    ppermute x0 -> x17, starting transfers between devices: none -> 19.3 us  [the longest x14 16.9 us: swap(): return lax.ppermute(values, axis, [(i, i ^ distance) for i in range(count)])]
    dot_general x4 -> x0, matrix products: 15.5 us -> none  [the longest x2 7.87 us: contract_tokens(): lax.dot_general(left_side, right_side, (((0, 1), (0, 1)), ((), ())), pref...]
    pallas_call x0 -> x3, Pallas kernels: none -> 8.02 us  [the longest x1 6.66 us: paired(): pl.pallas_call(final_kernel, grid=(steps,), out_shape=jax.ShapeDtypeStruc...]
    reshape x1 -> x0, local copies, waits for them, and re-layouts: 2.56 us -> none  [on_device(): rotated = jnp.dot(plain_rows.reshape(-1, width_block), basis_whole, prefe...]
    unnamed x4 -> x0, waiting for transfers between devices: 2.1 us -> none
    unnamed x6 -> x8, local copies, waits for them, and re-layouts: 0.01 us -> 2.09 us
  transfers between devices with their start and end apart: 4 -> 17, of which waited for: 4 -> 6; matrix products, arithmetic and copies ran while one was open for 6% -> 2% of each run, Pallas kernels for 0% -> 2%
where the time goes in v1:
time: 55.2 us; the launch traced here: 55 us
  waiting for transfers between devices  24.6 us (45%)
  starting transfers between devices  19.3 us (35%)
  Pallas kernels  8.02 us (15%)
  local copies, waits for them, and re-layouts  2.09 us (4%)
  other arithmetic  0.88 us (2%)
    ppermute x14, waiting for transfers between devices, swap(): return lax.ppermute(values, axis, [(i, i ^ distance) for i in range(count)])  17.8 us
    ppermute x14, starting transfers between devices, swap(): return lax.ppermute(values, axis, [(i, i ^ distance) for i in range(count)])  16.9 us
    ppermute x1, waiting for transfers between devices, paired(): t4 = lax.ppermute(t2, 'hid', outer)  6.76 us
    pallas_call x1, Pallas kernels, paired(): pl.pallas_call(final_kernel, grid=(steps,), out_shape=jax.ShapeDtypeStruc...  6.66 us
    unnamed x8, local copies, waits for them, and re-layouts  2.09 us
    ppermute x1, starting transfers between devices, paired(): t4 = lax.ppermute(t2, 'hid', outer)  1.28 us
  transfers between devices with their start and end apart: 17, of which 6 were waited for; matrix products, arithmetic and copies ran while one was open for 2% of the time, Pallas kernels for 2%

profile of v1, /device:TPU:0, one launch (start us, length us, event | category | flops | bytes accessed | tf_op | source)
XLA Modules:
  0.0 55.0 jit_solution(17375007656871369323)
XLA Ops:
  0.0 2.9 %collective-permute-start.12 = (bf16[2,128,1024]{2,1,0:T(8,128)(2,1)}, bf16[2,128,1024]{2,1,0:T(8,128)(2,1)S(1)}, u32[]{:S(2)}, u32[]{:S(2)}) collective-permute-start(bf16[2,128,1024]{2,1,0:T(8,128)(2,1)} %refs_0_.1), channel_id=1, source_target_pairs={{0,8},{8,0},{16,24},{24,16},{1,9},{9,1},{17,25},{25,17},{2,10},{10... | collective-permute-start | bytes 1572872 | tf_op jit(solution)/shard_map/ppermute | solution.py:51
  2.9 1.5 %collective-permute-start.13 = (bf16[1024,256]{1,0:T(8,128)(2,1)}, bf16[1024,256]{1,0:T(8,128)(2,1)S(1)}, u32[]{:S(2)}, u32[]{:S(2)}) collective-permute-start(bf16[1024,256]{1,0:T(8,128)(2,1)} %refs_2_.1), channel_id=1, source_target_pairs={{0,16},{8,24},{16,0},{24,8},{1,17},{9,25},{17,1},{25,9},{2,18},{10... | collective-permute-start | bytes 1572872 | tf_op jit(solution)/shard_map/ppermute | solution.py:51
  4.5 1.6 %collective-permute-start.1 = (bf16[2,64,1024]{2,1,0:T(8,128)(2,1)}, bf16[2,64,1024]{2,1,0:T(8,128)(2,1)S(1)}, u32[]{:S(2)}, u32[]{:S(2)}) collective-permute-start(bf16[2,64,1024]{2,1,0:T(8,128)(2,1)} %own_ref.1), channel_id=1, source_target_pairs={{0,2},{1,3},{2,0},{3,1},{4,6},{5,7},{6,4},{7,5},{8,10},{9,11},{10,... | collective-permute-start | bytes 786440 | tf_op jit(solution)/shard_map/ppermute | solution.py:51
  6.0 0.0 collective-permute-start
  6.0 2.6 %collective-permute-start.3 = (bf16[1024,128]{1,0:T(8,128)(2,1)}, bf16[1024,128]{1,0:T(8,128)(2,1)S(1)}, u32[]{:S(2)}, u32[]{:S(2)}) collective-permute-start(bf16[1024,128]{1,0:T(8,128)(2,1)} %basis_ref.1), channel_id=1, source_target_pairs={{0,4},{1,5},{2,6},{3,7},{4,0},{5,1},{6,2},{7,3},{8,12},{9,13},{10,... | collective-permute-start | bytes 786440 | tf_op jit(solution)/shard_map/ppermute | solution.py:51
  8.6 7.5 %collective-permute-done.1.near_ref = bf16[2,64,1024]{2,1,0:T(8,128)(2,1)S(1)} collective-permute-done((bf16[2,64,1024]{2,1,0:T(8,128)(2,1)}, bf16[2,64,1024]{2,1,0:T(8,128)(2,1)S(1)}, u32[]{:S(2)}, u32[]{:S(2)}) %collective-permute-start.1) | collective-permute-done | bytes 262176 | tf_op jit(solution)/shard_map/ppermute | solution.py:51
  16.1 0.0 collective-permute-start.2
  16.1 0.0 collective-permute-done.12.refs_1_
  16.2 0.4 collective-permute-done.13.refs_3_
  16.5 0.0 copy-start
  16.5 1.0 %copy-done = bf16[2,128,1024]{2,1,0:T(8,128)(2,1)S(1)} copy-done((bf16[2,128,1024]{2,1,0:T(8,128)(2,1)S(1)}, bf16[2,128,1024]{2,1,0:T(8,128)(2,1)}, u32[]{:S(2)}) %copy-start) | copy-done | bytes 524312
  17.6 0.0 copy-start.1
  17.6 1.0 %copy-done.1 = bf16[1024,256]{1,0:T(8,128)(2,1)S(1)} copy-done((bf16[1024,256]{1,0:T(8,128)(2,1)S(1)}, bf16[1024,256]{1,0:T(8,128)(2,1)}, u32[]{:S(2)}) %copy-start.1) | copy-done | bytes 524312
  18.6 0.0 copy-start.2
  18.6 0.0 copy-start.3
  18.6 0.7 %shard_map.47.g0 = bf16[512,512]{1,0:T(8,128)(2,1)S(1)} custom-call(bf16[2,128,1024]{2,1,0:T(8,128)(2,1)S(1)} %copy-done, bf16[2,128,1024]{2,1,0:T(8,128)(2,1)S(1)} %collective-permute-done.12.refs_1_, bf16[1024,256]{1,0:T(8,128)(2,1)S(1)} %copy-done.1, bf16[1024,256]{1,0:T(8,128)(2,1)S(1)} %collective-permute-done.13.refs_3_), custom_call_target="tpu_custom_call" | custom-call | tf_op jit(solution)/shard_map/pallas_call | solution.py:163
  19.3 1.6 %collective-permute-start.15 = (bf16[512,512]{1,0:T(8,128)(2,1)S(1)}, bf16[512,512]{1,0:T(8,128)(2,1)S(1)}, u32[]{:S(2)}, u32[]{:S(2)}) collective-permute-start(bf16[512,512]{1,0:T(8,128)(2,1)S(1)} %shard_map.47.g0), channel_id=1, source_target_pairs={{0,16},{8,24},{16,0},{24,8},{1,17},{9,25},{17,1},{25,9},{2,18},{10... | collective-permute-start | bytes 1572872 | tf_op jit(solution)/shard_map/ppermute | solution.py:51
  20.9 0.5 collective-permute-start.14
  21.5 0.1 collective-permute-done.3.far_ref
  21.5 0.0 collective-permute-done.core_ref
  21.5 0.0 collective-permute-done.2.near_core_ref
  21.5 0.0 copy-done.2
  21.5 0.0 copy-done.3
  21.6 0.6 %shard_map.46.t0 = bf16[256,512]{1,0:T(8,128)(2,1)S(1)} custom-call(bf16[2,64,1024]{2,1,0:T(8,128)(2,1)S(1)} %copy-done.2, bf16[2,64,1024]{2,1,0:T(8,128)(2,1)S(1)} %collective-permute-done.core_ref, bf16[2,64,1024]{2,1,0:T(8,128)(2,1)S(1)} %collective-permute-done.1.near_ref, bf16[2,64,1024]{2,1,0:T(8,128)(2,1)S(1)} %collective-permute-done.2.near_core_ref, ...), custom_call_target="tpu_custom_call" | custom-call | tf_op jit(solution)/shard_map/pallas_call | solution.py:155
  22.2 2.6 %collective-permute-start.5 = (bf16[256,512]{1,0:T(8,128)(2,1)S(1)}, bf16[256,512]{1,0:T(8,128)(2,1)S(1)}, u32[]{:S(2)}, u32[]{:S(2)}) collective-permute-start(bf16[256,512]{1,0:T(8,128)(2,1)S(1)} %shard_map.46.t0), channel_id=1, source_target_pairs={{0,4},{1,5},{2,6},{3,7},{4,0},{5,1},{6,2},{7,3},{8,12},{9,13},{10,... | collective-permute-start | bytes 786440 | tf_op jit(solution)/shard_map/ppermute | solution.py:51
  24.8 0.7 %collective-permute-start.6 = (bf16[256,512]{1,0:T(8,128)(2,1)S(1)}, bf16[256,512]{1,0:T(8,128)(2,1)S(1)}, u32[]{:S(2)}, u32[]{:S(2)}) collective-permute-start(bf16[256,512]{1,0:T(8,128)(2,1)S(1)} %shard_map.46.t0), channel_id=1, source_target_pairs={{2,4},{3,5},{4,2},{5,3},{10,12},{11,13},{12,10},{13,11},{18,20},{1... | collective-permute-start | bytes 786440 | tf_op jit(solution)/shard_map/ppermute | solution.py:181
  25.5 2.9 %collective-permute-start.4 = (bf16[256,512]{1,0:T(8,128)(2,1)S(1)}, bf16[256,512]{1,0:T(8,128)(2,1)S(1)}, u32[]{:S(2)}, u32[]{:S(2)}) collective-permute-start(bf16[256,512]{1,0:T(8,128)(2,1)S(1)} %shard_map.46.t0), channel_id=1, source_target_pairs={{0,2},{1,3},{2,0},{3,1},{4,6},{5,7},{6,4},{7,5},{8,10},{9,11},{10,... | collective-permute-start | bytes 786440 | tf_op jit(solution)/shard_map/ppermute | solution.py:51
  28.4 8.3 %collective-permute-done.5.t2 = bf16[256,512]{1,0:T(8,128)(2,1)S(1)} collective-permute-done((bf16[256,512]{1,0:T(8,128)(2,1)S(1)}, bf16[256,512]{1,0:T(8,128)(2,1)S(1)}, u32[]{:S(2)}, u32[]{:S(2)}) %collective-permute-start.5) | collective-permute-done | bytes 262176 | tf_op jit(solution)/shard_map/ppermute | solution.py:51
  36.7 1.3 %collective-permute-start.7 = (bf16[256,512]{1,0:T(8,128)(2,1)S(1)}, bf16[256,512]{1,0:T(8,128)(2,1)S(1)}, u32[]{:S(2)}, u32[]{:S(2)}) collective-permute-start(bf16[256,512]{1,0:T(8,128)(2,1)S(1)} %collective-permute-done.5.t2), channel_id=1, source_target_pairs={{2,0},{3,1},{4,6},{5,7},{10,8},{11,9},{12,14},{13,15},{18,16},{19,... | collective-permute-start | bytes 786440 | tf_op jit(solution)/shard_map/ppermute | solution.py:182
  38.0 0.0 collective-permute-done.15.g2
  38.0 0.0 collective-permute-done.14.g1
  38.0 0.9 %broadcast_select_fusion = bf16[512,512]{1,0:T(8,128)(2,1)} fusion(bf16[512,512]{1,0:T(8,128)(2,1)S(1)} %collective-permute-done.14.g1, bf16[512,512]{1,0:T(8,128)(2,1)S(1)} %collective-permute-done.15.g2, pred[]{:T(512)S(6)} %eq.3), kind=kLoop, calls=%fused_computation | loop fusion | flops 262144 | bytes 1572865 | tf_op jit(solution)/shard_map/jit(_where)/select_n | solution.py:188
  38.9 0.5 collective-permute-start.16
  39.4 0.0 collective-permute-start.8
  39.4 0.0 collective-permute-done.6.t3
  39.4 0.5 collective-permute-start.10
  39.9 0.0 collective-permute-done.4.t1
  39.9 0.1 collective-permute-start.9
  40.0 6.8 %collective-permute-done.7.t4 = bf16[256,512]{1,0:T(8,128)(2,1)S(1)} collective-permute-done((bf16[256,512]{1,0:T(8,128)(2,1)S(1)}, bf16[256,512]{1,0:T(8,128)(2,1)S(1)}, u32[]{:S(2)}, u32[]{:S(2)}) %collective-permute-start.7) | collective-permute-done | bytes 262176 | tf_op jit(solution)/shard_map/ppermute | solution.py:182
  46.8 0.1 collective-permute-start.11
  46.8 0.0 collective-permute-done.8.s0
  46.8 0.0 collective-permute-done.10.s2
  46.9 0.0 collective-permute-done.9.s1
  46.9 1.5 %collective-permute-done.11.s3 = bf16[256,512]{1,0:T(8,128)(2,1)S(1)} collective-permute-done((bf16[256,512]{1,0:T(8,128)(2,1)S(1)}, bf16[256,512]{1,0:T(8,128)(2,1)S(1)}, u32[]{:S(2)}, u32[]{:S(2)}) %collective-permute-start.11) | collective-permute-done | bytes 262176 | tf_op jit(solution)/shard_map/ppermute | solution.py:51
  48.4 0.0 collective-permute-done.16.g3
  48.4 6.7 %shard_map.48 = bf16[1024,1024]{1,0:T(8,128)(2,1)} custom-call(bf16[256,512]{1,0:T(8,128)(2,1)S(1)} %shard_map.46.t0, bf16[256,512]{1,0:T(8,128)(2,1)S(1)} %collective-permute-done.4.t1, bf16[256,512]{1,0:T(8,128)(2,1)S(1)} %collective-permute-done.5.t2, bf16[256,512]{1,0:T(8,128)(2,1)S(1)} %collective-permute-done.6.t3, ...), custom_call_target="tpu_custom_call" | custom-call | tf_op jit(solution)/shard_map/pallas_call | solution.py:198
  (1 shorter events, 0.0 us)
Async XLA Ops:
  0.0 16.1 %collective-permute-start.12 = (bf16[2,128,1024]{2,1,0:T(8,128)(2,1)}, bf16[2,128,1024]{2,1,0:T(8,128)(2,1)S(1)}, u32[]{:S(2)}, u32[]{:S(2)}) collective-permute-start(bf16[2,128,1024]{2,1,0:T(8,128)(2,1)} %refs_0_.1), channel_id=1, source_target_pairs={{0,8},{8,0},{16,24},{24,16},{1,9},{9,1},{17,25},{25,17},{2,10},{10... | collective-permute-start | bytes 1572872 | tf_op jit(solution)/shard_map/ppermute | solution.py:51
  2.9 13.6 %collective-permute-start.13 = (bf16[1024,256]{1,0:T(8,128)(2,1)}, bf16[1024,256]{1,0:T(8,128)(2,1)S(1)}, u32[]{:S(2)}, u32[]{:S(2)}) collective-permute-start(bf16[1024,256]{1,0:T(8,128)(2,1)} %refs_2_.1), channel_id=1, source_target_pairs={{0,16},{8,24},{16,0},{24,8},{1,17},{9,25},{17,1},{25,9},{2,18},{10... | collective-permute-start | bytes 1572872 | tf_op jit(solution)/shard_map/ppermute | solution.py:51
  4.5 11.7 %collective-permute-start.1 = (bf16[2,64,1024]{2,1,0:T(8,128)(2,1)}, bf16[2,64,1024]{2,1,0:T(8,128)(2,1)S(1)}, u32[]{:S(2)}, u32[]{:S(2)}) collective-permute-start(bf16[2,64,1024]{2,1,0:T(8,128)(2,1)} %own_ref.1), channel_id=1, source_target_pairs={{0,2},{1,3},{2,0},{3,1},{4,6},{5,7},{6,4},{7,5},{8,10},{9,11},{10,... | collective-permute-start | bytes 786440 | tf_op jit(solution)/shard_map/ppermute | solution.py:51
  6.0 15.5 %collective-permute-start = (bf16[2,64,1024]{2,1,0:T(8,128)(2,1)}, bf16[2,64,1024]{2,1,0:T(8,128)(2,1)S(1)}, u32[]{:S(2)}, u32[]{:S(2)}) collective-permute-start(bf16[2,64,1024]{2,1,0:T(8,128)(2,1)} %own_ref.1), channel_id=1, source_target_pairs={{0,1},{1,0},{2,3},{3,2},{4,5},{5,4},{6,7},{7,6},{8,9},{9,8},{10,11... | collective-permute-start | bytes 786440 | tf_op jit(solution)/shard_map/ppermute | solution.py:51
  6.0 15.5 %collective-permute-start.3 = (bf16[1024,128]{1,0:T(8,128)(2,1)}, bf16[1024,128]{1,0:T(8,128)(2,1)S(1)}, u32[]{:S(2)}, u32[]{:S(2)}) collective-permute-start(bf16[1024,128]{1,0:T(8,128)(2,1)} %basis_ref.1), channel_id=1, source_target_pairs={{0,4},{1,5},{2,6},{3,7},{4,0},{5,1},{6,2},{7,3},{8,12},{9,13},{10,... | collective-permute-start | bytes 786440 | tf_op jit(solution)/shard_map/ppermute | solution.py:51
  16.1 5.4 %collective-permute-start.2 = (bf16[2,64,1024]{2,1,0:T(8,128)(2,1)S(1)}, bf16[2,64,1024]{2,1,0:T(8,128)(2,1)S(1)}, u32[]{:S(2)}, u32[]{:S(2)}) collective-permute-start(bf16[2,64,1024]{2,1,0:T(8,128)(2,1)S(1)} %collective-permute-done.1.near_ref), channel_id=1, source_target_pairs={{0,1},{1,0},{2,3},{3,2},{4,5},{5,4},{6,7},{7,6},{8,9},{9,8},{10,11... | collective-permute-start | bytes 786440 | tf_op jit(solution)/shard_map/ppermute | solution.py:51
  16.5 1.0 %copy-start = (bf16[2,128,1024]{2,1,0:T(8,128)(2,1)S(1)}, bf16[2,128,1024]{2,1,0:T(8,128)(2,1)}, u32[]{:S(2)}) copy-start(bf16[2,128,1024]{2,1,0:T(8,128)(2,1)} %refs_0_.1) | copy-start | bytes 1572868
  17.6 1.0 %copy-start.1 = (bf16[1024,256]{1,0:T(8,128)(2,1)S(1)}, bf16[1024,256]{1,0:T(8,128)(2,1)}, u32[]{:S(2)}) copy-start(bf16[1024,256]{1,0:T(8,128)(2,1)} %refs_2_.1) | copy-start | bytes 1572868
  18.6 2.9 %copy-start.2 = (bf16[2,64,1024]{2,1,0:T(8,128)(2,1)S(1)}, bf16[2,64,1024]{2,1,0:T(8,128)(2,1)}, u32[]{:S(2)}) copy-start(bf16[2,64,1024]{2,1,0:T(8,128)(2,1)} %own_ref.1) | copy-start | bytes 786436
  18.6 2.9 %copy-start.3 = (bf16[1024,128]{1,0:T(8,128)(2,1)S(1)}, bf16[1024,128]{1,0:T(8,128)(2,1)}, u32[]{:S(2)}) copy-start(bf16[1024,128]{1,0:T(8,128)(2,1)} %basis_ref.1) | copy-start | bytes 786436
  19.3 18.7 %collective-permute-start.15 = (bf16[512,512]{1,0:T(8,128)(2,1)S(1)}, bf16[512,512]{1,0:T(8,128)(2,1)S(1)}, u32[]{:S(2)}, u32[]{:S(2)}) collective-permute-start(bf16[512,512]{1,0:T(8,128)(2,1)S(1)} %shard_map.47.g0), channel_id=1, source_target_pairs={{0,16},{8,24},{16,0},{24,8},{1,17},{9,25},{17,1},{25,9},{2,18},{10... | collective-permute-start | bytes 1572872 | tf_op jit(solution)/shard_map/ppermute | solution.py:51
  20.9 17.1 %collective-permute-start.14 = (bf16[512,512]{1,0:T(8,128)(2,1)S(1)}, bf16[512,512]{1,0:T(8,128)(2,1)S(1)}, u32[]{:S(2)}, u32[]{:S(2)}) collective-permute-start(bf16[512,512]{1,0:T(8,128)(2,1)S(1)} %shard_map.47.g0), channel_id=1, source_target_pairs={{0,8},{8,0},{16,24},{24,16},{1,9},{9,1},{17,25},{25,17},{2,10},{10... | collective-permute-start | bytes 1572872 | tf_op jit(solution)/shard_map/ppermute | solution.py:51
  22.2 14.5 %collective-permute-start.5 = (bf16[256,512]{1,0:T(8,128)(2,1)S(1)}, bf16[256,512]{1,0:T(8,128)(2,1)S(1)}, u32[]{:S(2)}, u32[]{:S(2)}) collective-permute-start(bf16[256,512]{1,0:T(8,128)(2,1)S(1)} %shard_map.46.t0), channel_id=1, source_target_pairs={{0,4},{1,5},{2,6},{3,7},{4,0},{5,1},{6,2},{7,3},{8,12},{9,13},{10,... | collective-permute-start | bytes 786440 | tf_op jit(solution)/shard_map/ppermute | solution.py:51
  24.8 14.6 %collective-permute-start.6 = (bf16[256,512]{1,0:T(8,128)(2,1)S(1)}, bf16[256,512]{1,0:T(8,128)(2,1)S(1)}, u32[]{:S(2)}, u32[]{:S(2)}) collective-permute-start(bf16[256,512]{1,0:T(8,128)(2,1)S(1)} %shard_map.46.t0), channel_id=1, source_target_pairs={{2,4},{3,5},{4,2},{5,3},{10,12},{11,13},{12,10},{13,11},{18,20},{1... | collective-permute-start | bytes 786440 | tf_op jit(solution)/shard_map/ppermute | solution.py:181
  25.5 14.4 %collective-permute-start.4 = (bf16[256,512]{1,0:T(8,128)(2,1)S(1)}, bf16[256,512]{1,0:T(8,128)(2,1)S(1)}, u32[]{:S(2)}, u32[]{:S(2)}) collective-permute-start(bf16[256,512]{1,0:T(8,128)(2,1)S(1)} %shard_map.46.t0), channel_id=1, source_target_pairs={{0,2},{1,3},{2,0},{3,1},{4,6},{5,7},{6,4},{7,5},{8,10},{9,11},{10,... | collective-permute-start | bytes 786440 | tf_op jit(solution)/shard_map/ppermute | solution.py:51
  36.7 10.0 %collective-permute-start.7 = (bf16[256,512]{1,0:T(8,128)(2,1)S(1)}, bf16[256,512]{1,0:T(8,128)(2,1)S(1)}, u32[]{:S(2)}, u32[]{:S(2)}) collective-permute-start(bf16[256,512]{1,0:T(8,128)(2,1)S(1)} %collective-permute-done.5.t2), channel_id=1, source_target_pairs={{2,0},{3,1},{4,6},{5,7},{10,8},{11,9},{12,14},{13,15},{18,16},{19,... | collective-permute-start | bytes 786440 | tf_op jit(solution)/shard_map/ppermute | solution.py:182
  38.9 9.5 %collective-permute-start.16 = (bf16[512,512]{1,0:T(8,128)(2,1)}, bf16[512,512]{1,0:T(8,128)(2,1)S(1)}, u32[]{:S(2)}, u32[]{:S(2)}) collective-permute-start(bf16[512,512]{1,0:T(8,128)(2,1)} %broadcast_select_fusion), channel_id=1, source_target_pairs={{0,16},{8,24},{16,0},{24,8},{1,9},{9,1},{17,25},{25,17},{2,18},{10... | collective-permute-start | bytes 1572872 | tf_op jit(solution)/shard_map/ppermute | solution.py:188
  39.4 7.5 %collective-permute-start.8 = (bf16[256,512]{1,0:T(8,128)(2,1)S(1)}, bf16[256,512]{1,0:T(8,128)(2,1)S(1)}, u32[]{:S(2)}, u32[]{:S(2)}) collective-permute-start(bf16[256,512]{1,0:T(8,128)(2,1)S(1)} %shard_map.46.t0), channel_id=1, source_target_pairs={{0,1},{1,0},{2,3},{3,2},{4,5},{5,4},{6,7},{7,6},{8,9},{9,8},{10,11... | collective-permute-start | bytes 786440 | tf_op jit(solution)/shard_map/ppermute | solution.py:51
  39.4 7.5 %collective-permute-start.10 = (bf16[256,512]{1,0:T(8,128)(2,1)S(1)}, bf16[256,512]{1,0:T(8,128)(2,1)S(1)}, u32[]{:S(2)}, u32[]{:S(2)}) collective-permute-start(bf16[256,512]{1,0:T(8,128)(2,1)S(1)} %collective-permute-done.5.t2), channel_id=1, source_target_pairs={{0,1},{1,0},{2,3},{3,2},{4,5},{5,4},{6,7},{7,6},{8,9},{9,8},{10,11... | collective-permute-start | bytes 786440 | tf_op jit(solution)/shard_map/ppermute | solution.py:51
  39.9 7.0 %collective-permute-start.9 = (bf16[256,512]{1,0:T(8,128)(2,1)S(1)}, bf16[256,512]{1,0:T(8,128)(2,1)S(1)}, u32[]{:S(2)}, u32[]{:S(2)}) collective-permute-start(bf16[256,512]{1,0:T(8,128)(2,1)S(1)} %collective-permute-done.4.t1), channel_id=1, source_target_pairs={{0,1},{1,0},{2,3},{3,2},{4,5},{5,4},{6,7},{7,6},{8,9},{9,8},{10,11... | collective-permute-start | bytes 786440 | tf_op jit(solution)/shard_map/ppermute | solution.py:51
  46.8 1.6 %collective-permute-start.11 = (bf16[256,512]{1,0:T(8,128)(2,1)S(1)}, bf16[256,512]{1,0:T(8,128)(2,1)S(1)}, u32[]{:S(2)}, u32[]{:S(2)}) collective-permute-start(bf16[256,512]{1,0:T(8,128)(2,1)S(1)} %broadcast_select_fusion.1), channel_id=1, source_target_pairs={{0,1},{1,0},{2,3},{3,2},{4,5},{5,4},{6,7},{7,6},{8,9},{9,8},{10,11... | collective-permute-start | bytes 786440 | tf_op jit(solution)/shard_map/ppermute | solution.py:51

commit v2 on v0

--- a/solution.py
+++ b/solution.py
@@ -1,6 +1,8 @@
 import jax
 import jax.numpy as jnp
 from jax import lax
+from jax.experimental import pallas as pl
+from jax.experimental.pallas import tpu as pltpu
 from jax.sharding import PartitionSpec as P
 
 damping = 0.1
@@ -17,7 +19,7 @@
     )
 
 
-def on_device(activations, out_grads, basis_in, basis_out):
+def gathered(activations, out_grads, basis_in, basis_out):
     width_block = basis_in.shape[0]
     grads_flat = out_grads.reshape(-1, width_block)
     grads_rot = (
@@ -45,9 +47,313 @@
     return (grad_sum / (fisher_sum + damping)).astype(jnp.bfloat16)
 
 
+def swap(values, axis, count, distance):
+    return lax.ppermute(values, axis, [(i, i ^ distance) for i in range(count)])
+
+
+def rows_of(index, size):
+    return pl.ds(pl.multiple_of(index * size, size), size)
+
+
+def hid_digits():
+    index = lax.axis_index("hid")
+    return index // 4, lax.rem(index // 2, 2), lax.rem(index, 2)
+
+
+def inb_digits():
+    index = lax.axis_index("inb")
+    return index // 2, lax.rem(index, 2)
+
+
+def other_tokens():
+    return lax.rem(hid_digits()[1] + inb_digits()[1], 2)
+
+
+def dot(a, b):
+    return jnp.dot(a, b, preferred_element_type=jnp.float32)
+
+
+def fetch_kernel(*refs):
+    count = len(refs) // 2
+    copies = [pltpu.make_async_copy(refs[k], refs[count + k], refs[-1].at[k]) for k in range(count)]
+    for copy in copies:
+        copy.start()
+    for copy in copies:
+        copy.wait()
+
+
+def rotate_out_kernel(run, own_ref, near_ref, basis_ref, far_ref, tile_ref, weights):
+    tok, col = inb_digits()
+    micro, tokens, depth = own_ref.shape
+    width = basis_ref.shape[1]
+    weights[:, rows_of(col, width)] = basis_ref[...]
+    weights[:, rows_of(1 - col, width)] = far_ref[...]
+    for grads_ref, place in ((own_ref, tok), (near_ref, 1 - tok)):
+        part = dot(grads_ref[...].reshape(micro * tokens, depth), weights[...]).astype(jnp.bfloat16)
+        for m in range(micro):
+            for k in range(tokens // run):
+                here = m * tokens + k * run
+                row = place * (micro * tokens) + (k * micro + m) * run
+                tile_ref[pl.ds(pl.multiple_of(row, run), run), :] = part[here : here + run]
+
+
+def join_kernel(basis_ref, far_ref, weights):
+    col = hid_digits()[1]
+    width = basis_ref.shape[1]
+    weights[:, rows_of(col, width)] = basis_ref[...]
+    weights[:, rows_of(1 - col, width)] = far_ref[...]
+
+
+def rotate_in_kernel(own_ref, core_ref, near_ref, near_core_ref, weights, tile_ref):
+    tok, _, core = hid_digits()
+    micro, tokens, depth = own_ref.shape
+    for acts_ref, place in (
+        (own_ref, 2 * tok + core),
+        (core_ref, 2 * tok + 1 - core),
+        (near_ref, 2 * (1 - tok) + core),
+        (near_core_ref, 2 * (1 - tok) + 1 - core),
+    ):
+        acts = acts_ref[...].reshape(micro * tokens, depth)
+        part = dot(acts, weights[...])
+        tile_ref[:, rows_of(place, micro * tokens)] = part.astype(jnp.bfloat16).T
+
+
+def pick_kernel(which, a_ref, b_ref, out_ref):
+    first = which()
+
+    @pl.when(first)
+    def _():
+        out_ref[...] = a_ref[...]
+
+    @pl.when(jnp.logical_not(first))
+    def _():
+        out_ref[...] = b_ref[...]
+
+
+def copy_kernel(a_ref, out_ref):
+    out_ref[...] = a_ref[...]
+
+
+def is_first_core():
+    return hid_digits()[2] == 0
+
+
+def is_inner_chip():
+    tok, col, _ = hid_digits()
+    return tok != col
+
+
+def early_kernel(t0, t1, t2, s0, s1, s2, g0, g1, g2, ready, grad, fisher, left, right, side):
+    other = other_tokens()
+    size, span = t0.shape
+    for k, (t, t_far, t_side) in enumerate(((t0, t2, t1), (s0, s2, s1))):
+        at = slice(k * size, (k + 1) * size)
+        left[at, :span] = t[...]
+        left[at, span:] = t_far[...]
+        side[at] = t_side[...]
+    right[rows_of(other, span), :] = g0[...]
+    right[rows_of(1 - other, span), :] = g2[...]
+    whole, below = right[...], g1[...]
+    whole_squared, below_squared = whole * whole, below * below
+    for k in range(2):
+        at = slice(k * size, (k + 1) * size)
+        rows = left[at]
+        g = dot(rows, whole)
+        f = dot(rows * rows, whole_squared)
+        ready[at] = (g / (f + damping)).astype(jnp.bfloat16)
+        rows = left[at, rows_of(other, span)]
+        grad[0, at] = dot(rows, below)
+        fisher[0, at] = dot(rows * rows, below_squared)
+        rows = side[at]
+        grad[1, at] = dot(rows, whole[:span])
+        fisher[1, at] = dot(rows * rows, whole_squared[:span])
+
+    @pl.when(other == 0)
+    def _():
+        for k in range(2):
+            at = slice(k * size, (k + 1) * size)
+            rows = side[at]
+            grad[2, at] = dot(rows, below)
+            fisher[2, at] = dot(rows * rows, below_squared)
+
+
+def late_kernel(ready, grad, fisher, left, right, side, g1, t3, s3, g3, out_ref, done, sems):
+    tok, col, core = hid_digits()
+    out_tok, _ = inb_digits()
+    other = other_tokens()
+    size, span = t3.shape
+    row_size, width = size // 2, ready.shape[1]
+    copies = []
+
+    def send(quadrant, part, source, row_tok, column_tok):
+        for k in range(2):
+            row = 4 * row_tok + 2 * k + (core if part == 0 else 1 - core)
+            copy = pltpu.make_async_copy(
+                source.at[pl.ds(part * size + k * row_size, row_size), :],
+                out_ref.at[rows_of(row, row_size), rows_of(column_tok, width)],
+                sems.at[4 * quadrant + 2 * part + k],
+            )
+            copy.start()
+            copies.append(copy)
+
+    def divided(quadrant, at, g, f):
+        done[quadrant, at] = (g / (f + damping)).astype(jnp.bfloat16)
+
+    for part in range(2):
+        send(3, part, ready, tok, out_tok)
+    below, beside = g3[...], right[span:]
+    below_squared, beside_squared = below * below, beside * beside
+    parts = [(slice(k * size, (k + 1) * size), k, t) for k, t in enumerate((t3, s3))]
+    for at, k, _ in parts:
+        rows = left[at, rows_of(1 - other, span)]
+        divided(0, at, grad[0, at] + dot(rows, below), fisher[0, at] + dot(rows * rows, below_squared))
+        send(0, k, done.at[0], tok, 1 - out_tok)
+    for at, k, t in parts:
+        rows = t[...]
+        divided(1, at, grad[1, at] + dot(rows, beside), fisher[1, at] + dot(rows * rows, beside_squared))
+        send(1, k, done.at[1], 1 - tok, out_tok)
+
+    @pl.when(other == 0)
+    def _():
+        for at, _, t in parts:
+            rows = t[...]
+            divided(2, at, grad[2, at] + dot(rows, below), fisher[2, at] + dot(rows * rows, below_squared))
+
+    @pl.when(other == 1)
+    def _():
+        last = g1[...]
+        last_squared = last * last
+        for at, _, t in parts:
+            rows, near = t[...], side[at]
+            g = dot(rows, last) + dot(near, below)
+            f = dot(rows * rows, last_squared) + dot(near * near, below_squared)
+            divided(2, at, g, f)
+
+    for part in range(2):
+        send(2, part, done.at[2], 1 - tok, 1 - out_tok)
+    for copy in copies:
+        copy.wait()
+
+
+def paired(n_inb, n_hid, activations, out_grads, basis_in, basis_out):
+    vmem, anywhere = pl.BlockSpec(memory_space=pltpu.VMEM), pl.BlockSpec(memory_space=pl.ANY)
+    params = pltpu.CompilerParams(vmem_limit_bytes=24 * 1024 * 1024)
+    bf16, f32 = jnp.bfloat16, jnp.float32
+    shape = jax.ShapeDtypeStruct
+
+    def hid(values, distance):
+        return swap(values, "hid", n_hid, distance)
+
+    def inb(values, distance):
+        return swap(values, "inb", n_inb, distance)
+
+    tok_in, col_in = n_hid // 2, n_hid // 4
+    tok_out, col_out = n_inb // 2, n_inb // 4
+
+    def call(kernel, outs, operands, scratch=(), flops=0, space=vmem, out_space=vmem):
+        one = not isinstance(outs, list)
+        return pl.pallas_call(
+            kernel,
+            out_shape=outs,
+            in_specs=[space] * len(operands),
+            out_specs=out_space if one else [out_space] * len(outs),
+            scratch_shapes=scratch,
+            compiler_params=params,
+            cost_estimate=pl.CostEstimate(flops=flops, bytes_accessed=0, transcendentals=0),
+        )(*operands)
+
+    acts_near = hid(activations, tok_in)
+    basis_far = hid(basis_in, col_in)
+    grads_near = inb(out_grads, tok_out)
+    basis_out_far = inb(basis_out, col_out)
+    acts_core = hid(activations, 1)
+
+    own = (out_grads, basis_out, activations, basis_in)
+    own_grads, own_basis_out, own_acts, own_basis_in = call(
+        fetch_kernel,
+        [shape(v.shape, v.dtype) for v in own],
+        own,
+        [pltpu.SemaphoreType.DMA((len(own),))],
+        space=anywhere,
+    )
+    acts_near, own_acts, own_grads = lax.optimization_barrier((acts_near, own_acts, own_grads))
+    acts_near_core = hid(acts_near, 1)
+
+    micro, tin, depth = activations.shape
+    tout = out_grads.shape[1]
+    rows_out, width_out = micro * tout, basis_out.shape[1]
+    rows_in, width_in = micro * tin, basis_in.shape[1]
+    tile_in, tile_out = (2 * width_in, 4 * rows_in), (2 * rows_out, 2 * width_out)
+    weights = call(join_kernel, shape((depth, 2 * width_in), bf16), (own_basis_in, basis_far), flops=4000000000)
+    t0 = call(
+        rotate_in_kernel,
+        shape(tile_in, bf16),
+        (own_acts, acts_core, acts_near, acts_near_core, weights),
+        flops=16 * rows_in * width_in * depth,
+    )
+    grads_near, basis_out_far, t0 = lax.optimization_barrier((grads_near, basis_out_far, t0))
+    g0 = call(
+        lambda *refs: rotate_out_kernel(tin, *refs),
+        shape(tile_out, bf16),
+        (own_grads, grads_near, own_basis_out, basis_out_far),
+        [pltpu.VMEM((depth, 2 * width_out), bf16)],
+        flops=8 * rows_out * width_out * depth,
+    )
+    t1 = hid(t0, tok_in)
+    t2 = hid(t0, col_in)
+    g1 = inb(g0, tok_out)
+    g2 = inb(g0, col_out)
+    s0 = hid(t0, 1)
+    s1 = hid(t1, 1)
+    s2 = hid(t2, 1)
+    chips = n_hid // 2
+    ends = (0, chips - 1)
+    inner = [(2 * z + c, 2 * (z if z in ends else chips - 1 - z) + c) for z in range(chips) for c in range(2)]
+    t4 = hid(call(copy_kernel, shape(tile_in, bf16), (t1,), flops=4000000000), col_in)
+    t0_then, _, g1, g2 = lax.optimization_barrier((t0, t1, g1, g2))
+    t3 = lax.ppermute(t0_then, "hid", inner)
+    onward = []
+    for h in range(n_hid):
+        step = col_out if h % 2 == 0 else tok_out
+        onward += [(i * n_hid + h, (i ^ step) * n_hid + h) for i in range(n_inb)]
+    picked = call(lambda *refs: pick_kernel(is_first_core, *refs), shape(tile_out, bf16), (g1, g2))
+    g3 = lax.ppermute(picked, ("inb", "hid"), onward)
+
+    half_rows, half_columns, half_tokens = 2 * tile_in[0], tile_out[1], tile_out[0]
+    quarter = (half_rows, half_columns)
+    ready, grad, fisher, left, right, side = call(
+        early_kernel,
+        [
+            shape(quarter, bf16),
+            shape((3,) + quarter, f32),
+            shape((3,) + quarter, f32),
+            shape((half_rows, 2 * half_tokens), bf16),
+            shape((2 * half_tokens, half_columns), bf16),
+            shape((half_rows, half_tokens), bf16),
+        ],
+        (t0, t1, t2, s0, s1, s2, g0, g1, g2),
+        flops=20 * half_rows * half_columns * half_tokens,
+    )
+    t3, t4, ready = lax.optimization_barrier((t3, t4, ready))
+    t3 = call(lambda *refs: pick_kernel(is_inner_chip, *refs), shape(tile_in, bf16), (t3, t4))
+    s3 = hid(t3, 1)
+    operands = (ready, grad, fisher, left, right, side, g1, t3, s3, g3)
+    return call(
+        late_kernel,
+        shape((activations.shape[2], out_grads.shape[2]), bf16),
+        operands,
+        [pltpu.VMEM((3,) + quarter, bf16), pltpu.SemaphoreType.DMA((16,))],
+        flops=16 * half_rows * half_columns * half_tokens,
+        out_space=anywhere,
+    )
+
+
 def solution(mesh):
+    n_inb, n_hid = mesh.shape["inb"], mesh.shape["hid"]
+    two_by_two = n_inb == 2 * 2 and n_hid == 2 * n_inb
+    body = (lambda *a: paired(n_inb, n_hid, *a)) if two_by_two else gathered
     return jax.shard_map(
-        on_device,
+        body,
         mesh=mesh,
         in_specs=(P(None, "hid", "inb"), P(None, "inb", "hid"), P("inb", "hid"), P("hid", "inb")),
         out_specs=P("inb", "hid"),

time: 160 us -> 51.4 us (0.32)
  waiting for transfers between devices: 129 us -> 22 us
  starting transfers between devices: 0.12 us -> 17 us
  matrix products: 15.5 us -> 0 us
  between operations: 13.2 us -> 0.11 us
  Pallas kernels: 0 us -> 8.04 us
    all_gather x4 -> x0, waiting for transfers between devices: 127 us -> none  [the longest x1 38.3 us: on_device(): lax.all_gather(basis_out, 'inb', axis=1, tiled=True)]
    ppermute x0 -> x17, waiting for transfers between devices: none -> 22 us  [the longest x15 17.7 us: swap(): return lax.ppermute(values, axis, [(i, i ^ distance) for i in range(count)])]
    ppermute x0 -> x17, starting transfers between devices: none -> 17 us  [the longest x15 14.8 us: swap(): return lax.ppermute(values, axis, [(i, i ^ distance) for i in range(count)])]
    dot_general x4 -> x0, matrix products: 15.5 us -> none  [the longest x2 7.87 us: contract_tokens(): lax.dot_general(left_side, right_side, (((0, 1), (0, 1)), ((), ())), pref...]
    pallas_call x0 -> x9, Pallas kernels: none -> 8.04 us  [call(): pl.pallas_call(kernel, out_shape=outs, in_specs=[space] * len(operands),...]
    unnamed x6 -> x8, local copies, waits for them, and re-layouts: 0.01 us -> 3.98 us
    reshape x1 -> x0, local copies, waits for them, and re-layouts: 2.56 us -> none  [on_device(): rotated = jnp.dot(plain_rows.reshape(-1, width_block), basis_whole, prefe...]
    unnamed x4 -> x0, waiting for transfers between devices: 2.1 us -> none
  transfers between devices with their start and end apart: 4 -> 17, of which waited for: 4 -> 11; matrix products, arithmetic and copies ran while one was open for 6% -> 0% of each run, Pallas kernels for 0% -> 10%
where the time goes in v2:
time: 51.4 us; the launch traced here: 51.1 us
  waiting for transfers between devices  22 us (43%)
  starting transfers between devices  17 us (33%)
  Pallas kernels  8.04 us (16%)
  local copies, waits for them, and re-layouts  3.98 us (8%)
    ppermute x15, waiting for transfers between devices, swap(): return lax.ppermute(values, axis, [(i, i ^ distance) for i in range(count)])  17.7 us
    ppermute x15, starting transfers between devices, swap(): return lax.ppermute(values, axis, [(i, i ^ distance) for i in range(count)])  14.8 us
    pallas_call x9, Pallas kernels, call(): pl.pallas_call(kernel, out_shape=outs, in_specs=[space] * len(operands),...  8.04 us
    ppermute x1, waiting for transfers between devices, paired(): g3 = lax.ppermute(picked, ('inb', 'hid'), onward)  4.26 us
    unnamed x8, local copies, waits for them, and re-layouts  3.98 us
    ppermute x1, starting transfers between devices, paired(): g3 = lax.ppermute(picked, ('inb', 'hid'), onward)  1.56 us
  transfers between devices with their start and end apart: 17, of which 11 were waited for; matrix products, arithmetic and copies ran while one was open for 0% of the time, Pallas kernels for 10%

profile of v2, /device:TPU:0, one launch (start us, length us, event | category | flops | bytes accessed | tf_op | source)
XLA Modules:
  0.0 51.1 jit_solution(2770778403313216604)
XLA Ops:
  0.0 4.0 %collective-permute-start.2 = (bf16[2,64,1024]{2,1,0:T(8,128)(2,1)}, bf16[2,64,1024]{2,1,0:T(8,128)(2,1)S(1)}, u32[]{:S(2)}, u32[]{:S(2)}) collective-permute-start(bf16[2,64,1024]{2,1,0:T(8,128)(2,1)} %refs_2_.1), channel_id=1, source_target_pairs={{0,4},{1,5},{2,6},{3,7},{4,0},{5,1},{6,2},{7,3},{8,12},{9,13},{10,... | collective-permute-start | bytes 786440 | tf_op jit(solution)/shard_map/ppermute | solution.py:51
  4.0 1.6 %collective-permute-start.5 = (bf16[1024,128]{1,0:T(8,128)(2,1)}, bf16[1024,128]{1,0:T(8,128)(2,1)S(1)}, u32[]{:S(2)}, u32[]{:S(2)}) collective-permute-start(bf16[1024,128]{1,0:T(8,128)(2,1)} %refs_3_.1), channel_id=1, source_target_pairs={{0,2},{1,3},{2,0},{3,1},{4,6},{5,7},{6,4},{7,5},{8,10},{9,11},{10,... | collective-permute-start | bytes 786440 | tf_op jit(solution)/shard_map/ppermute | solution.py:51
  5.6 1.5 %collective-permute-start = (bf16[2,128,1024]{2,1,0:T(8,128)(2,1)}, bf16[2,128,1024]{2,1,0:T(8,128)(2,1)S(1)}, u32[]{:S(2)}, u32[]{:S(2)}) collective-permute-start(bf16[2,128,1024]{2,1,0:T(8,128)(2,1)} %refs_0_.1), channel_id=1, source_target_pairs={{0,16},{8,24},{16,0},{24,8},{1,17},{9,25},{17,1},{25,9},{2,18},{10... | collective-permute-start | bytes 1572872 | tf_op jit(solution)/shard_map/ppermute | solution.py:51
  7.1 1.5 %collective-permute-start.1 = (bf16[1024,256]{1,0:T(8,128)(2,1)}, bf16[1024,256]{1,0:T(8,128)(2,1)S(1)}, u32[]{:S(2)}, u32[]{:S(2)}) collective-permute-start(bf16[1024,256]{1,0:T(8,128)(2,1)} %refs_1_.1), channel_id=1, source_target_pairs={{0,8},{8,0},{16,24},{24,16},{1,9},{9,1},{17,25},{25,17},{2,10},{10... | collective-permute-start | bytes 1572872 | tf_op jit(solution)/shard_map/ppermute | solution.py:51
  8.6 0.0 collective-permute-start.3
  8.6 0.0 copy-start
  8.6 1.0 %copy-done = bf16[2,128,1024]{2,1,0:T(8,128)(2,1)S(1)} copy-done((bf16[2,128,1024]{2,1,0:T(8,128)(2,1)S(1)}, bf16[2,128,1024]{2,1,0:T(8,128)(2,1)}, u32[]{:S(2)}) %copy-start) | copy-done | bytes 524312
  9.7 0.0 copy-start.1
  9.7 1.0 %copy-done.1 = bf16[1024,256]{1,0:T(8,128)(2,1)S(1)} copy-done((bf16[1024,256]{1,0:T(8,128)(2,1)S(1)}, bf16[1024,256]{1,0:T(8,128)(2,1)}, u32[]{:S(2)}) %copy-start.1) | copy-done | bytes 524312
  10.7 0.0 copy-start.2
  10.7 0.9 %copy-done.2 = bf16[1024,128]{1,0:T(8,128)(2,1)S(1)} copy-done((bf16[1024,128]{1,0:T(8,128)(2,1)S(1)}, bf16[1024,128]{1,0:T(8,128)(2,1)}, u32[]{:S(2)}) %copy-start.2) | copy-done | bytes 262168
  11.7 0.0 copy-start.3
  11.7 0.9 %copy-done.3 = bf16[2,64,1024]{2,1,0:T(8,128)(2,1)S(1)} copy-done((bf16[2,64,1024]{2,1,0:T(8,128)(2,1)S(1)}, bf16[2,64,1024]{2,1,0:T(8,128)(2,1)}, u32[]{:S(2)}) %copy-start.3) | copy-done | bytes 262168
  12.6 0.1 shard_map.46
  12.8 3.5 %collective-permute-done.2.near_ref = bf16[2,64,1024]{2,1,0:T(8,128)(2,1)S(1)} collective-permute-done((bf16[2,64,1024]{2,1,0:T(8,128)(2,1)}, bf16[2,64,1024]{2,1,0:T(8,128)(2,1)S(1)}, u32[]{:S(2)}, u32[]{:S(2)}) %collective-permute-start.2) | collective-permute-done | bytes 262176 | tf_op jit(solution)/shard_map/ppermute | solution.py:51
  16.3 0.0 collective-permute-start.4
  16.3 0.2 collective-permute-done.5.far_ref
  16.5 0.1 shard_map.47.weights
  16.6 0.0 collective-permute-done.3.core_ref
  16.6 1.2 %collective-permute-done.4.near_core_ref = bf16[2,64,1024]{2,1,0:T(8,128)(2,1)S(1)} collective-permute-done((bf16[2,64,1024]{2,1,0:T(8,128)(2,1)S(1)}, bf16[2,64,1024]{2,1,0:T(8,128)(2,1)S(1)}, u32[]{:S(2)}, u32[]{:S(2)}) %collective-permute-start.4) | collective-permute-done | bytes 262176 | tf_op jit(solution)/shard_map/ppermute | solution.py:51
  17.8 0.5 %shard_map.48.t0 = bf16[256,512]{1,0:T(8,128)(2,1)S(1)} custom-call(bf16[2,64,1024]{2,1,0:T(8,128)(2,1)S(1)} %get-tuple-element.29.own_ref, bf16[2,64,1024]{2,1,0:T(8,128)(2,1)S(1)} %collective-permute-done.3.core_ref, bf16[2,64,1024]{2,1,0:T(8,128)(2,1)S(1)} %collective-permute-done.2.near_ref, ...), custom_call_target="tpu_custom_call" | custom-call | flops 268435456 | tf_op jit(solution)/shard_map/pallas_call | solution.py:255
  18.3 0.6 %collective-permute-done.refs_1_ = bf16[2,128,1024]{2,1,0:T(8,128)(2,1)S(1)} collective-permute-done((bf16[2,128,1024]{2,1,0:T(8,128)(2,1)}, bf16[2,128,1024]{2,1,0:T(8,128)(2,1)S(1)}, u32[]{:S(2)}, u32[]{:S(2)}) %collective-permute-start) | collective-permute-done | bytes 524320 | tf_op jit(solution)/shard_map/ppermute | solution.py:51
  18.9 1.2 %collective-permute-done.1.refs_3_ = bf16[1024,256]{1,0:T(8,128)(2,1)S(1)} collective-permute-done((bf16[1024,256]{1,0:T(8,128)(2,1)}, bf16[1024,256]{1,0:T(8,128)(2,1)S(1)}, u32[]{:S(2)}, u32[]{:S(2)}) %collective-permute-start.1) | collective-permute-done | bytes 524320 | tf_op jit(solution)/shard_map/ppermute | solution.py:51
  20.2 0.3 collective-permute-start.6
  20.5 1.9 %collective-permute-start.11 = (bf16[256,512]{1,0:T(8,128)(2,1)S(1)}, bf16[256,512]{1,0:T(8,128)(2,1)S(1)}, u32[]{:S(2)}, u32[]{:S(2)}) collective-permute-start(bf16[256,512]{1,0:T(8,128)(2,1)S(1)} %shard_map.48.t0), channel_id=1, source_target_pairs={{0,2},{1,3},{2,0},{3,1},{4,6},{5,7},{6,4},{7,5},{8,10},{9,11},{10,... | collective-permute-start | bytes 786440 | tf_op jit(solution)/shard_map/ppermute | solution.py:51
  22.4 0.8 %shard_map.49.g0 = bf16[512,512]{1,0:T(8,128)(2,1)S(1)} custom-call(bf16[2,128,1024]{2,1,0:T(8,128)(2,1)S(1)} %get-tuple-element.33.refs_0_, bf16[2,128,1024]{2,1,0:T(8,128)(2,1)S(1)} %collective-permute-done.refs_1_, bf16[1024,256]{1,0:T(8,128)(2,1)S(1)} %get-tuple-element.35.refs_2_, bf16[1024,256]{1,0:T(8,128)(2,1)S(1)} %collective-permute-done.1.refs_3_), custom_call_target="tpu_custom_call" | custom-call | flops 536870912 | tf_op jit(solution)/shard_map/pallas_call | solution.py:255
  23.2 1.6 %collective-permute-start.7 = (bf16[512,512]{1,0:T(8,128)(2,1)S(1)}, bf16[512,512]{1,0:T(8,128)(2,1)S(1)}, u32[]{:S(2)}, u32[]{:S(2)}) collective-permute-start(bf16[512,512]{1,0:T(8,128)(2,1)S(1)} %shard_map.49.g0), channel_id=1, source_target_pairs={{0,16},{8,24},{16,0},{24,8},{1,17},{9,25},{17,1},{25,9},{2,18},{10... | collective-permute-start | bytes 1572872 | tf_op jit(solution)/shard_map/ppermute | solution.py:51
  24.8 1.5 %collective-permute-start.8 = (bf16[512,512]{1,0:T(8,128)(2,1)S(1)}, bf16[512,512]{1,0:T(8,128)(2,1)S(1)}, u32[]{:S(2)}, u32[]{:S(2)}) collective-permute-start(bf16[512,512]{1,0:T(8,128)(2,1)S(1)} %shard_map.49.g0), channel_id=1, source_target_pairs={{0,8},{8,0},{16,24},{24,16},{1,9},{9,1},{17,25},{25,17},{2,10},{10... | collective-permute-start | bytes 1572872 | tf_op jit(solution)/shard_map/ppermute | solution.py:51
  26.3 0.0 collective-permute-start.12
  26.3 7.1 %collective-permute-done.6.a_ref.t1 = bf16[256,512]{1,0:T(8,128)(2,1)S(1)} collective-permute-done((bf16[256,512]{1,0:T(8,128)(2,1)S(1)}, bf16[256,512]{1,0:T(8,128)(2,1)S(1)}, u32[]{:S(2)}, u32[]{:S(2)}) %collective-permute-start.6) | collective-permute-done | bytes 262176 | tf_op jit(solution)/shard_map/ppermute | solution.py:51
  33.4 0.0 collective-permute-start.13
  33.4 0.1 collective-permute-done.11.t2
  33.5 0.4 collective-permute-start.14
  33.9 2.7 %collective-permute-done.7.g1.refs_0_ = bf16[512,512]{1,0:T(8,128)(2,1)S(1)} collective-permute-done((bf16[512,512]{1,0:T(8,128)(2,1)S(1)}, bf16[512,512]{1,0:T(8,128)(2,1)S(1)}, u32[]{:S(2)}, u32[]{:S(2)}) %collective-permute-start.7) | collective-permute-done | bytes 524320 | tf_op jit(solution)/shard_map/ppermute | solution.py:51
  36.7 0.3 collective-permute-start.10
  37.0 0.9 %collective-permute-done.8.g2.refs_1_ = bf16[512,512]{1,0:T(8,128)(2,1)S(1)} collective-permute-done((bf16[512,512]{1,0:T(8,128)(2,1)S(1)}, bf16[512,512]{1,0:T(8,128)(2,1)S(1)}, u32[]{:S(2)}, u32[]{:S(2)}) %collective-permute-start.8) | collective-permute-done | bytes 524320 | tf_op jit(solution)/shard_map/ppermute | solution.py:51
  37.9 0.7 %collective-permute-start.9 = (bf16[256,512]{1,0:T(8,128)(2,1)S(1)}, bf16[256,512]{1,0:T(8,128)(2,1)S(1)}, u32[]{:S(2)}, u32[]{:S(2)}) collective-permute-start(bf16[256,512]{1,0:T(8,128)(2,1)S(1)} %shard_map.48.t0), channel_id=1, source_target_pairs={{0,0},{1,1},{2,4},{3,5},{4,2},{5,3},{6,6},{7,7},{8,8},{9,9},{10,12... | collective-permute-start | bytes 786440 | tf_op jit(solution)/shard_map/ppermute | solution.py:314
  38.6 0.1 shard_map.53
  38.7 0.0 collective-permute-done.12.s0
  38.7 1.6 %collective-permute-start.16 = (bf16[512,512]{1,0:T(8,128)(2,1)S(1)}, bf16[512,512]{1,0:T(8,128)(2,1)S(1)}, u32[]{:S(2)}, u32[]{:S(2)}) collective-permute-start(bf16[512,512]{1,0:T(8,128)(2,1)S(1)} %shard_map.53), channel_id=1, source_target_pairs={{0,8},{8,0},{16,24},{24,16},{1,17},{9,25},{17,1},{25,9},{2,10},{10... | collective-permute-start | bytes 1572872 | tf_op jit(solution)/shard_map/ppermute | solution.py:320
  40.2 0.0 collective-permute-done.13.s1
  40.2 0.0 collective-permute-done.14.s2
  40.2 3.2 %shard_map.51 = (bf16[512,512]{1,0:T(8,128)(2,1)S(1)}, f32[3,512,512]{2,1,0:T(8,128)S(1)}, f32[3,512,512]{2,1,0:T(8,128)S(1)}, bf16[512,1024]{1,0:T(8,128)(2,1)S...) custom-call(bf16[256,512]{1,0:T(8,128)(2,1)S(1)} %shard_map.48.t0, ...), custom_call_target="tpu_custom_call" | custom-call | flops 2684354560 | tf_op jit(solution)/shard_map/pallas_call | solution.py:255
  43.4 0.1 collective-permute-done.10.refs_1_
  43.6 0.0 collective-permute-done.9.refs_0_
  43.6 0.1 collective-permute-start.15
  43.7 4.3 %collective-permute-done.16.g3 = bf16[512,512]{1,0:T(8,128)(2,1)S(1)} collective-permute-done((bf16[512,512]{1,0:T(8,128)(2,1)S(1)}, bf16[512,512]{1,0:T(8,128)(2,1)S(1)}, u32[]{:S(2)}, u32[]{:S(2)}) %collective-permute-start.16) | collective-permute-done | bytes 524320 | tf_op jit(solution)/shard_map/ppermute | solution.py:320
  47.9 0.0 collective-permute-done.15.s3
  47.9 3.2 %shard_map.54 = bf16[1024,1024]{1,0:T(8,128)(2,1)} custom-call(bf16[512,512]{1,0:T(8,128)(2,1)S(1)} %get-tuple-element.41.ready, f32[3,512,512]{2,1,0:T(8,128)S(1)} %get-tuple-element.42.grad, f32[3,512,512]{2,1,0:T(8,128)S(1)} %get-tuple-element.43.fisher, bf16[512,1024]{1,0:T(8,128)(2,1)S(1)} %get-tuple-element.44.left, ...), custom_call_target="tpu_custom_call" | custom-call | flops 2147483648 | tf_op jit(solution)/shard_map/pallas_call | solution.py:255
  (2 shorter events, 0.0 us)
Async XLA Ops:
  0.0 16.3 %collective-permute-start.2 = (bf16[2,64,1024]{2,1,0:T(8,128)(2,1)}, bf16[2,64,1024]{2,1,0:T(8,128)(2,1)S(1)}, u32[]{:S(2)}, u32[]{:S(2)}) collective-permute-start(bf16[2,64,1024]{2,1,0:T(8,128)(2,1)} %refs_2_.1), channel_id=1, source_target_pairs={{0,4},{1,5},{2,6},{3,7},{4,0},{5,1},{6,2},{7,3},{8,12},{9,13},{10,... | collective-permute-start | bytes 786440 | tf_op jit(solution)/shard_map/ppermute | solution.py:51
  4.0 12.4 %collective-permute-start.5 = (bf16[1024,128]{1,0:T(8,128)(2,1)}, bf16[1024,128]{1,0:T(8,128)(2,1)S(1)}, u32[]{:S(2)}, u32[]{:S(2)}) collective-permute-start(bf16[1024,128]{1,0:T(8,128)(2,1)} %refs_3_.1), channel_id=1, source_target_pairs={{0,2},{1,3},{2,0},{3,1},{4,6},{5,7},{6,4},{7,5},{8,10},{9,11},{10,... | collective-permute-start | bytes 786440 | tf_op jit(solution)/shard_map/ppermute | solution.py:51
  5.6 13.3 %collective-permute-start = (bf16[2,128,1024]{2,1,0:T(8,128)(2,1)}, bf16[2,128,1024]{2,1,0:T(8,128)(2,1)S(1)}, u32[]{:S(2)}, u32[]{:S(2)}) collective-permute-start(bf16[2,128,1024]{2,1,0:T(8,128)(2,1)} %refs_0_.1), channel_id=1, source_target_pairs={{0,16},{8,24},{16,0},{24,8},{1,17},{9,25},{17,1},{25,9},{2,18},{10... | collective-permute-start | bytes 1572872 | tf_op jit(solution)/shard_map/ppermute | solution.py:51
  7.1 13.0 %collective-permute-start.1 = (bf16[1024,256]{1,0:T(8,128)(2,1)}, bf16[1024,256]{1,0:T(8,128)(2,1)S(1)}, u32[]{:S(2)}, u32[]{:S(2)}) collective-permute-start(bf16[1024,256]{1,0:T(8,128)(2,1)} %refs_1_.1), channel_id=1, source_target_pairs={{0,8},{8,0},{16,24},{24,16},{1,9},{9,1},{17,25},{25,17},{2,10},{10... | collective-permute-start | bytes 1572872 | tf_op jit(solution)/shard_map/ppermute | solution.py:51
  8.6 8.0 %collective-permute-start.3 = (bf16[2,64,1024]{2,1,0:T(8,128)(2,1)}, bf16[2,64,1024]{2,1,0:T(8,128)(2,1)S(1)}, u32[]{:S(2)}, u32[]{:S(2)}) collective-permute-start(bf16[2,64,1024]{2,1,0:T(8,128)(2,1)} %refs_2_.1), channel_id=1, source_target_pairs={{0,1},{1,0},{2,3},{3,2},{4,5},{5,4},{6,7},{7,6},{8,9},{9,8},{10,11... | collective-permute-start | bytes 786440 | tf_op jit(solution)/shard_map/ppermute | solution.py:51
  8.6 1.0 %copy-start = (bf16[2,128,1024]{2,1,0:T(8,128)(2,1)S(1)}, bf16[2,128,1024]{2,1,0:T(8,128)(2,1)}, u32[]{:S(2)}) copy-start(bf16[2,128,1024]{2,1,0:T(8,128)(2,1)} %refs_0_.1) | copy-start | bytes 1572868
  9.7 1.0 %copy-start.1 = (bf16[1024,256]{1,0:T(8,128)(2,1)S(1)}, bf16[1024,256]{1,0:T(8,128)(2,1)}, u32[]{:S(2)}) copy-start(bf16[1024,256]{1,0:T(8,128)(2,1)} %refs_1_.1) | copy-start | bytes 1572868
  10.7 0.9 %copy-start.2 = (bf16[1024,128]{1,0:T(8,128)(2,1)S(1)}, bf16[1024,128]{1,0:T(8,128)(2,1)}, u32[]{:S(2)}) copy-start(bf16[1024,128]{1,0:T(8,128)(2,1)} %refs_3_.1) | copy-start | bytes 786436
  11.7 0.9 %copy-start.3 = (bf16[2,64,1024]{2,1,0:T(8,128)(2,1)S(1)}, bf16[2,64,1024]{2,1,0:T(8,128)(2,1)}, u32[]{:S(2)}) copy-start(bf16[2,64,1024]{2,1,0:T(8,128)(2,1)} %refs_2_.1) | copy-start | bytes 786436
  16.3 1.5 %collective-permute-start.4 = (bf16[2,64,1024]{2,1,0:T(8,128)(2,1)S(1)}, bf16[2,64,1024]{2,1,0:T(8,128)(2,1)S(1)}, u32[]{:S(2)}, u32[]{:S(2)}) collective-permute-start(bf16[2,64,1024]{2,1,0:T(8,128)(2,1)S(1)} %collective-permute-done.2.near_ref), channel_id=1, source_target_pairs={{0,1},{1,0},{2,3},{3,2},{4,5},{5,4},{6,7},{7,6},{8,9},{9,8},{10,11... | collective-permute-start | bytes 786440 | tf_op jit(solution)/shard_map/ppermute | solution.py:51
  20.2 13.2 %collective-permute-start.6 = (bf16[256,512]{1,0:T(8,128)(2,1)S(1)}, bf16[256,512]{1,0:T(8,128)(2,1)S(1)}, u32[]{:S(2)}, u32[]{:S(2)}) collective-permute-start(bf16[256,512]{1,0:T(8,128)(2,1)S(1)} %shard_map.48.t0), channel_id=1, source_target_pairs={{0,4},{1,5},{2,6},{3,7},{4,0},{5,1},{6,2},{7,3},{8,12},{9,13},{10,... | collective-permute-start | bytes 786440 | tf_op jit(solution)/shard_map/ppermute | solution.py:51
  20.5 13.0 %collective-permute-start.11 = (bf16[256,512]{1,0:T(8,128)(2,1)S(1)}, bf16[256,512]{1,0:T(8,128)(2,1)S(1)}, u32[]{:S(2)}, u32[]{:S(2)}) collective-permute-start(bf16[256,512]{1,0:T(8,128)(2,1)S(1)} %shard_map.48.t0), channel_id=1, source_target_pairs={{0,2},{1,3},{2,0},{3,1},{4,6},{5,7},{6,4},{7,5},{8,10},{9,11},{10,... | collective-permute-start | bytes 786440 | tf_op jit(solution)/shard_map/ppermute | solution.py:51
  23.2 13.5 %collective-permute-start.7 = (bf16[512,512]{1,0:T(8,128)(2,1)S(1)}, bf16[512,512]{1,0:T(8,128)(2,1)S(1)}, u32[]{:S(2)}, u32[]{:S(2)}) collective-permute-start(bf16[512,512]{1,0:T(8,128)(2,1)S(1)} %shard_map.49.g0), channel_id=1, source_target_pairs={{0,16},{8,24},{16,0},{24,8},{1,17},{9,25},{17,1},{25,9},{2,18},{10... | collective-permute-start | bytes 1572872 | tf_op jit(solution)/shard_map/ppermute | solution.py:51
  24.8 13.1 %collective-permute-start.8 = (bf16[512,512]{1,0:T(8,128)(2,1)S(1)}, bf16[512,512]{1,0:T(8,128)(2,1)S(1)}, u32[]{:S(2)}, u32[]{:S(2)}) collective-permute-start(bf16[512,512]{1,0:T(8,128)(2,1)S(1)} %shard_map.49.g0), channel_id=1, source_target_pairs={{0,8},{8,0},{16,24},{24,16},{1,9},{9,1},{17,25},{25,17},{2,10},{10... | collective-permute-start | bytes 1572872 | tf_op jit(solution)/shard_map/ppermute | solution.py:51
  26.3 12.4 %collective-permute-start.12 = (bf16[256,512]{1,0:T(8,128)(2,1)S(1)}, bf16[256,512]{1,0:T(8,128)(2,1)S(1)}, u32[]{:S(2)}, u32[]{:S(2)}) collective-permute-start(bf16[256,512]{1,0:T(8,128)(2,1)S(1)} %shard_map.48.t0), channel_id=1, source_target_pairs={{0,1},{1,0},{2,3},{3,2},{4,5},{5,4},{6,7},{7,6},{8,9},{9,8},{10,11... | collective-permute-start | bytes 786440 | tf_op jit(solution)/shard_map/ppermute | solution.py:51
  33.4 6.8 %collective-permute-start.13 = (bf16[256,512]{1,0:T(8,128)(2,1)S(1)}, bf16[256,512]{1,0:T(8,128)(2,1)S(1)}, u32[]{:S(2)}, u32[]{:S(2)}) collective-permute-start(bf16[256,512]{1,0:T(8,128)(2,1)S(1)} %collective-permute-done.6.a_ref.t1), channel_id=1, source_target_pairs={{0,1},{1,0},{2,3},{3,2},{4,5},{5,4},{6,7},{7,6},{8,9},{9,8},{10,11... | collective-permute-start | bytes 786440 | tf_op jit(solution)/shard_map/ppermute | solution.py:51
  33.5 6.8 %collective-permute-start.14 = (bf16[256,512]{1,0:T(8,128)(2,1)S(1)}, bf16[256,512]{1,0:T(8,128)(2,1)S(1)}, u32[]{:S(2)}, u32[]{:S(2)}) collective-permute-start(bf16[256,512]{1,0:T(8,128)(2,1)S(1)} %collective-permute-done.11.t2), channel_id=1, source_target_pairs={{0,1},{1,0},{2,3},{3,2},{4,5},{5,4},{6,7},{7,6},{8,9},{9,8},{10,11... | collective-permute-start | bytes 786440 | tf_op jit(solution)/shard_map/ppermute | solution.py:51
  36.7 6.9 %collective-permute-start.10 = (bf16[256,512]{1,0:T(8,128)(2,1)S(1)}, bf16[256,512]{1,0:T(8,128)(2,1)S(1)}, u32[]{:S(2)}, u32[]{:S(2)}) collective-permute-start(bf16[256,512]{1,0:T(8,128)(2,1)S(1)} %shard_map.50), channel_id=1, source_target_pairs={{0,2},{1,3},{2,0},{3,1},{4,6},{5,7},{6,4},{7,5},{8,10},{9,11},{10,... | collective-permute-start | bytes 786440 | tf_op jit(solution)/shard_map/ppermute | solution.py:51
  37.9 5.6 %collective-permute-start.9 = (bf16[256,512]{1,0:T(8,128)(2,1)S(1)}, bf16[256,512]{1,0:T(8,128)(2,1)S(1)}, u32[]{:S(2)}, u32[]{:S(2)}) collective-permute-start(bf16[256,512]{1,0:T(8,128)(2,1)S(1)} %shard_map.48.t0), channel_id=1, source_target_pairs={{0,0},{1,1},{2,4},{3,5},{4,2},{5,3},{6,6},{7,7},{8,8},{9,9},{10,12... | collective-permute-start | bytes 786440 | tf_op jit(solution)/shard_map/ppermute | solution.py:314
  38.7 9.2 %collective-permute-start.16 = (bf16[512,512]{1,0:T(8,128)(2,1)S(1)}, bf16[512,512]{1,0:T(8,128)(2,1)S(1)}, u32[]{:S(2)}, u32[]{:S(2)}) collective-permute-start(bf16[512,512]{1,0:T(8,128)(2,1)S(1)} %shard_map.53), channel_id=1, source_target_pairs={{0,8},{8,0},{16,24},{24,16},{1,17},{9,25},{17,1},{25,9},{2,10},{10... | collective-permute-start | bytes 1572872 | tf_op jit(solution)/shard_map/ppermute | solution.py:320
  43.6 4.3 %collective-permute-start.15 = (bf16[256,512]{1,0:T(8,128)(2,1)S(1)}, bf16[256,512]{1,0:T(8,128)(2,1)S(1)}, u32[]{:S(2)}, u32[]{:S(2)}) collective-permute-start(bf16[256,512]{1,0:T(8,128)(2,1)S(1)} %shard_map.52.t3), channel_id=1, source_target_pairs={{0,1},{1,0},{2,3},{3,2},{4,5},{5,4},{6,7},{7,6},{8,9},{9,8},{10,11... | collective-permute-start | bytes 786440 | tf_op jit(solution)/shard_map/ppermute | solution.py:51

commit v3 on v2

--- a/solution.py
+++ b/solution.py
@@ -138,99 +138,69 @@
     return hid_digits()[2] == 0
 
 
-def is_inner_chip():
-    tok, col, _ = hid_digits()
-    return tok != col
-
-
-def early_kernel(t0, t1, t2, s0, s1, s2, g0, g1, g2, ready, grad, fisher, left, right, side):
+def squared(values):
+    return values * values
+
+
+def ratio(g, f):
+    return (g / (f + damping)).astype(jnp.bfloat16)
+
+
+def early_kernel(t0, t1, t2, s0, s1, s2, g0, g1, g2, g3, top, grad, fisher, left, right, side):
+    out_tok, _ = inb_digits()
     other = other_tokens()
     size, span = t0.shape
+    width = g0.shape[1]
     for k, (t, t_far, t_side) in enumerate(((t0, t2, t1), (s0, s2, s1))):
         at = slice(k * size, (k + 1) * size)
         left[at, :span] = t[...]
         left[at, span:] = t_far[...]
         side[at] = t_side[...]
-    right[rows_of(other, span), :] = g0[...]
-    right[rows_of(1 - other, span), :] = g2[...]
-    whole, below = right[...], g1[...]
-    whole_squared, below_squared = whole * whole, below * below
-    for k in range(2):
-        at = slice(k * size, (k + 1) * size)
-        rows = left[at]
-        g = dot(rows, whole)
-        f = dot(rows * rows, whole_squared)
-        ready[at] = (g / (f + damping)).astype(jnp.bfloat16)
-        rows = left[at, rows_of(other, span)]
-        grad[0, at] = dot(rows, below)
-        fisher[0, at] = dot(rows * rows, below_squared)
-        rows = side[at]
-        grad[1, at] = dot(rows, whole[:span])
-        fisher[1, at] = dot(rows * rows, whole_squared[:span])
-
-    @pl.when(other == 0)
-    def _():
+    for half, column, tile in ((other, out_tok, g0), (1 - other, out_tok, g2), (other, 1 - out_tok, g1), (1 - other, 1 - out_tok, g3)):
+        right[rows_of(half, span), rows_of(column, width)] = tile[...]
+    for c in range(2):
+        columns = slice(c * width, (c + 1) * width)
+        whole = right[:, columns]
+        whole_squared = squared(whole)
         for k in range(2):
             at = slice(k * size, (k + 1) * size)
+            rows = left[at]
+            top[at, columns] = ratio(dot(rows, whole), dot(squared(rows), whole_squared))
             rows = side[at]
-            grad[2, at] = dot(rows, below)
-            fisher[2, at] = dot(rows * rows, below_squared)
-
-
-def late_kernel(ready, grad, fisher, left, right, side, g1, t3, s3, g3, out_ref, done, sems):
-    tok, col, core = hid_digits()
-    out_tok, _ = inb_digits()
-    other = other_tokens()
+            grad[at, columns] = dot(rows, whole[:span])
+            fisher[at, columns] = dot(squared(rows), whole_squared[:span])
+
+
+def late_kernel(top, grad, fisher, right, t3, s3, out_ref, done, sems):
+    tok, _, core = hid_digits()
     size, span = t3.shape
-    row_size, width = size // 2, ready.shape[1]
+    row_size, width = size // 2, right.shape[1] // 2
     copies = []
 
-    def send(quadrant, part, source, row_tok, column_tok):
+    def send(part, source, row_tok, number):
         for k in range(2):
             row = 4 * row_tok + 2 * k + (core if part == 0 else 1 - core)
             copy = pltpu.make_async_copy(
                 source.at[pl.ds(part * size + k * row_size, row_size), :],
-                out_ref.at[rows_of(row, row_size), rows_of(column_tok, width)],
-                sems.at[4 * quadrant + 2 * part + k],
+                out_ref.at[rows_of(row, row_size), :],
+                sems.at[number + k],
             )
             copy.start()
             copies.append(copy)
 
-    def divided(quadrant, at, g, f):
-        done[quadrant, at] = (g / (f + damping)).astype(jnp.bfloat16)
-
     for part in range(2):
-        send(3, part, ready, tok, out_tok)
-    below, beside = g3[...], right[span:]
-    below_squared, beside_squared = below * below, beside * beside
-    parts = [(slice(k * size, (k + 1) * size), k, t) for k, t in enumerate((t3, s3))]
-    for at, k, _ in parts:
-        rows = left[at, rows_of(1 - other, span)]
-        divided(0, at, grad[0, at] + dot(rows, below), fisher[0, at] + dot(rows * rows, below_squared))
-        send(0, k, done.at[0], tok, 1 - out_tok)
-    for at, k, t in parts:
+        send(part, top, tok, 2 * part)
+    for part, t in enumerate((t3, s3)):
+        at = slice(part * size, (part + 1) * size)
         rows = t[...]
-        divided(1, at, grad[1, at] + dot(rows, beside), fisher[1, at] + dot(rows * rows, beside_squared))
-        send(1, k, done.at[1], 1 - tok, out_tok)
-
-    @pl.when(other == 0)
-    def _():
-        for at, _, t in parts:
-            rows = t[...]
-            divided(2, at, grad[2, at] + dot(rows, below), fisher[2, at] + dot(rows * rows, below_squared))
-
-    @pl.when(other == 1)
-    def _():
-        last = g1[...]
-        last_squared = last * last
-        for at, _, t in parts:
-            rows, near = t[...], side[at]
-            g = dot(rows, last) + dot(near, below)
-            f = dot(rows * rows, last_squared) + dot(near * near, below_squared)
-            divided(2, at, g, f)
-
-    for part in range(2):
-        send(2, part, done.at[2], 1 - tok, 1 - out_tok)
+        rows_squared = squared(rows)
+        for c in range(2):
+            columns = slice(c * width, (c + 1) * width)
+            beside = right[span:, columns]
+            g = grad[at, columns] + dot(rows, beside)
+            f = fisher[at, columns] + dot(rows_squared, squared(beside))
+            done[at, columns] = ratio(g, f)
+        send(part, done, 1 - tok, 4 + 2 * part)
     for copy in copies:
         copy.wait()
 
@@ -276,28 +246,27 @@
         [pltpu.SemaphoreType.DMA((len(own),))],
         space=anywhere,
     )
-    acts_near, own_acts, own_grads = lax.optimization_barrier((acts_near, own_acts, own_grads))
-    acts_near_core = hid(acts_near, 1)
 
     micro, tin, depth = activations.shape
     tout = out_grads.shape[1]
     rows_out, width_out = micro * tout, basis_out.shape[1]
     rows_in, width_in = micro * tin, basis_in.shape[1]
     tile_in, tile_out = (2 * width_in, 4 * rows_in), (2 * rows_out, 2 * width_out)
-    weights = call(join_kernel, shape((depth, 2 * width_in), bf16), (own_basis_in, basis_far), flops=4000000000)
-    t0 = call(
-        rotate_in_kernel,
-        shape(tile_in, bf16),
-        (own_acts, acts_core, acts_near, acts_near_core, weights),
-        flops=16 * rows_in * width_in * depth,
-    )
-    grads_near, basis_out_far, t0 = lax.optimization_barrier((grads_near, basis_out_far, t0))
     g0 = call(
         lambda *refs: rotate_out_kernel(tin, *refs),
         shape(tile_out, bf16),
         (own_grads, grads_near, own_basis_out, basis_out_far),
         [pltpu.VMEM((depth, 2 * width_out), bf16)],
         flops=8 * rows_out * width_out * depth,
+    )
+    acts_near, _ = lax.optimization_barrier((acts_near, g0))
+    acts_near_core = hid(acts_near, 1)
+    weights = call(join_kernel, shape((depth, 2 * width_in), bf16), (own_basis_in, basis_far), flops=8000000000)
+    t0 = call(
+        rotate_in_kernel,
+        shape(tile_in, bf16),
+        (own_acts, acts_core, acts_near, acts_near_core, weights),
+        flops=16 * rows_in * width_in * depth + 2000000000,
     )
     t1 = hid(t0, tok_in)
     t2 = hid(t0, col_in)
@@ -306,44 +275,40 @@
     s0 = hid(t0, 1)
     s1 = hid(t1, 1)
     s2 = hid(t2, 1)
-    chips = n_hid // 2
-    ends = (0, chips - 1)
-    inner = [(2 * z + c, 2 * (z if z in ends else chips - 1 - z) + c) for z in range(chips) for c in range(2)]
-    t4 = hid(call(copy_kernel, shape(tile_in, bf16), (t1,), flops=4000000000), col_in)
-    t0_then, _, g1, g2 = lax.optimization_barrier((t0, t1, g1, g2))
-    t3 = lax.ppermute(t0_then, "hid", inner)
+    t1_then = call(copy_kernel, shape(tile_in, bf16), (t1,), flops=4000000000)
+    t3 = hid(t1_then, col_in)
     onward = []
     for h in range(n_hid):
         step = col_out if h % 2 == 0 else tok_out
         onward += [(i * n_hid + h, (i ^ step) * n_hid + h) for i in range(n_inb)]
-    picked = call(lambda *refs: pick_kernel(is_first_core, *refs), shape(tile_out, bf16), (g1, g2))
+    g1_then, g2_then, _ = lax.optimization_barrier((g1, g2, t0))
+    picked = call(lambda *refs: pick_kernel(is_first_core, *refs), shape(tile_out, bf16), (g1_then, g2_then), flops=0)
     g3 = lax.ppermute(picked, ("inb", "hid"), onward)
 
     half_rows, half_columns, half_tokens = 2 * tile_in[0], tile_out[1], tile_out[0]
-    quarter = (half_rows, half_columns)
-    ready, grad, fisher, left, right, side = call(
+    columns, half_out = 2 * half_columns, (half_rows, 2 * half_columns)
+    top, grad, fisher, _, right, _ = call(
         early_kernel,
         [
-            shape(quarter, bf16),
-            shape((3,) + quarter, f32),
-            shape((3,) + quarter, f32),
+            shape(half_out, bf16),
+            shape(half_out, f32),
+            shape(half_out, f32),
             shape((half_rows, 2 * half_tokens), bf16),
-            shape((2 * half_tokens, half_columns), bf16),
+            shape((2 * half_tokens, columns), bf16),
             shape((half_rows, half_tokens), bf16),
         ],
-        (t0, t1, t2, s0, s1, s2, g0, g1, g2),
-        flops=20 * half_rows * half_columns * half_tokens,
-    )
-    t3, t4, ready = lax.optimization_barrier((t3, t4, ready))
-    t3 = call(lambda *refs: pick_kernel(is_inner_chip, *refs), shape(tile_in, bf16), (t3, t4))
+        (t0, t1, t2, s0, s1, s2, g0, g1, g2, g3),
+        flops=2000000000,
+    )
+    t3, top = lax.optimization_barrier((t3, top))
+    t3 = call(copy_kernel, shape(tile_in, bf16), (t3,), flops=4000000000)
     s3 = hid(t3, 1)
-    operands = (ready, grad, fisher, left, right, side, g1, t3, s3, g3)
     return call(
         late_kernel,
         shape((activations.shape[2], out_grads.shape[2]), bf16),
-        operands,
-        [pltpu.VMEM((3,) + quarter, bf16), pltpu.SemaphoreType.DMA((16,))],
-        flops=16 * half_rows * half_columns * half_tokens,
+        (top, grad, fisher, right, t3, s3),
+        [pltpu.VMEM(half_out, bf16), pltpu.SemaphoreType.DMA((8,))],
+        flops=4 * half_rows * half_columns * half_tokens,
         out_space=anywhere,
     )
 

time: 51.4 us -> 49.7 us (0.967)
  waiting for transfers between devices: 22 us -> 18.9 us
  starting transfers between devices: 17 us -> 18.1 us
    ppermute x1, waiting for transfers between devices: 4.26 us -> 1.06 us  [paired(): g3 = lax.ppermute(picked, ('inb', 'hid'), onward)]
    ppermute x15, starting transfers between devices: 14.8 us -> 16.5 us  [swap(): return lax.ppermute(values, axis, [(i, i ^ distance) for i in range(count)])]
    ppermute x1 -> x0, starting transfers between devices: 0.67 us -> none  [paired(): t3 = lax.ppermute(t0_then, 'hid', inner)]
  transfers between devices with their start and end apart: 17 -> 16, of which waited for: 11 -> 11; matrix products, arithmetic and copies ran while one was open for 0% -> 0% of each run, Pallas kernels for 10% -> 12%
where the time goes in v3:
time: 49.7 us; the launch traced here: 49.4 us
  waiting for transfers between devices  18.9 us (38%)
  starting transfers between devices  18.1 us (36%)
  Pallas kernels  8.46 us (17%)
  local copies, waits for them, and re-layouts  3.98 us (8%)
    ppermute x15, waiting for transfers between devices, swap(): return lax.ppermute(values, axis, [(i, i ^ distance) for i in range(count)])  17.8 us
    ppermute x15, starting transfers between devices, swap(): return lax.ppermute(values, axis, [(i, i ^ distance) for i in range(count)])  16.5 us
    pallas_call x9, Pallas kernels, call(): pl.pallas_call(kernel, out_shape=outs, in_specs=[space] * len(operands),...  8.46 us
    unnamed x8, local copies, waits for them, and re-layouts  3.98 us
    ppermute x1, starting transfers between devices, paired(): g3 = lax.ppermute(picked, ('inb', 'hid'), onward)  1.56 us
    ppermute x1, waiting for transfers between devices, paired(): g3 = lax.ppermute(picked, ('inb', 'hid'), onward)  1.06 us
  transfers between devices with their start and end apart: 16, of which 11 were waited for; matrix products, arithmetic and copies ran while one was open for 0% of the time, Pallas kernels for 12%

profile of v3, /device:TPU:0, one launch (start us, length us, event | category | flops | bytes accessed | tf_op | source)
XLA Modules:
  0.0 49.4 jit_solution(6116030633777719594)
XLA Ops:
  0.0 3.0 %collective-permute-start.2 = (bf16[2,128,1024]{2,1,0:T(8,128)(2,1)}, bf16[2,128,1024]{2,1,0:T(8,128)(2,1)S(1)}, u32[]{:S(2)}, u32[]{:S(2)}) collective-permute-start(bf16[2,128,1024]{2,1,0:T(8,128)(2,1)} %refs_0_.1), channel_id=1, source_target_pairs={{0,16},{8,24},{16,0},{24,8},{1,17},{9,25},{17,1},{25,9},{2,18},{10... | collective-permute-start | bytes 1572872 | tf_op jit(solution)/shard_map/ppermute | solution.py:51
  3.0 1.5 %collective-permute-start.3 = (bf16[1024,256]{1,0:T(8,128)(2,1)}, bf16[1024,256]{1,0:T(8,128)(2,1)S(1)}, u32[]{:S(2)}, u32[]{:S(2)}) collective-permute-start(bf16[1024,256]{1,0:T(8,128)(2,1)} %refs_1_.1), channel_id=1, source_target_pairs={{0,8},{8,0},{16,24},{24,16},{1,9},{9,1},{17,25},{25,17},{2,10},{10... | collective-permute-start | bytes 1572872 | tf_op jit(solution)/shard_map/ppermute | solution.py:51
  4.5 2.6 %collective-permute-start.1 = (bf16[2,64,1024]{2,1,0:T(8,128)(2,1)}, bf16[2,64,1024]{2,1,0:T(8,128)(2,1)S(1)}, u32[]{:S(2)}, u32[]{:S(2)}) collective-permute-start(bf16[2,64,1024]{2,1,0:T(8,128)(2,1)} %refs_2_.1), channel_id=1, source_target_pairs={{0,4},{1,5},{2,6},{3,7},{4,0},{5,1},{6,2},{7,3},{8,12},{9,13},{10,... | collective-permute-start | bytes 786440 | tf_op jit(solution)/shard_map/ppermute | solution.py:51
  7.0 1.6 %collective-permute-start.5 = (bf16[1024,128]{1,0:T(8,128)(2,1)}, bf16[1024,128]{1,0:T(8,128)(2,1)S(1)}, u32[]{:S(2)}, u32[]{:S(2)}) collective-permute-start(bf16[1024,128]{1,0:T(8,128)(2,1)} %refs_3_.1), channel_id=1, source_target_pairs={{0,2},{1,3},{2,0},{3,1},{4,6},{5,7},{6,4},{7,5},{8,10},{9,11},{10,... | collective-permute-start | bytes 786440 | tf_op jit(solution)/shard_map/ppermute | solution.py:51
  8.6 0.0 collective-permute-start
  8.6 0.0 copy-start
  8.6 1.0 %copy-done = bf16[2,128,1024]{2,1,0:T(8,128)(2,1)S(1)} copy-done((bf16[2,128,1024]{2,1,0:T(8,128)(2,1)S(1)}, bf16[2,128,1024]{2,1,0:T(8,128)(2,1)}, u32[]{:S(2)}) %copy-start) | copy-done | bytes 524312
  9.7 0.0 copy-start.1
  9.7 1.0 %copy-done.1 = bf16[1024,256]{1,0:T(8,128)(2,1)S(1)} copy-done((bf16[1024,256]{1,0:T(8,128)(2,1)S(1)}, bf16[1024,256]{1,0:T(8,128)(2,1)}, u32[]{:S(2)}) %copy-start.1) | copy-done | bytes 524312
  10.7 0.0 copy-start.2
  10.7 0.9 %copy-done.2 = bf16[1024,128]{1,0:T(8,128)(2,1)S(1)} copy-done((bf16[1024,128]{1,0:T(8,128)(2,1)S(1)}, bf16[1024,128]{1,0:T(8,128)(2,1)}, u32[]{:S(2)}) %copy-start.2) | copy-done | bytes 262168
  11.7 0.0 copy-start.3
  11.7 0.9 %copy-done.3 = bf16[2,64,1024]{2,1,0:T(8,128)(2,1)S(1)} copy-done((bf16[2,64,1024]{2,1,0:T(8,128)(2,1)S(1)}, bf16[2,64,1024]{2,1,0:T(8,128)(2,1)}, u32[]{:S(2)}) %copy-start.3) | copy-done | bytes 262168
  12.6 0.1 shard_map.46
  12.8 2.3 %collective-permute-done.2.refs_1_ = bf16[2,128,1024]{2,1,0:T(8,128)(2,1)S(1)} collective-permute-done((bf16[2,128,1024]{2,1,0:T(8,128)(2,1)}, bf16[2,128,1024]{2,1,0:T(8,128)(2,1)S(1)}, u32[]{:S(2)}, u32[]{:S(2)}) %collective-permute-start.2) | collective-permute-done | bytes 524320 | tf_op jit(solution)/shard_map/ppermute | solution.py:51
  15.1 1.5 %collective-permute-done.3.refs_3_ = bf16[1024,256]{1,0:T(8,128)(2,1)S(1)} collective-permute-done((bf16[1024,256]{1,0:T(8,128)(2,1)}, bf16[1024,256]{1,0:T(8,128)(2,1)S(1)}, u32[]{:S(2)}, u32[]{:S(2)}) %collective-permute-start.3) | collective-permute-done | bytes 524320 | tf_op jit(solution)/shard_map/ppermute | solution.py:51
  16.6 0.8 %shard_map.47.g0 = bf16[512,512]{1,0:T(8,128)(2,1)S(1)} custom-call(bf16[2,128,1024]{2,1,0:T(8,128)(2,1)S(1)} %get-tuple-element.19.refs_0_, bf16[2,128,1024]{2,1,0:T(8,128)(2,1)S(1)} %collective-permute-done.2.refs_1_, bf16[1024,256]{1,0:T(8,128)(2,1)S(1)} %get-tuple-element.20.refs_2_, bf16[1024,256]{1,0:T(8,128)(2,1)S(1)} %collective-permute-done.3.refs_3_), custom_call_target="tpu_custom_call" | custom-call | flops 536870912 | tf_op jit(solution)/shard_map/pallas_call | solution.py:225
  17.4 0.3 collective-permute-start.12
  17.7 1.7 %collective-permute-start.13 = (bf16[512,512]{1,0:T(8,128)(2,1)S(1)}, bf16[512,512]{1,0:T(8,128)(2,1)S(1)}, u32[]{:S(2)}, u32[]{:S(2)}) collective-permute-start(bf16[512,512]{1,0:T(8,128)(2,1)S(1)} %shard_map.47.g0), channel_id=1, source_target_pairs={{0,8},{8,0},{16,24},{24,16},{1,9},{9,1},{17,25},{25,17},{2,10},{10... | collective-permute-start | bytes 1572872 | tf_op jit(solution)/shard_map/ppermute | solution.py:51
  19.4 0.0 collective-permute-done.1.near_ref
  19.4 0.0 collective-permute-start.4
  19.4 0.0 collective-permute-done.5.far_ref
  19.4 0.2 shard_map.48.weights
  19.6 0.0 collective-permute-done.core_ref
  19.6 1.4 %collective-permute-done.4.near_core_ref = bf16[2,64,1024]{2,1,0:T(8,128)(2,1)S(1)} collective-permute-done((bf16[2,64,1024]{2,1,0:T(8,128)(2,1)S(1)}, bf16[2,64,1024]{2,1,0:T(8,128)(2,1)S(1)}, u32[]{:S(2)}, u32[]{:S(2)}) %collective-permute-start.4) | collective-permute-done | bytes 262176 | tf_op jit(solution)/shard_map/ppermute | solution.py:51
  21.0 0.5 %shard_map.49.t0 = bf16[256,512]{1,0:T(8,128)(2,1)S(1)} custom-call(bf16[2,64,1024]{2,1,0:T(8,128)(2,1)S(1)} %get-tuple-element.18.own_ref, bf16[2,64,1024]{2,1,0:T(8,128)(2,1)S(1)} %collective-permute-done.core_ref, bf16[2,64,1024]{2,1,0:T(8,128)(2,1)S(1)} %collective-permute-done.1.near_ref, bf16[2,64,1024]{2,1,0:T(8,128)(2,1)S(1)} %collective-permute-done.4.near_core_ref, ...), custom_call_target="tpu_custom_call" | custom-call | flops 2268435456 | tf_op jit(solution)/shard_map/pallas_call | solution.py:225
  21.5 2.7 %collective-permute-start.6 = (bf16[256,512]{1,0:T(8,128)(2,1)S(1)}, bf16[256,512]{1,0:T(8,128)(2,1)S(1)}, u32[]{:S(2)}, u32[]{:S(2)}) collective-permute-start(bf16[256,512]{1,0:T(8,128)(2,1)S(1)} %shard_map.49.t0), channel_id=1, source_target_pairs={{0,4},{1,5},{2,6},{3,7},{4,0},{5,1},{6,2},{7,3},{8,12},{9,13},{10,... | collective-permute-start | bytes 786440 | tf_op jit(solution)/shard_map/ppermute | solution.py:51
  24.1 1.6 %collective-permute-start.8 = (bf16[256,512]{1,0:T(8,128)(2,1)S(1)}, bf16[256,512]{1,0:T(8,128)(2,1)S(1)}, u32[]{:S(2)}, u32[]{:S(2)}) collective-permute-start(bf16[256,512]{1,0:T(8,128)(2,1)S(1)} %shard_map.49.t0), channel_id=1, source_target_pairs={{0,2},{1,3},{2,0},{3,1},{4,6},{5,7},{6,4},{7,5},{8,10},{9,11},{10,... | collective-permute-start | bytes 786440 | tf_op jit(solution)/shard_map/ppermute | solution.py:51
  25.7 4.2 %collective-permute-done.12.refs_0_.g1 = bf16[512,512]{1,0:T(8,128)(2,1)S(1)} collective-permute-done((bf16[512,512]{1,0:T(8,128)(2,1)S(1)}, bf16[512,512]{1,0:T(8,128)(2,1)S(1)}, u32[]{:S(2)}, u32[]{:S(2)}) %collective-permute-start.12) | collective-permute-done | bytes 524320 | tf_op jit(solution)/shard_map/ppermute | solution.py:51
  29.9 0.3 collective-permute-done.13.refs_1_.g2
  30.3 1.6 %collective-permute-start.14 = (bf16[512,512]{1,0:T(8,128)(2,1)S(1)}, bf16[512,512]{1,0:T(8,128)(2,1)S(1)}, u32[]{:S(2)}, u32[]{:S(2)}) collective-permute-start(bf16[512,512]{1,0:T(8,128)(2,1)S(1)} %shard_map.51), channel_id=1, source_target_pairs={{0,8},{8,0},{16,24},{24,16},{1,17},{9,25},{17,1},{25,9},{2,10},{10... | collective-permute-start | bytes 1572872 | tf_op jit(solution)/shard_map/ppermute | solution.py:286
  31.8 0.0 collective-permute-start.9
  31.8 4.7 %collective-permute-done.6.a_ref.t1 = bf16[256,512]{1,0:T(8,128)(2,1)S(1)} collective-permute-done((bf16[256,512]{1,0:T(8,128)(2,1)S(1)}, bf16[256,512]{1,0:T(8,128)(2,1)S(1)}, u32[]{:S(2)}, u32[]{:S(2)}) %collective-permute-start.6) | collective-permute-done | bytes 262176 | tf_op jit(solution)/shard_map/ppermute | solution.py:51
  36.5 0.0 collective-permute-start.10
  36.5 0.2 collective-permute-done.8.t2
  36.7 0.3 collective-permute-start.11
  37.1 1.2 %collective-permute-start.7 = (bf16[256,512]{1,0:T(8,128)(2,1)S(1)}, bf16[256,512]{1,0:T(8,128)(2,1)S(1)}, u32[]{:S(2)}, u32[]{:S(2)}) collective-permute-start(bf16[256,512]{1,0:T(8,128)(2,1)S(1)} %shard_map.50), channel_id=1, source_target_pairs={{0,2},{1,3},{2,0},{3,1},{4,6},{5,7},{6,4},{7,5},{8,10},{9,11},{10,... | collective-permute-start | bytes 786440 | tf_op jit(solution)/shard_map/ppermute | solution.py:51
  38.2 0.0 collective-permute-done.9.s0
  38.3 0.0 collective-permute-done.10.s1
  38.3 0.2 collective-permute-done.11.s2
  38.4 1.1 %collective-permute-done.14.g3 = bf16[512,512]{1,0:T(8,128)(2,1)S(1)} collective-permute-done((bf16[512,512]{1,0:T(8,128)(2,1)S(1)}, bf16[512,512]{1,0:T(8,128)(2,1)S(1)}, u32[]{:S(2)}, u32[]{:S(2)}) %collective-permute-start.14) | collective-permute-done | bytes 524320 | tf_op jit(solution)/shard_map/ppermute | solution.py:286
  39.5 4.5 %shard_map.52 = (bf16[512,1024]{1,0:T(8,128)(2,1)S(1)}, f32[512,1024]{1,0:T(8,128)S(1)}, f32[512,1024]{1,0:T(8,128)S(1)}, bf16[512,1024]{1,0:T(8,128)(2,1)}, bf1...) custom-call(bf16[256,512]{1,0:T(8,128)(2,1)S(1)} %shard_map.49.t0, ...), custom_call_target="tpu_custom_call" | custom-call | flops 2000000000 | tf_op jit(solution)/shard_map/pallas_call | solution.py:225
  44.0 1.5 %collective-permute-done.7.a_ref = bf16[256,512]{1,0:T(8,128)(2,1)S(1)} collective-permute-done((bf16[256,512]{1,0:T(8,128)(2,1)S(1)}, bf16[256,512]{1,0:T(8,128)(2,1)S(1)}, u32[]{:S(2)}, u32[]{:S(2)}) %collective-permute-start.7) | collective-permute-done | bytes 262176 | tf_op jit(solution)/shard_map/ppermute | solution.py:51
  45.5 0.1 collective-permute-start.15
  45.6 1.5 %collective-permute-done.15.s3 = bf16[256,512]{1,0:T(8,128)(2,1)S(1)} collective-permute-done((bf16[256,512]{1,0:T(8,128)(2,1)S(1)}, bf16[256,512]{1,0:T(8,128)(2,1)S(1)}, u32[]{:S(2)}, u32[]{:S(2)}) %collective-permute-start.15) | collective-permute-done | bytes 262176 | tf_op jit(solution)/shard_map/ppermute | solution.py:51
  47.1 2.3 %shard_map.54 = bf16[1024,1024]{1,0:T(8,128)(2,1)} custom-call(bf16[512,1024]{1,0:T(8,128)(2,1)S(1)} %get-tuple-element.26.top, f32[512,1024]{1,0:T(8,128)S(1)} %get-tuple-element.27.grad, f32[512,1024]{1,0:T(8,128)S(1)} %get-tuple-element.28.fisher, bf16[1024,1024]{1,0:T(8,128)(2,1)S(1)} %get-tuple-element.29.right, bf16[256,512]{1,0:T(8,128)(2,1)S(1)} %shard_map.53.t3, ...), custom_call_target="tpu_custom_call" | custom-call | flops 536870912 | tf_op jit(solution)/shard_map/pallas_call | solution.py:225
  (3 shorter events, 0.1 us)
Async XLA Ops:
  0.0 15.1 %collective-permute-start.2 = (bf16[2,128,1024]{2,1,0:T(8,128)(2,1)}, bf16[2,128,1024]{2,1,0:T(8,128)(2,1)S(1)}, u32[]{:S(2)}, u32[]{:S(2)}) collective-permute-start(bf16[2,128,1024]{2,1,0:T(8,128)(2,1)} %refs_0_.1), channel_id=1, source_target_pairs={{0,16},{8,24},{16,0},{24,8},{1,17},{9,25},{17,1},{25,9},{2,18},{10... | collective-permute-start | bytes 1572872 | tf_op jit(solution)/shard_map/ppermute | solution.py:51
  3.0 13.6 %collective-permute-start.3 = (bf16[1024,256]{1,0:T(8,128)(2,1)}, bf16[1024,256]{1,0:T(8,128)(2,1)S(1)}, u32[]{:S(2)}, u32[]{:S(2)}) collective-permute-start(bf16[1024,256]{1,0:T(8,128)(2,1)} %refs_1_.1), channel_id=1, source_target_pairs={{0,8},{8,0},{16,24},{24,16},{1,9},{9,1},{17,25},{25,17},{2,10},{10... | collective-permute-start | bytes 1572872 | tf_op jit(solution)/shard_map/ppermute | solution.py:51
  4.5 15.0 %collective-permute-start.1 = (bf16[2,64,1024]{2,1,0:T(8,128)(2,1)}, bf16[2,64,1024]{2,1,0:T(8,128)(2,1)S(1)}, u32[]{:S(2)}, u32[]{:S(2)}) collective-permute-start(bf16[2,64,1024]{2,1,0:T(8,128)(2,1)} %refs_2_.1), channel_id=1, source_target_pairs={{0,4},{1,5},{2,6},{3,7},{4,0},{5,1},{6,2},{7,3},{8,12},{9,13},{10,... | collective-permute-start | bytes 786440 | tf_op jit(solution)/shard_map/ppermute | solution.py:51
  7.0 12.4 %collective-permute-start.5 = (bf16[1024,128]{1,0:T(8,128)(2,1)}, bf16[1024,128]{1,0:T(8,128)(2,1)S(1)}, u32[]{:S(2)}, u32[]{:S(2)}) collective-permute-start(bf16[1024,128]{1,0:T(8,128)(2,1)} %refs_3_.1), channel_id=1, source_target_pairs={{0,2},{1,3},{2,0},{3,1},{4,6},{5,7},{6,4},{7,5},{8,10},{9,11},{10,... | collective-permute-start | bytes 786440 | tf_op jit(solution)/shard_map/ppermute | solution.py:51
  8.6 11.0 %collective-permute-start = (bf16[2,64,1024]{2,1,0:T(8,128)(2,1)}, bf16[2,64,1024]{2,1,0:T(8,128)(2,1)S(1)}, u32[]{:S(2)}, u32[]{:S(2)}) collective-permute-start(bf16[2,64,1024]{2,1,0:T(8,128)(2,1)} %refs_2_.1), channel_id=1, source_target_pairs={{0,1},{1,0},{2,3},{3,2},{4,5},{5,4},{6,7},{7,6},{8,9},{9,8},{10,11... | collective-permute-start | bytes 786440 | tf_op jit(solution)/shard_map/ppermute | solution.py:51
  8.6 1.0 %copy-start = (bf16[2,128,1024]{2,1,0:T(8,128)(2,1)S(1)}, bf16[2,128,1024]{2,1,0:T(8,128)(2,1)}, u32[]{:S(2)}) copy-start(bf16[2,128,1024]{2,1,0:T(8,128)(2,1)} %refs_0_.1) | copy-start | bytes 1572868
  9.7 1.0 %copy-start.1 = (bf16[1024,256]{1,0:T(8,128)(2,1)S(1)}, bf16[1024,256]{1,0:T(8,128)(2,1)}, u32[]{:S(2)}) copy-start(bf16[1024,256]{1,0:T(8,128)(2,1)} %refs_1_.1) | copy-start | bytes 1572868
  10.7 0.9 %copy-start.2 = (bf16[1024,128]{1,0:T(8,128)(2,1)S(1)}, bf16[1024,128]{1,0:T(8,128)(2,1)}, u32[]{:S(2)}) copy-start(bf16[1024,128]{1,0:T(8,128)(2,1)} %refs_3_.1) | copy-start | bytes 786436
  11.7 0.9 %copy-start.3 = (bf16[2,64,1024]{2,1,0:T(8,128)(2,1)S(1)}, bf16[2,64,1024]{2,1,0:T(8,128)(2,1)}, u32[]{:S(2)}) copy-start(bf16[2,64,1024]{2,1,0:T(8,128)(2,1)} %refs_2_.1) | copy-start | bytes 786436
  17.4 12.5 %collective-permute-start.12 = (bf16[512,512]{1,0:T(8,128)(2,1)S(1)}, bf16[512,512]{1,0:T(8,128)(2,1)S(1)}, u32[]{:S(2)}, u32[]{:S(2)}) collective-permute-start(bf16[512,512]{1,0:T(8,128)(2,1)S(1)} %shard_map.47.g0), channel_id=1, source_target_pairs={{0,16},{8,24},{16,0},{24,8},{1,17},{9,25},{17,1},{25,9},{2,18},{10... | collective-permute-start | bytes 1572872 | tf_op jit(solution)/shard_map/ppermute | solution.py:51
  17.7 12.5 %collective-permute-start.13 = (bf16[512,512]{1,0:T(8,128)(2,1)S(1)}, bf16[512,512]{1,0:T(8,128)(2,1)S(1)}, u32[]{:S(2)}, u32[]{:S(2)}) collective-permute-start(bf16[512,512]{1,0:T(8,128)(2,1)S(1)} %shard_map.47.g0), channel_id=1, source_target_pairs={{0,8},{8,0},{16,24},{24,16},{1,9},{9,1},{17,25},{25,17},{2,10},{10... | collective-permute-start | bytes 1572872 | tf_op jit(solution)/shard_map/ppermute | solution.py:51
  19.4 1.5 %collective-permute-start.4 = (bf16[2,64,1024]{2,1,0:T(8,128)(2,1)S(1)}, bf16[2,64,1024]{2,1,0:T(8,128)(2,1)S(1)}, u32[]{:S(2)}, u32[]{:S(2)}) collective-permute-start(bf16[2,64,1024]{2,1,0:T(8,128)(2,1)S(1)} %collective-permute-done.1.near_ref), channel_id=1, source_target_pairs={{0,1},{1,0},{2,3},{3,2},{4,5},{5,4},{6,7},{7,6},{8,9},{9,8},{10,11... | collective-permute-start | bytes 786440 | tf_op jit(solution)/shard_map/ppermute | solution.py:51
  21.5 15.0 %collective-permute-start.6 = (bf16[256,512]{1,0:T(8,128)(2,1)S(1)}, bf16[256,512]{1,0:T(8,128)(2,1)S(1)}, u32[]{:S(2)}, u32[]{:S(2)}) collective-permute-start(bf16[256,512]{1,0:T(8,128)(2,1)S(1)} %shard_map.49.t0), channel_id=1, source_target_pairs={{0,4},{1,5},{2,6},{3,7},{4,0},{5,1},{6,2},{7,3},{8,12},{9,13},{10,... | collective-permute-start | bytes 786440 | tf_op jit(solution)/shard_map/ppermute | solution.py:51
  24.1 12.6 %collective-permute-start.8 = (bf16[256,512]{1,0:T(8,128)(2,1)S(1)}, bf16[256,512]{1,0:T(8,128)(2,1)S(1)}, u32[]{:S(2)}, u32[]{:S(2)}) collective-permute-start(bf16[256,512]{1,0:T(8,128)(2,1)S(1)} %shard_map.49.t0), channel_id=1, source_target_pairs={{0,2},{1,3},{2,0},{3,1},{4,6},{5,7},{6,4},{7,5},{8,10},{9,11},{10,... | collective-permute-start | bytes 786440 | tf_op jit(solution)/shard_map/ppermute | solution.py:51
  30.3 9.2 %collective-permute-start.14 = (bf16[512,512]{1,0:T(8,128)(2,1)S(1)}, bf16[512,512]{1,0:T(8,128)(2,1)S(1)}, u32[]{:S(2)}, u32[]{:S(2)}) collective-permute-start(bf16[512,512]{1,0:T(8,128)(2,1)S(1)} %shard_map.51), channel_id=1, source_target_pairs={{0,8},{8,0},{16,24},{24,16},{1,17},{9,25},{17,1},{25,9},{2,10},{10... | collective-permute-start | bytes 1572872 | tf_op jit(solution)/shard_map/ppermute | solution.py:286
  31.8 6.4 %collective-permute-start.9 = (bf16[256,512]{1,0:T(8,128)(2,1)S(1)}, bf16[256,512]{1,0:T(8,128)(2,1)S(1)}, u32[]{:S(2)}, u32[]{:S(2)}) collective-permute-start(bf16[256,512]{1,0:T(8,128)(2,1)S(1)} %shard_map.49.t0), channel_id=1, source_target_pairs={{0,1},{1,0},{2,3},{3,2},{4,5},{5,4},{6,7},{7,6},{8,9},{9,8},{10,11... | collective-permute-start | bytes 786440 | tf_op jit(solution)/shard_map/ppermute | solution.py:51
  36.5 1.7 %collective-permute-start.10 = (bf16[256,512]{1,0:T(8,128)(2,1)S(1)}, bf16[256,512]{1,0:T(8,128)(2,1)S(1)}, u32[]{:S(2)}, u32[]{:S(2)}) collective-permute-start(bf16[256,512]{1,0:T(8,128)(2,1)S(1)} %collective-permute-done.6.a_ref.t1), channel_id=1, source_target_pairs={{0,1},{1,0},{2,3},{3,2},{4,5},{5,4},{6,7},{7,6},{8,9},{9,8},{10,11... | collective-permute-start | bytes 786440 | tf_op jit(solution)/shard_map/ppermute | solution.py:51
  36.7 1.7 %collective-permute-start.11 = (bf16[256,512]{1,0:T(8,128)(2,1)S(1)}, bf16[256,512]{1,0:T(8,128)(2,1)S(1)}, u32[]{:S(2)}, u32[]{:S(2)}) collective-permute-start(bf16[256,512]{1,0:T(8,128)(2,1)S(1)} %collective-permute-done.8.t2), channel_id=1, source_target_pairs={{0,1},{1,0},{2,3},{3,2},{4,5},{5,4},{6,7},{7,6},{8,9},{9,8},{10,11... | collective-permute-start | bytes 786440 | tf_op jit(solution)/shard_map/ppermute | solution.py:51
  37.1 8.5 %collective-permute-start.7 = (bf16[256,512]{1,0:T(8,128)(2,1)S(1)}, bf16[256,512]{1,0:T(8,128)(2,1)S(1)}, u32[]{:S(2)}, u32[]{:S(2)}) collective-permute-start(bf16[256,512]{1,0:T(8,128)(2,1)S(1)} %shard_map.50), channel_id=1, source_target_pairs={{0,2},{1,3},{2,0},{3,1},{4,6},{5,7},{6,4},{7,5},{8,10},{9,11},{10,... | collective-permute-start | bytes 786440 | tf_op jit(solution)/shard_map/ppermute | solution.py:51
  45.5 1.6 %collective-permute-start.15 = (bf16[256,512]{1,0:T(8,128)(2,1)S(1)}, bf16[256,512]{1,0:T(8,128)(2,1)S(1)}, u32[]{:S(2)}, u32[]{:S(2)}) collective-permute-start(bf16[256,512]{1,0:T(8,128)(2,1)S(1)} %shard_map.53.t3), channel_id=1, source_target_pairs={{0,1},{1,0},{2,3},{3,2},{4,5},{5,4},{6,7},{7,6},{8,9},{9,8},{10,11... | collective-permute-start | bytes 786440 | tf_op jit(solution)/shard_map/ppermute | solution.py:51

commit v4 on v3

--- a/solution.py
+++ b/solution.py
@@ -1,3 +1,5 @@
+import functools
+
 import jax
 import jax.numpy as jnp
 from jax import lax
@@ -146,7 +148,20 @@
     return (g / (f + damping)).astype(jnp.bfloat16)
 
 
-def early_kernel(t0, t1, t2, s0, s1, s2, g0, g1, g2, g3, top, grad, fisher, left, right, side):
+def send_rows(source, out_ref, row_tok, core, number, columns, sems):
+    size = source.shape[0] // 2
+    copies = []
+    for k in range(2):
+        here = rows_of(4 * row_tok + 2 * k + core, size)
+        copies.append(
+            pltpu.make_async_copy(source.at[k * size : (k + 1) * size, columns], out_ref.at[here, columns], sems.at[number + k])
+        )
+    for copy in copies:
+        copy.start()
+    return copies
+
+
+def early_kernel(t0, t1, t2, s0, s1, s2, g0, g1, g2, g3, out_ref, grad, fisher, left, right, side, top, sems):
     out_tok, _ = inb_digits()
     other = other_tokens()
     size, span = t0.shape
@@ -158,6 +173,8 @@
         side[at] = t_side[...]
     for half, column, tile in ((other, out_tok, g0), (1 - other, out_tok, g2), (other, 1 - out_tok, g1), (1 - other, 1 - out_tok, g3)):
         right[rows_of(half, span), rows_of(column, width)] = tile[...]
+    tok, _, core = hid_digits()
+    cores, copies = (core, 1 - core), []
     for c in range(2):
         columns = slice(c * width, (c + 1) * width)
         whole = right[:, columns]
@@ -166,41 +183,29 @@
             at = slice(k * size, (k + 1) * size)
             rows = left[at]
             top[at, columns] = ratio(dot(rows, whole), dot(squared(rows), whole_squared))
+            copies += send_rows(top.at[at, :], out_ref, tok, cores[k], 4 * c + 2 * k, columns, sems)
             rows = side[at]
             grad[at, columns] = dot(rows, whole[:span])
             fisher[at, columns] = dot(squared(rows), whole_squared[:span])
-
-
-def late_kernel(top, grad, fisher, right, t3, s3, out_ref, done, sems):
+    for copy in copies:
+        copy.wait()
+
+
+def rest_kernel(part, out_in, grad, fisher, right, t, out_ref, done, sems):
     tok, _, core = hid_digits()
-    size, span = t3.shape
-    row_size, width = size // 2, right.shape[1] // 2
+    size, span = t.shape
+    width = right.shape[1] // 2
+    at = slice(part * size, (part + 1) * size)
+    rows = t[...]
+    rows_squared = squared(rows)
     copies = []
-
-    def send(part, source, row_tok, number):
-        for k in range(2):
-            row = 4 * row_tok + 2 * k + (core if part == 0 else 1 - core)
-            copy = pltpu.make_async_copy(
-                source.at[pl.ds(part * size + k * row_size, row_size), :],
-                out_ref.at[rows_of(row, row_size), :],
-                sems.at[number + k],
-            )
-            copy.start()
-            copies.append(copy)
-
-    for part in range(2):
-        send(part, top, tok, 2 * part)
-    for part, t in enumerate((t3, s3)):
-        at = slice(part * size, (part + 1) * size)
-        rows = t[...]
-        rows_squared = squared(rows)
-        for c in range(2):
-            columns = slice(c * width, (c + 1) * width)
-            beside = right[span:, columns]
-            g = grad[at, columns] + dot(rows, beside)
-            f = fisher[at, columns] + dot(rows_squared, squared(beside))
-            done[at, columns] = ratio(g, f)
-        send(part, done, 1 - tok, 4 + 2 * part)
+    for c in range(2):
+        columns = slice(c * width, (c + 1) * width)
+        beside = right[span:, columns]
+        g = grad[at, columns] + dot(rows, beside)
+        f = fisher[at, columns] + dot(rows_squared, squared(beside))
+        done[:, columns] = ratio(g, f)
+        copies += send_rows(done, out_ref, 1 - tok, core if part == 0 else 1 - core, 2 * c, columns, sems)
     for copy in copies:
         copy.wait()
 
@@ -220,13 +225,13 @@
     tok_in, col_in = n_hid // 2, n_hid // 4
     tok_out, col_out = n_inb // 2, n_inb // 4
 
-    def call(kernel, outs, operands, scratch=(), flops=0, space=vmem, out_space=vmem):
+    def call(kernel, outs, operands, scratch=(), flops=0, space=vmem, out_specs=None):
         one = not isinstance(outs, list)
         return pl.pallas_call(
             kernel,
             out_shape=outs,
             in_specs=[space] * len(operands),
-            out_specs=out_space if one else [out_space] * len(outs),
+            out_specs=out_specs or (vmem if one else [vmem] * len(outs)),
             scratch_shapes=scratch,
             compiler_params=params,
             cost_estimate=pl.CostEstimate(flops=flops, bytes_accessed=0, transcendentals=0),
@@ -287,10 +292,10 @@
 
     half_rows, half_columns, half_tokens = 2 * tile_in[0], tile_out[1], tile_out[0]
     columns, half_out = 2 * half_columns, (half_rows, 2 * half_columns)
-    top, grad, fisher, _, right, _ = call(
+    out, grad, fisher, _, right, _ = call(
         early_kernel,
         [
-            shape(half_out, bf16),
+            shape((activations.shape[2], out_grads.shape[2]), bf16),
             shape(half_out, f32),
             shape(half_out, f32),
             shape((half_rows, 2 * half_tokens), bf16),
@@ -298,19 +303,25 @@
             shape((half_rows, half_tokens), bf16),
         ],
         (t0, t1, t2, s0, s1, s2, g0, g1, g2, g3),
+        [pltpu.VMEM(half_out, bf16), pltpu.SemaphoreType.DMA((8,))],
         flops=2000000000,
-    )
-    t3, top = lax.optimization_barrier((t3, top))
+        out_specs=[anywhere] + [vmem] * 5,
+    )
+    t3, grad = lax.optimization_barrier((t3, grad))
     t3 = call(copy_kernel, shape(tile_in, bf16), (t3,), flops=4000000000)
     s3 = hid(t3, 1)
-    return call(
-        late_kernel,
-        shape((activations.shape[2], out_grads.shape[2]), bf16),
-        (top, grad, fisher, right, t3, s3),
-        [pltpu.VMEM(half_out, bf16), pltpu.SemaphoreType.DMA((8,))],
-        flops=4 * half_rows * half_columns * half_tokens,
-        out_space=anywhere,
-    )
+    for part, tile in enumerate((t3, s3)):
+        out = pl.pallas_call(
+            functools.partial(rest_kernel, part),
+            out_shape=shape(out.shape, bf16),
+            in_specs=[anywhere] + [vmem] * 4,
+            out_specs=anywhere,
+            scratch_shapes=[pltpu.VMEM((tile_in[0], columns), bf16), pltpu.SemaphoreType.DMA((4,))],
+            input_output_aliases={0: 0},
+            compiler_params=params,
+            cost_estimate=pl.CostEstimate(flops=500000000, bytes_accessed=0, transcendentals=0),
+        )(out, grad, fisher, right, tile)
+    return out
 
 
 def solution(mesh):

time: 49.7 us -> 49 us (0.986)
  waiting for transfers between devices: 18.9 us -> 16.4 us
  Pallas kernels: 8.46 us -> 10.2 us
    pallas_call x0 -> x2, Pallas kernels: none -> 3.05 us  [paired(): pl.pallas_call(functools.partial(rest_kernel, part), out_shape=shape(out....]
    ppermute x15, waiting for transfers between devices: 17.8 us -> 15.3 us  [swap(): return lax.ppermute(values, axis, [(i, i ^ distance) for i in range(count)])]
    pallas_call x9 -> x8, Pallas kernels: 8.46 us -> 7.13 us  [call(): pl.pallas_call(kernel, out_shape=outs, in_specs=[space] * len(operands),...]
  transfers between devices with their start and end apart: 16 -> 16, of which waited for: 11 -> 10; matrix products, arithmetic and copies ran while one was open for 0% -> 0% of each run, Pallas kernels for 12% -> 18%
where the time goes in v4:
time: 49 us; the launch traced here: 48.7 us
  starting transfers between devices  18.1 us (37%)
  waiting for transfers between devices  16.4 us (33%)
  Pallas kernels  10.2 us (21%)
  local copies, waits for them, and re-layouts  3.98 us (8%)
    ppermute x15, starting transfers between devices, swap(): return lax.ppermute(values, axis, [(i, i ^ distance) for i in range(count)])  16.5 us
    ppermute x15, waiting for transfers between devices, swap(): return lax.ppermute(values, axis, [(i, i ^ distance) for i in range(count)])  15.3 us
    pallas_call x8, Pallas kernels, call(): pl.pallas_call(kernel, out_shape=outs, in_specs=[space] * len(operands),...  7.13 us
    unnamed x8, local copies, waits for them, and re-layouts  3.98 us
    pallas_call x2, Pallas kernels, paired(): pl.pallas_call(functools.partial(rest_kernel, part), out_shape=shape(out....  3.05 us
    ppermute x1, starting transfers between devices, paired(): g3 = lax.ppermute(picked, ('inb', 'hid'), onward)  1.56 us
    ppermute x1, waiting for transfers between devices, paired(): g3 = lax.ppermute(picked, ('inb', 'hid'), onward)  1.06 us
  transfers between devices with their start and end apart: 16, of which 10 were waited for; matrix products, arithmetic and copies ran while one was open for 0% of the time, Pallas kernels for 18%

profile of v4, /device:TPU:0, one launch (start us, length us, event | category | flops | bytes accessed | tf_op | source)
XLA Modules:
  0.0 48.7 jit_solution(15911660205043847738)
XLA Ops:
  0.0 3.0 %collective-permute-start.2 = (bf16[2,128,1024]{2,1,0:T(8,128)(2,1)}, bf16[2,128,1024]{2,1,0:T(8,128)(2,1)S(1)}, u32[]{:S(2)}, u32[]{:S(2)}) collective-permute-start(bf16[2,128,1024]{2,1,0:T(8,128)(2,1)} %refs_0_.1), channel_id=1, source_target_pairs={{0,16},{8,24},{16,0},{24,8},{1,17},{9,25},{17,1},{25,9},{2,18},{10... | collective-permute-start | bytes 1572872 | tf_op jit(solution)/shard_map/ppermute | solution.py:53
  3.0 1.5 %collective-permute-start.3 = (bf16[1024,256]{1,0:T(8,128)(2,1)}, bf16[1024,256]{1,0:T(8,128)(2,1)S(1)}, u32[]{:S(2)}, u32[]{:S(2)}) collective-permute-start(bf16[1024,256]{1,0:T(8,128)(2,1)} %refs_1_.1), channel_id=1, source_target_pairs={{0,8},{8,0},{16,24},{24,16},{1,9},{9,1},{17,25},{25,17},{2,10},{10... | collective-permute-start | bytes 1572872 | tf_op jit(solution)/shard_map/ppermute | solution.py:53
  4.5 2.6 %collective-permute-start.1 = (bf16[2,64,1024]{2,1,0:T(8,128)(2,1)}, bf16[2,64,1024]{2,1,0:T(8,128)(2,1)S(1)}, u32[]{:S(2)}, u32[]{:S(2)}) collective-permute-start(bf16[2,64,1024]{2,1,0:T(8,128)(2,1)} %refs_2_.1), channel_id=1, source_target_pairs={{0,4},{1,5},{2,6},{3,7},{4,0},{5,1},{6,2},{7,3},{8,12},{9,13},{10,... | collective-permute-start | bytes 786440 | tf_op jit(solution)/shard_map/ppermute | solution.py:53
  7.0 1.6 %collective-permute-start.5 = (bf16[1024,128]{1,0:T(8,128)(2,1)}, bf16[1024,128]{1,0:T(8,128)(2,1)S(1)}, u32[]{:S(2)}, u32[]{:S(2)}) collective-permute-start(bf16[1024,128]{1,0:T(8,128)(2,1)} %refs_3_.1), channel_id=1, source_target_pairs={{0,2},{1,3},{2,0},{3,1},{4,6},{5,7},{6,4},{7,5},{8,10},{9,11},{10,... | collective-permute-start | bytes 786440 | tf_op jit(solution)/shard_map/ppermute | solution.py:53
  8.6 0.0 collective-permute-start
  8.6 0.0 copy-start
  8.6 1.0 %copy-done = bf16[2,128,1024]{2,1,0:T(8,128)(2,1)S(1)} copy-done((bf16[2,128,1024]{2,1,0:T(8,128)(2,1)S(1)}, bf16[2,128,1024]{2,1,0:T(8,128)(2,1)}, u32[]{:S(2)}) %copy-start) | copy-done | bytes 524312
  9.7 0.0 copy-start.1
  9.7 1.0 %copy-done.1 = bf16[1024,256]{1,0:T(8,128)(2,1)S(1)} copy-done((bf16[1024,256]{1,0:T(8,128)(2,1)S(1)}, bf16[1024,256]{1,0:T(8,128)(2,1)}, u32[]{:S(2)}) %copy-start.1) | copy-done | bytes 524312
  10.7 0.0 copy-start.2
  10.7 0.9 %copy-done.2 = bf16[1024,128]{1,0:T(8,128)(2,1)S(1)} copy-done((bf16[1024,128]{1,0:T(8,128)(2,1)S(1)}, bf16[1024,128]{1,0:T(8,128)(2,1)}, u32[]{:S(2)}) %copy-start.2) | copy-done | bytes 262168
  11.7 0.0 copy-start.3
  11.7 0.9 %copy-done.3 = bf16[2,64,1024]{2,1,0:T(8,128)(2,1)S(1)} copy-done((bf16[2,64,1024]{2,1,0:T(8,128)(2,1)S(1)}, bf16[2,64,1024]{2,1,0:T(8,128)(2,1)}, u32[]{:S(2)}) %copy-start.3) | copy-done | bytes 262168
  12.6 0.1 shard_map.46
  12.8 2.3 %collective-permute-done.2.refs_1_ = bf16[2,128,1024]{2,1,0:T(8,128)(2,1)S(1)} collective-permute-done((bf16[2,128,1024]{2,1,0:T(8,128)(2,1)}, bf16[2,128,1024]{2,1,0:T(8,128)(2,1)S(1)}, u32[]{:S(2)}, u32[]{:S(2)}) %collective-permute-start.2) | collective-permute-done | bytes 524320 | tf_op jit(solution)/shard_map/ppermute | solution.py:53
  15.1 1.5 %collective-permute-done.3.refs_3_ = bf16[1024,256]{1,0:T(8,128)(2,1)S(1)} collective-permute-done((bf16[1024,256]{1,0:T(8,128)(2,1)}, bf16[1024,256]{1,0:T(8,128)(2,1)S(1)}, u32[]{:S(2)}, u32[]{:S(2)}) %collective-permute-start.3) | collective-permute-done | bytes 524320 | tf_op jit(solution)/shard_map/ppermute | solution.py:53
  16.6 0.8 %shard_map.47.g0 = bf16[512,512]{1,0:T(8,128)(2,1)S(1)} custom-call(bf16[2,128,1024]{2,1,0:T(8,128)(2,1)S(1)} %get-tuple-element.19.refs_0_, bf16[2,128,1024]{2,1,0:T(8,128)(2,1)S(1)} %collective-permute-done.2.refs_1_, bf16[1024,256]{1,0:T(8,128)(2,1)S(1)} %get-tuple-element.20.refs_2_, bf16[1024,256]{1,0:T(8,128)(2,1)S(1)} %collective-permute-done.3.refs_3_), custom_call_target="tpu_custom_call" | custom-call | flops 536870912 | tf_op jit(solution)/shard_map/pallas_call | solution.py:230
  17.4 0.3 collective-permute-start.11
  17.7 1.7 %collective-permute-start.12 = (bf16[512,512]{1,0:T(8,128)(2,1)S(1)}, bf16[512,512]{1,0:T(8,128)(2,1)S(1)}, u32[]{:S(2)}, u32[]{:S(2)}) collective-permute-start(bf16[512,512]{1,0:T(8,128)(2,1)S(1)} %shard_map.47.g0), channel_id=1, source_target_pairs={{0,8},{8,0},{16,24},{24,16},{1,9},{9,1},{17,25},{25,17},{2,10},{10... | collective-permute-start | bytes 1572872 | tf_op jit(solution)/shard_map/ppermute | solution.py:53
  19.4 0.0 collective-permute-done.1.near_ref
  19.4 0.0 collective-permute-start.4
  19.4 0.0 collective-permute-done.5.far_ref
  19.4 0.2 shard_map.48.weights
  19.6 0.0 collective-permute-done.core_ref
  19.6 1.4 %collective-permute-done.4.near_core_ref = bf16[2,64,1024]{2,1,0:T(8,128)(2,1)S(1)} collective-permute-done((bf16[2,64,1024]{2,1,0:T(8,128)(2,1)S(1)}, bf16[2,64,1024]{2,1,0:T(8,128)(2,1)S(1)}, u32[]{:S(2)}, u32[]{:S(2)}) %collective-permute-start.4) | collective-permute-done | bytes 262176 | tf_op jit(solution)/shard_map/ppermute | solution.py:53
  21.0 0.5 %shard_map.49.t0 = bf16[256,512]{1,0:T(8,128)(2,1)S(1)} custom-call(bf16[2,64,1024]{2,1,0:T(8,128)(2,1)S(1)} %get-tuple-element.18.own_ref, bf16[2,64,1024]{2,1,0:T(8,128)(2,1)S(1)} %collective-permute-done.core_ref, bf16[2,64,1024]{2,1,0:T(8,128)(2,1)S(1)} %collective-permute-done.1.near_ref, bf16[2,64,1024]{2,1,0:T(8,128)(2,1)S(1)} %collective-permute-done.4.near_core_ref, ...), custom_call_target="tpu_custom_call" | custom-call | flops 2268435456 | tf_op jit(solution)/shard_map/pallas_call | solution.py:230
  21.5 2.7 %collective-permute-start.6 = (bf16[256,512]{1,0:T(8,128)(2,1)S(1)}, bf16[256,512]{1,0:T(8,128)(2,1)S(1)}, u32[]{:S(2)}, u32[]{:S(2)}) collective-permute-start(bf16[256,512]{1,0:T(8,128)(2,1)S(1)} %shard_map.49.t0), channel_id=1, source_target_pairs={{0,4},{1,5},{2,6},{3,7},{4,0},{5,1},{6,2},{7,3},{8,12},{9,13},{10,... | collective-permute-start | bytes 786440 | tf_op jit(solution)/shard_map/ppermute | solution.py:53
  24.1 1.6 %collective-permute-start.7 = (bf16[256,512]{1,0:T(8,128)(2,1)S(1)}, bf16[256,512]{1,0:T(8,128)(2,1)S(1)}, u32[]{:S(2)}, u32[]{:S(2)}) collective-permute-start(bf16[256,512]{1,0:T(8,128)(2,1)S(1)} %shard_map.49.t0), channel_id=1, source_target_pairs={{0,2},{1,3},{2,0},{3,1},{4,6},{5,7},{6,4},{7,5},{8,10},{9,11},{10,... | collective-permute-start | bytes 786440 | tf_op jit(solution)/shard_map/ppermute | solution.py:53
  25.7 4.2 %collective-permute-done.11.refs_0_.g1 = bf16[512,512]{1,0:T(8,128)(2,1)S(1)} collective-permute-done((bf16[512,512]{1,0:T(8,128)(2,1)S(1)}, bf16[512,512]{1,0:T(8,128)(2,1)S(1)}, u32[]{:S(2)}, u32[]{:S(2)}) %collective-permute-start.11) | collective-permute-done | bytes 524320 | tf_op jit(solution)/shard_map/ppermute | solution.py:53
  29.9 0.3 collective-permute-done.12.refs_1_.g2
  30.3 1.6 %collective-permute-start.13 = (bf16[512,512]{1,0:T(8,128)(2,1)S(1)}, bf16[512,512]{1,0:T(8,128)(2,1)S(1)}, u32[]{:S(2)}, u32[]{:S(2)}) collective-permute-start(bf16[512,512]{1,0:T(8,128)(2,1)S(1)} %shard_map.50), channel_id=1, source_target_pairs={{0,8},{8,0},{16,24},{24,16},{1,17},{9,25},{17,1},{25,9},{2,10},{10... | collective-permute-start | bytes 1572872 | tf_op jit(solution)/shard_map/ppermute | solution.py:291
  31.8 0.0 collective-permute-start.8
  31.8 4.7 %collective-permute-done.6.t1.a_ref = bf16[256,512]{1,0:T(8,128)(2,1)S(1)} collective-permute-done((bf16[256,512]{1,0:T(8,128)(2,1)S(1)}, bf16[256,512]{1,0:T(8,128)(2,1)S(1)}, u32[]{:S(2)}, u32[]{:S(2)}) %collective-permute-start.6) | collective-permute-done | bytes 262176 | tf_op jit(solution)/shard_map/ppermute | solution.py:53
  36.5 0.0 collective-permute-start.9
  36.5 0.2 collective-permute-done.7.t2
  36.7 0.3 collective-permute-start.10
  37.1 1.2 %collective-permute-start.14 = (bf16[256,512]{1,0:T(8,128)(2,1)S(1)}, bf16[256,512]{1,0:T(8,128)(2,1)S(1)}, u32[]{:S(2)}, u32[]{:S(2)}) collective-permute-start(bf16[256,512]{1,0:T(8,128)(2,1)S(1)} %shard_map.52), channel_id=1, source_target_pairs={{0,2},{1,3},{2,0},{3,1},{4,6},{5,7},{6,4},{7,5},{8,10},{9,11},{10,... | collective-permute-start | bytes 786440 | tf_op jit(solution)/shard_map/ppermute | solution.py:53
  38.2 0.0 collective-permute-done.8.s0
  38.3 0.0 collective-permute-done.9.s1
  38.3 0.2 collective-permute-done.10.s2
  38.4 1.1 %collective-permute-done.13.g3 = bf16[512,512]{1,0:T(8,128)(2,1)S(1)} collective-permute-done((bf16[512,512]{1,0:T(8,128)(2,1)S(1)}, bf16[512,512]{1,0:T(8,128)(2,1)S(1)}, u32[]{:S(2)}, u32[]{:S(2)}) %collective-permute-start.13) | collective-permute-done | bytes 524320 | tf_op jit(solution)/shard_map/ppermute | solution.py:291
  39.5 5.4 %shard_map.51 = (bf16[1024,1024]{1,0:T(8,128)(2,1)}, f32[512,1024]{1,0:T(8,128)S(1)}, f32[512,1024]{1,0:T(8,128)S(1)}, bf16[512,1024]{1,0:T(8,128)(2,1)}, bf16[1...) custom-call(bf16[256,512]{1,0:T(8,128)(2,1)S(1)} %shard_map.49.t0, ...), custom_call_target="tpu_custom_call" | custom-call | flops 2000000000 | tf_op jit(solution)/shard_map/pallas_call | solution.py:230
  45.0 0.6 %collective-permute-done.14.a_ref = bf16[256,512]{1,0:T(8,128)(2,1)S(1)} collective-permute-done((bf16[256,512]{1,0:T(8,128)(2,1)S(1)}, bf16[256,512]{1,0:T(8,128)(2,1)S(1)}, u32[]{:S(2)}, u32[]{:S(2)}) %collective-permute-start.14) | collective-permute-done | bytes 262176 | tf_op jit(solution)/shard_map/ppermute | solution.py:53
  45.5 0.1 collective-permute-start.15
  45.6 1.5 %shard_map.54.out_in = bf16[1024,1024]{1,0:T(8,128)(2,1)} custom-call(bf16[1024,1024]{1,0:T(8,128)(2,1)} %get-tuple-element.25.out_in, f32[512,1024]{1,0:T(8,128)S(1)} %get-tuple-element.27.grad, f32[512,1024]{1,0:T(8,128)S(1)} %get-tuple-element.28.fisher, bf16[1024,1024]{1,0:T(8,128)(2,1)S(1)} %get-tuple-element.29.right, ...), custom_call_target="tpu_custom_call", output_to_operand_aliasing={{}: (0, {})} | custom-call | flops 500000000 | tf_op jit(solution)/shard_map/pallas_call | solution.py:314
  47.2 0.0 collective-permute-done.15.t
  47.2 1.5 %shard_map.55 = bf16[1024,1024]{1,0:T(8,128)(2,1)} custom-call(bf16[1024,1024]{1,0:T(8,128)(2,1)} %shard_map.54.out_in, f32[512,1024]{1,0:T(8,128)S(1)} %get-tuple-element.27.grad, f32[512,1024]{1,0:T(8,128)S(1)} %get-tuple-element.28.fisher, bf16[1024,1024]{1,0:T(8,128)(2,1)S(1)} %get-tuple-element.29.right, ...), custom_call_target="tpu_custom_call", output_to_operand_aliasing={{}: (0, {})} | custom-call | flops 500000000 | tf_op jit(solution)/shard_map/pallas_call | solution.py:314
  (3 shorter events, 0.1 us)
Async XLA Ops:
  0.0 15.1 %collective-permute-start.2 = (bf16[2,128,1024]{2,1,0:T(8,128)(2,1)}, bf16[2,128,1024]{2,1,0:T(8,128)(2,1)S(1)}, u32[]{:S(2)}, u32[]{:S(2)}) collective-permute-start(bf16[2,128,1024]{2,1,0:T(8,128)(2,1)} %refs_0_.1), channel_id=1, source_target_pairs={{0,16},{8,24},{16,0},{24,8},{1,17},{9,25},{17,1},{25,9},{2,18},{10... | collective-permute-start | bytes 1572872 | tf_op jit(solution)/shard_map/ppermute | solution.py:53
  3.0 13.6 %collective-permute-start.3 = (bf16[1024,256]{1,0:T(8,128)(2,1)}, bf16[1024,256]{1,0:T(8,128)(2,1)S(1)}, u32[]{:S(2)}, u32[]{:S(2)}) collective-permute-start(bf16[1024,256]{1,0:T(8,128)(2,1)} %refs_1_.1), channel_id=1, source_target_pairs={{0,8},{8,0},{16,24},{24,16},{1,9},{9,1},{17,25},{25,17},{2,10},{10... | collective-permute-start | bytes 1572872 | tf_op jit(solution)/shard_map/ppermute | solution.py:53
  4.5 15.0 %collective-permute-start.1 = (bf16[2,64,1024]{2,1,0:T(8,128)(2,1)}, bf16[2,64,1024]{2,1,0:T(8,128)(2,1)S(1)}, u32[]{:S(2)}, u32[]{:S(2)}) collective-permute-start(bf16[2,64,1024]{2,1,0:T(8,128)(2,1)} %refs_2_.1), channel_id=1, source_target_pairs={{0,4},{1,5},{2,6},{3,7},{4,0},{5,1},{6,2},{7,3},{8,12},{9,13},{10,... | collective-permute-start | bytes 786440 | tf_op jit(solution)/shard_map/ppermute | solution.py:53
  7.0 12.4 %collective-permute-start.5 = (bf16[1024,128]{1,0:T(8,128)(2,1)}, bf16[1024,128]{1,0:T(8,128)(2,1)S(1)}, u32[]{:S(2)}, u32[]{:S(2)}) collective-permute-start(bf16[1024,128]{1,0:T(8,128)(2,1)} %refs_3_.1), channel_id=1, source_target_pairs={{0,2},{1,3},{2,0},{3,1},{4,6},{5,7},{6,4},{7,5},{8,10},{9,11},{10,... | collective-permute-start | bytes 786440 | tf_op jit(solution)/shard_map/ppermute | solution.py:53
  8.6 11.0 %collective-permute-start = (bf16[2,64,1024]{2,1,0:T(8,128)(2,1)}, bf16[2,64,1024]{2,1,0:T(8,128)(2,1)S(1)}, u32[]{:S(2)}, u32[]{:S(2)}) collective-permute-start(bf16[2,64,1024]{2,1,0:T(8,128)(2,1)} %refs_2_.1), channel_id=1, source_target_pairs={{0,1},{1,0},{2,3},{3,2},{4,5},{5,4},{6,7},{7,6},{8,9},{9,8},{10,11... | collective-permute-start | bytes 786440 | tf_op jit(solution)/shard_map/ppermute | solution.py:53
  8.6 1.0 %copy-start = (bf16[2,128,1024]{2,1,0:T(8,128)(2,1)S(1)}, bf16[2,128,1024]{2,1,0:T(8,128)(2,1)}, u32[]{:S(2)}) copy-start(bf16[2,128,1024]{2,1,0:T(8,128)(2,1)} %refs_0_.1) | copy-start | bytes 1572868
  9.7 1.0 %copy-start.1 = (bf16[1024,256]{1,0:T(8,128)(2,1)S(1)}, bf16[1024,256]{1,0:T(8,128)(2,1)}, u32[]{:S(2)}) copy-start(bf16[1024,256]{1,0:T(8,128)(2,1)} %refs_1_.1) | copy-start | bytes 1572868
  10.7 0.9 %copy-start.2 = (bf16[1024,128]{1,0:T(8,128)(2,1)S(1)}, bf16[1024,128]{1,0:T(8,128)(2,1)}, u32[]{:S(2)}) copy-start(bf16[1024,128]{1,0:T(8,128)(2,1)} %refs_3_.1) | copy-start | bytes 786436
  11.7 0.9 %copy-start.3 = (bf16[2,64,1024]{2,1,0:T(8,128)(2,1)S(1)}, bf16[2,64,1024]{2,1,0:T(8,128)(2,1)}, u32[]{:S(2)}) copy-start(bf16[2,64,1024]{2,1,0:T(8,128)(2,1)} %refs_2_.1) | copy-start | bytes 786436
  17.4 12.5 %collective-permute-start.11 = (bf16[512,512]{1,0:T(8,128)(2,1)S(1)}, bf16[512,512]{1,0:T(8,128)(2,1)S(1)}, u32[]{:S(2)}, u32[]{:S(2)}) collective-permute-start(bf16[512,512]{1,0:T(8,128)(2,1)S(1)} %shard_map.47.g0), channel_id=1, source_target_pairs={{0,16},{8,24},{16,0},{24,8},{1,17},{9,25},{17,1},{25,9},{2,18},{10... | collective-permute-start | bytes 1572872 | tf_op jit(solution)/shard_map/ppermute | solution.py:53
  17.7 12.5 %collective-permute-start.12 = (bf16[512,512]{1,0:T(8,128)(2,1)S(1)}, bf16[512,512]{1,0:T(8,128)(2,1)S(1)}, u32[]{:S(2)}, u32[]{:S(2)}) collective-permute-start(bf16[512,512]{1,0:T(8,128)(2,1)S(1)} %shard_map.47.g0), channel_id=1, source_target_pairs={{0,8},{8,0},{16,24},{24,16},{1,9},{9,1},{17,25},{25,17},{2,10},{10... | collective-permute-start | bytes 1572872 | tf_op jit(solution)/shard_map/ppermute | solution.py:53
  19.4 1.5 %collective-permute-start.4 = (bf16[2,64,1024]{2,1,0:T(8,128)(2,1)S(1)}, bf16[2,64,1024]{2,1,0:T(8,128)(2,1)S(1)}, u32[]{:S(2)}, u32[]{:S(2)}) collective-permute-start(bf16[2,64,1024]{2,1,0:T(8,128)(2,1)S(1)} %collective-permute-done.1.near_ref), channel_id=1, source_target_pairs={{0,1},{1,0},{2,3},{3,2},{4,5},{5,4},{6,7},{7,6},{8,9},{9,8},{10,11... | collective-permute-start | bytes 786440 | tf_op jit(solution)/shard_map/ppermute | solution.py:53
  21.5 15.0 %collective-permute-start.6 = (bf16[256,512]{1,0:T(8,128)(2,1)S(1)}, bf16[256,512]{1,0:T(8,128)(2,1)S(1)}, u32[]{:S(2)}, u32[]{:S(2)}) collective-permute-start(bf16[256,512]{1,0:T(8,128)(2,1)S(1)} %shard_map.49.t0), channel_id=1, source_target_pairs={{0,4},{1,5},{2,6},{3,7},{4,0},{5,1},{6,2},{7,3},{8,12},{9,13},{10,... | collective-permute-start | bytes 786440 | tf_op jit(solution)/shard_map/ppermute | solution.py:53
  24.1 12.6 %collective-permute-start.7 = (bf16[256,512]{1,0:T(8,128)(2,1)S(1)}, bf16[256,512]{1,0:T(8,128)(2,1)S(1)}, u32[]{:S(2)}, u32[]{:S(2)}) collective-permute-start(bf16[256,512]{1,0:T(8,128)(2,1)S(1)} %shard_map.49.t0), channel_id=1, source_target_pairs={{0,2},{1,3},{2,0},{3,1},{4,6},{5,7},{6,4},{7,5},{8,10},{9,11},{10,... | collective-permute-start | bytes 786440 | tf_op jit(solution)/shard_map/ppermute | solution.py:53
  30.3 9.2 %collective-permute-start.13 = (bf16[512,512]{1,0:T(8,128)(2,1)S(1)}, bf16[512,512]{1,0:T(8,128)(2,1)S(1)}, u32[]{:S(2)}, u32[]{:S(2)}) collective-permute-start(bf16[512,512]{1,0:T(8,128)(2,1)S(1)} %shard_map.50), channel_id=1, source_target_pairs={{0,8},{8,0},{16,24},{24,16},{1,17},{9,25},{17,1},{25,9},{2,10},{10... | collective-permute-start | bytes 1572872 | tf_op jit(solution)/shard_map/ppermute | solution.py:291
  31.8 6.4 %collective-permute-start.8 = (bf16[256,512]{1,0:T(8,128)(2,1)S(1)}, bf16[256,512]{1,0:T(8,128)(2,1)S(1)}, u32[]{:S(2)}, u32[]{:S(2)}) collective-permute-start(bf16[256,512]{1,0:T(8,128)(2,1)S(1)} %shard_map.49.t0), channel_id=1, source_target_pairs={{0,1},{1,0},{2,3},{3,2},{4,5},{5,4},{6,7},{7,6},{8,9},{9,8},{10,11... | collective-permute-start | bytes 786440 | tf_op jit(solution)/shard_map/ppermute | solution.py:53
  36.5 1.7 %collective-permute-start.9 = (bf16[256,512]{1,0:T(8,128)(2,1)S(1)}, bf16[256,512]{1,0:T(8,128)(2,1)S(1)}, u32[]{:S(2)}, u32[]{:S(2)}) collective-permute-start(bf16[256,512]{1,0:T(8,128)(2,1)S(1)} %collective-permute-done.6.t1.a_ref), channel_id=1, source_target_pairs={{0,1},{1,0},{2,3},{3,2},{4,5},{5,4},{6,7},{7,6},{8,9},{9,8},{10,11... | collective-permute-start | bytes 786440 | tf_op jit(solution)/shard_map/ppermute | solution.py:53
  36.7 1.7 %collective-permute-start.10 = (bf16[256,512]{1,0:T(8,128)(2,1)S(1)}, bf16[256,512]{1,0:T(8,128)(2,1)S(1)}, u32[]{:S(2)}, u32[]{:S(2)}) collective-permute-start(bf16[256,512]{1,0:T(8,128)(2,1)S(1)} %collective-permute-done.7.t2), channel_id=1, source_target_pairs={{0,1},{1,0},{2,3},{3,2},{4,5},{5,4},{6,7},{7,6},{8,9},{9,8},{10,11... | collective-permute-start | bytes 786440 | tf_op jit(solution)/shard_map/ppermute | solution.py:53
  37.1 8.5 %collective-permute-start.14 = (bf16[256,512]{1,0:T(8,128)(2,1)S(1)}, bf16[256,512]{1,0:T(8,128)(2,1)S(1)}, u32[]{:S(2)}, u32[]{:S(2)}) collective-permute-start(bf16[256,512]{1,0:T(8,128)(2,1)S(1)} %shard_map.52), channel_id=1, source_target_pairs={{0,2},{1,3},{2,0},{3,1},{4,6},{5,7},{6,4},{7,5},{8,10},{9,11},{10,... | collective-permute-start | bytes 786440 | tf_op jit(solution)/shard_map/ppermute | solution.py:53
  45.5 1.6 %collective-permute-start.15 = (bf16[256,512]{1,0:T(8,128)(2,1)S(1)}, bf16[256,512]{1,0:T(8,128)(2,1)S(1)}, u32[]{:S(2)}, u32[]{:S(2)}) collective-permute-start(bf16[256,512]{1,0:T(8,128)(2,1)S(1)} %shard_map.53.t), channel_id=1, source_target_pairs={{0,1},{1,0},{2,3},{3,2},{4,5},{5,4},{6,7},{7,6},{8,9},{9,8},{10,11... | collective-permute-start | bytes 786440 | tf_op jit(solution)/shard_map/ppermute | solution.py:53

commit v5 on v4

--- a/solution.py
+++ b/solution.py
@@ -1,5 +1,3 @@
-import functools
-
 import jax
 import jax.numpy as jnp
 from jax import lax
@@ -161,16 +159,15 @@
     return copies
 
 
-def early_kernel(t0, t1, t2, s0, s1, s2, g0, g1, g2, g3, out_ref, grad, fisher, left, right, side, top, sems):
+def early_kernel(t0, t2, s0, s1, s2, g0, g1, g2, g3, out_ref, grad, fisher, left, right, top, sems):
     out_tok, _ = inb_digits()
     other = other_tokens()
     size, span = t0.shape
     width = g0.shape[1]
-    for k, (t, t_far, t_side) in enumerate(((t0, t2, t1), (s0, s2, s1))):
+    for k, (t, t_far) in enumerate(((t0, t2), (s0, s2))):
         at = slice(k * size, (k + 1) * size)
         left[at, :span] = t[...]
         left[at, span:] = t_far[...]
-        side[at] = t_side[...]
     for half, column, tile in ((other, out_tok, g0), (1 - other, out_tok, g2), (other, 1 - out_tok, g1), (1 - other, 1 - out_tok, g3)):
         right[rows_of(half, span), rows_of(column, width)] = tile[...]
     tok, _, core = hid_digits()
@@ -184,28 +181,39 @@
             rows = left[at]
             top[at, columns] = ratio(dot(rows, whole), dot(squared(rows), whole_squared))
             copies += send_rows(top.at[at, :], out_ref, tok, cores[k], 4 * c + 2 * k, columns, sems)
-            rows = side[at]
-            grad[at, columns] = dot(rows, whole[:span])
-            fisher[at, columns] = dot(squared(rows), whole_squared[:span])
+        rows = s1[...]
+        grad[:, columns] = dot(rows, whole[:span])
+        fisher[:, columns] = dot(squared(rows), whole_squared[:span])
     for copy in copies:
         copy.wait()
 
 
-def rest_kernel(part, out_in, grad, fisher, right, t, out_ref, done, sems):
+def middle_kernel(right, t1, t3, done, rows):
+    span = t1.shape[1]
+    width = right.shape[1] // 2
+    rows[:, :span] = t1[...]
+    rows[:, span:] = t3[...]
+    values = rows[...]
+    values_squared = squared(values)
+    for c in range(2):
+        columns = slice(c * width, (c + 1) * width)
+        beside = right[:, columns]
+        done[:, columns] = ratio(dot(values, beside), dot(values_squared, squared(beside)))
+
+
+def late_kernel(out_in, first, grad, fisher, right, s, out_ref, done, sems):
     tok, _, core = hid_digits()
-    size, span = t.shape
-    width = right.shape[1] // 2
-    at = slice(part * size, (part + 1) * size)
-    rows = t[...]
+    span, width = s.shape[1], right.shape[1] // 2
+    copies = send_rows(first, out_ref, 1 - tok, core, 0, slice(0, done.shape[1]), sems)
+    rows = s[...]
     rows_squared = squared(rows)
-    copies = []
     for c in range(2):
         columns = slice(c * width, (c + 1) * width)
         beside = right[span:, columns]
-        g = grad[at, columns] + dot(rows, beside)
-        f = fisher[at, columns] + dot(rows_squared, squared(beside))
+        g = grad[:, columns] + dot(rows, beside)
+        f = fisher[:, columns] + dot(rows_squared, squared(beside))
         done[:, columns] = ratio(g, f)
-        copies += send_rows(done, out_ref, 1 - tok, core if part == 0 else 1 - core, 2 * c, columns, sems)
+        copies += send_rows(done, out_ref, 1 - tok, 1 - core, 2 + 2 * c, columns, sems)
     for copy in copies:
         copy.wait()
 
@@ -278,10 +286,11 @@
     g1 = inb(g0, tok_out)
     g2 = inb(g0, col_out)
     s0 = hid(t0, 1)
-    s1 = hid(t1, 1)
-    s2 = hid(t2, 1)
     t1_then = call(copy_kernel, shape(tile_in, bf16), (t1,), flops=4000000000)
     t3 = hid(t1_then, col_in)
+    s1 = hid(t1_then, 1)
+    t2_then, _ = lax.optimization_barrier((t2, t1_then))
+    s2 = hid(t2_then, 1)
     onward = []
     for h in range(n_hid):
         step = col_out if h % 2 == 0 else tok_out
@@ -292,36 +301,40 @@
 
     half_rows, half_columns, half_tokens = 2 * tile_in[0], tile_out[1], tile_out[0]
     columns, half_out = 2 * half_columns, (half_rows, 2 * half_columns)
-    out, grad, fisher, _, right, _ = call(
+    part_rows = (tile_in[0], columns)
+    out, grad, fisher, _, right = call(
         early_kernel,
         [
             shape((activations.shape[2], out_grads.shape[2]), bf16),
-            shape(half_out, f32),
-            shape(half_out, f32),
+            shape(part_rows, f32),
+            shape(part_rows, f32),
             shape((half_rows, 2 * half_tokens), bf16),
             shape((2 * half_tokens, columns), bf16),
-            shape((half_rows, half_tokens), bf16),
         ],
-        (t0, t1, t2, s0, s1, s2, g0, g1, g2, g3),
+        (t0, t2_then, s0, s1, s2, g0, g1, g2, g3),
         [pltpu.VMEM(half_out, bf16), pltpu.SemaphoreType.DMA((8,))],
-        flops=2000000000,
-        out_specs=[anywhere] + [vmem] * 5,
+        flops=0,
+        out_specs=[anywhere] + [vmem] * 4,
     )
     t3, grad = lax.optimization_barrier((t3, grad))
     t3 = call(copy_kernel, shape(tile_in, bf16), (t3,), flops=4000000000)
     s3 = hid(t3, 1)
-    for part, tile in enumerate((t3, s3)):
-        out = pl.pallas_call(
-            functools.partial(rest_kernel, part),
-            out_shape=shape(out.shape, bf16),
-            in_specs=[anywhere] + [vmem] * 4,
-            out_specs=anywhere,
-            scratch_shapes=[pltpu.VMEM((tile_in[0], columns), bf16), pltpu.SemaphoreType.DMA((4,))],
-            input_output_aliases={0: 0},
-            compiler_params=params,
-            cost_estimate=pl.CostEstimate(flops=500000000, bytes_accessed=0, transcendentals=0),
-        )(out, grad, fisher, right, tile)
-    return out
+    first = call(
+        middle_kernel,
+        shape(part_rows, bf16),
+        (right, t1_then, t3),
+        [pltpu.VMEM((tile_in[0], 2 * half_tokens), bf16)],
+        flops=500000000,
+    )
+    return pl.pallas_call(
+        late_kernel,
+        out_shape=shape(out.shape, bf16),
+        in_specs=[anywhere] + [vmem] * 5,
+        out_specs=anywhere,
+        scratch_shapes=[pltpu.VMEM(part_rows, bf16), pltpu.SemaphoreType.DMA((6,))],
+        input_output_aliases={0: 0},
+        compiler_params=params,
+    )(out, first, grad, fisher, right, s3)
 
 
 def solution(mesh):

time: 49 us -> 48.9 us (level)
  Pallas kernels: 10.2 us -> 9.1 us
  waiting for transfers between devices: 16.4 us -> 16.9 us
    pallas_call x2 -> x1, Pallas kernels: 3.05 us -> 1.56 us  [paired(): pl.pallas_call(late_kernel, out_shape=shape(out.shape, bf16), in_specs=[a...]
    ppermute x15, waiting for transfers between devices: 15.3 us -> 16.1 us  [swap(): return lax.ppermute(values, axis, [(i, i ^ distance) for i in range(count)])]
    pallas_call x8 -> x9, Pallas kernels: 7.13 us -> 7.54 us  [call(): pl.pallas_call(kernel, out_shape=outs, in_specs=[space] * len(operands),...]
  transfers between devices with their start and end apart: 16 -> 16, of which waited for: 10 -> 10; matrix products, arithmetic and copies ran while one was open for 0% -> 0% of each run, Pallas kernels for 18% -> 15%
where the time goes in v5:
time: 48.9 us; the launch traced here: 48.6 us
  starting transfers between devices  18.5 us (38%)
  waiting for transfers between devices  16.9 us (35%)
  Pallas kernels  9.1 us (19%)
  local copies, waits for them, and re-layouts  3.98 us (8%)
    ppermute x15, starting transfers between devices, swap(): return lax.ppermute(values, axis, [(i, i ^ distance) for i in range(count)])  16.9 us
    ppermute x15, waiting for transfers between devices, swap(): return lax.ppermute(values, axis, [(i, i ^ distance) for i in range(count)])  16.1 us
    pallas_call x9, Pallas kernels, call(): pl.pallas_call(kernel, out_shape=outs, in_specs=[space] * len(operands),...  7.54 us
    unnamed x8, local copies, waits for them, and re-layouts  3.98 us
    ppermute x1, starting transfers between devices, paired(): g3 = lax.ppermute(picked, ('inb', 'hid'), onward)  1.56 us
    pallas_call x1, Pallas kernels, paired(): pl.pallas_call(late_kernel, out_shape=shape(out.shape, bf16), in_specs=[a...  1.56 us
  transfers between devices with their start and end apart: 16, of which 10 were waited for; matrix products, arithmetic and copies ran while one was open for 0% of the time, Pallas kernels for 15%

profile of v5, /device:TPU:0, one launch (start us, length us, event | category | flops | bytes accessed | tf_op | source)
XLA Modules:
  0.0 48.6 jit_solution(9331261938289347073)
XLA Ops:
  0.0 3.0 %collective-permute-start.2 = (bf16[2,128,1024]{2,1,0:T(8,128)(2,1)}, bf16[2,128,1024]{2,1,0:T(8,128)(2,1)S(1)}, u32[]{:S(2)}, u32[]{:S(2)}) collective-permute-start(bf16[2,128,1024]{2,1,0:T(8,128)(2,1)} %refs_0_.1), channel_id=1, source_target_pairs={{0,16},{8,24},{16,0},{24,8},{1,17},{9,25},{17,1},{25,9},{2,18},{10... | collective-permute-start | bytes 1572872 | tf_op jit(solution)/shard_map/ppermute | solution.py:51
  3.0 1.5 %collective-permute-start.3 = (bf16[1024,256]{1,0:T(8,128)(2,1)}, bf16[1024,256]{1,0:T(8,128)(2,1)S(1)}, u32[]{:S(2)}, u32[]{:S(2)}) collective-permute-start(bf16[1024,256]{1,0:T(8,128)(2,1)} %refs_1_.1), channel_id=1, source_target_pairs={{0,8},{8,0},{16,24},{24,16},{1,9},{9,1},{17,25},{25,17},{2,10},{10... | collective-permute-start | bytes 1572872 | tf_op jit(solution)/shard_map/ppermute | solution.py:51
  4.5 2.6 %collective-permute-start.1 = (bf16[2,64,1024]{2,1,0:T(8,128)(2,1)}, bf16[2,64,1024]{2,1,0:T(8,128)(2,1)S(1)}, u32[]{:S(2)}, u32[]{:S(2)}) collective-permute-start(bf16[2,64,1024]{2,1,0:T(8,128)(2,1)} %refs_2_.1), channel_id=1, source_target_pairs={{0,4},{1,5},{2,6},{3,7},{4,0},{5,1},{6,2},{7,3},{8,12},{9,13},{10,... | collective-permute-start | bytes 786440 | tf_op jit(solution)/shard_map/ppermute | solution.py:51
  7.0 1.6 %collective-permute-start.5 = (bf16[1024,128]{1,0:T(8,128)(2,1)}, bf16[1024,128]{1,0:T(8,128)(2,1)S(1)}, u32[]{:S(2)}, u32[]{:S(2)}) collective-permute-start(bf16[1024,128]{1,0:T(8,128)(2,1)} %refs_3_.1), channel_id=1, source_target_pairs={{0,2},{1,3},{2,0},{3,1},{4,6},{5,7},{6,4},{7,5},{8,10},{9,11},{10,... | collective-permute-start | bytes 786440 | tf_op jit(solution)/shard_map/ppermute | solution.py:51
  8.6 0.0 collective-permute-start
  8.6 0.0 copy-start
  8.6 1.0 %copy-done = bf16[2,128,1024]{2,1,0:T(8,128)(2,1)S(1)} copy-done((bf16[2,128,1024]{2,1,0:T(8,128)(2,1)S(1)}, bf16[2,128,1024]{2,1,0:T(8,128)(2,1)}, u32[]{:S(2)}) %copy-start) | copy-done | bytes 524312
  9.7 0.0 copy-start.1
  9.7 1.0 %copy-done.1 = bf16[1024,256]{1,0:T(8,128)(2,1)S(1)} copy-done((bf16[1024,256]{1,0:T(8,128)(2,1)S(1)}, bf16[1024,256]{1,0:T(8,128)(2,1)}, u32[]{:S(2)}) %copy-start.1) | copy-done | bytes 524312
  10.7 0.0 copy-start.2
  10.7 0.9 %copy-done.2 = bf16[1024,128]{1,0:T(8,128)(2,1)S(1)} copy-done((bf16[1024,128]{1,0:T(8,128)(2,1)S(1)}, bf16[1024,128]{1,0:T(8,128)(2,1)}, u32[]{:S(2)}) %copy-start.2) | copy-done | bytes 262168
  11.7 0.0 copy-start.3
  11.7 0.9 %copy-done.3 = bf16[2,64,1024]{2,1,0:T(8,128)(2,1)S(1)} copy-done((bf16[2,64,1024]{2,1,0:T(8,128)(2,1)S(1)}, bf16[2,64,1024]{2,1,0:T(8,128)(2,1)}, u32[]{:S(2)}) %copy-start.3) | copy-done | bytes 262168
  12.6 0.1 shard_map.46
  12.8 2.3 %collective-permute-done.2.refs_1_ = bf16[2,128,1024]{2,1,0:T(8,128)(2,1)S(1)} collective-permute-done((bf16[2,128,1024]{2,1,0:T(8,128)(2,1)}, bf16[2,128,1024]{2,1,0:T(8,128)(2,1)S(1)}, u32[]{:S(2)}, u32[]{:S(2)}) %collective-permute-start.2) | collective-permute-done | bytes 524320 | tf_op jit(solution)/shard_map/ppermute | solution.py:51
  15.1 1.5 %collective-permute-done.3.refs_3_ = bf16[1024,256]{1,0:T(8,128)(2,1)S(1)} collective-permute-done((bf16[1024,256]{1,0:T(8,128)(2,1)}, bf16[1024,256]{1,0:T(8,128)(2,1)S(1)}, u32[]{:S(2)}, u32[]{:S(2)}) %collective-permute-start.3) | collective-permute-done | bytes 524320 | tf_op jit(solution)/shard_map/ppermute | solution.py:51
  16.6 0.8 %shard_map.47.g0 = bf16[512,512]{1,0:T(8,128)(2,1)S(1)} custom-call(bf16[2,128,1024]{2,1,0:T(8,128)(2,1)S(1)} %get-tuple-element.20.refs_0_, bf16[2,128,1024]{2,1,0:T(8,128)(2,1)S(1)} %collective-permute-done.2.refs_1_, bf16[1024,256]{1,0:T(8,128)(2,1)S(1)} %get-tuple-element.21.refs_2_, bf16[1024,256]{1,0:T(8,128)(2,1)S(1)} %collective-permute-done.3.refs_3_), custom_call_target="tpu_custom_call" | custom-call | flops 536870912 | tf_op jit(solution)/shard_map/pallas_call | solution.py:238
  17.4 0.3 collective-permute-start.11
  17.7 1.7 %collective-permute-start.12 = (bf16[512,512]{1,0:T(8,128)(2,1)S(1)}, bf16[512,512]{1,0:T(8,128)(2,1)S(1)}, u32[]{:S(2)}, u32[]{:S(2)}) collective-permute-start(bf16[512,512]{1,0:T(8,128)(2,1)S(1)} %shard_map.47.g0), channel_id=1, source_target_pairs={{0,8},{8,0},{16,24},{24,16},{1,9},{9,1},{17,25},{25,17},{2,10},{10... | collective-permute-start | bytes 1572872 | tf_op jit(solution)/shard_map/ppermute | solution.py:51
  19.4 0.0 collective-permute-done.1.near_ref
  19.4 0.0 collective-permute-start.4
  19.4 0.0 collective-permute-done.5.far_ref
  19.4 0.2 shard_map.48.weights
  19.6 0.0 collective-permute-done.core_ref
  19.6 1.4 %collective-permute-done.4.near_core_ref = bf16[2,64,1024]{2,1,0:T(8,128)(2,1)S(1)} collective-permute-done((bf16[2,64,1024]{2,1,0:T(8,128)(2,1)S(1)}, bf16[2,64,1024]{2,1,0:T(8,128)(2,1)S(1)}, u32[]{:S(2)}, u32[]{:S(2)}) %collective-permute-start.4) | collective-permute-done | bytes 262176 | tf_op jit(solution)/shard_map/ppermute | solution.py:51
  21.0 0.5 %shard_map.49.t0 = bf16[256,512]{1,0:T(8,128)(2,1)S(1)} custom-call(bf16[2,64,1024]{2,1,0:T(8,128)(2,1)S(1)} %get-tuple-element.19.own_ref, bf16[2,64,1024]{2,1,0:T(8,128)(2,1)S(1)} %collective-permute-done.core_ref, bf16[2,64,1024]{2,1,0:T(8,128)(2,1)S(1)} %collective-permute-done.1.near_ref, bf16[2,64,1024]{2,1,0:T(8,128)(2,1)S(1)} %collective-permute-done.4.near_core_ref, ...), custom_call_target="tpu_custom_call" | custom-call | flops 2268435456 | tf_op jit(solution)/shard_map/pallas_call | solution.py:238
  21.5 2.7 %collective-permute-start.7 = (bf16[256,512]{1,0:T(8,128)(2,1)S(1)}, bf16[256,512]{1,0:T(8,128)(2,1)S(1)}, u32[]{:S(2)}, u32[]{:S(2)}) collective-permute-start(bf16[256,512]{1,0:T(8,128)(2,1)S(1)} %shard_map.49.t0), channel_id=1, source_target_pairs={{0,4},{1,5},{2,6},{3,7},{4,0},{5,1},{6,2},{7,3},{8,12},{9,13},{10,... | collective-permute-start | bytes 786440 | tf_op jit(solution)/shard_map/ppermute | solution.py:51
  24.1 1.6 %collective-permute-start.6 = (bf16[256,512]{1,0:T(8,128)(2,1)S(1)}, bf16[256,512]{1,0:T(8,128)(2,1)S(1)}, u32[]{:S(2)}, u32[]{:S(2)}) collective-permute-start(bf16[256,512]{1,0:T(8,128)(2,1)S(1)} %shard_map.49.t0), channel_id=1, source_target_pairs={{0,2},{1,3},{2,0},{3,1},{4,6},{5,7},{6,4},{7,5},{8,10},{9,11},{10,... | collective-permute-start | bytes 786440 | tf_op jit(solution)/shard_map/ppermute | solution.py:51
  25.7 0.0 collective-permute-start.8
  25.7 4.2 %collective-permute-done.11.refs_0_.g1 = bf16[512,512]{1,0:T(8,128)(2,1)S(1)} collective-permute-done((bf16[512,512]{1,0:T(8,128)(2,1)S(1)}, bf16[512,512]{1,0:T(8,128)(2,1)S(1)}, u32[]{:S(2)}, u32[]{:S(2)}) %collective-permute-start.11) | collective-permute-done | bytes 524320 | tf_op jit(solution)/shard_map/ppermute | solution.py:51
  29.9 0.3 collective-permute-done.12.refs_1_.g2
  30.3 1.6 %collective-permute-start.13 = (bf16[512,512]{1,0:T(8,128)(2,1)S(1)}, bf16[512,512]{1,0:T(8,128)(2,1)S(1)}, u32[]{:S(2)}, u32[]{:S(2)}) collective-permute-start(bf16[512,512]{1,0:T(8,128)(2,1)S(1)} %shard_map.51), channel_id=1, source_target_pairs={{0,8},{8,0},{16,24},{24,16},{1,17},{9,25},{17,1},{25,9},{2,10},{10... | collective-permute-start | bytes 1572872 | tf_op jit(solution)/shard_map/ppermute | solution.py:300
  31.8 4.7 %collective-permute-done.7.a_ref = bf16[256,512]{1,0:T(8,128)(2,1)S(1)} collective-permute-done((bf16[256,512]{1,0:T(8,128)(2,1)S(1)}, bf16[256,512]{1,0:T(8,128)(2,1)S(1)}, u32[]{:S(2)}, u32[]{:S(2)}) %collective-permute-start.7) | collective-permute-done | bytes 262176 | tf_op jit(solution)/shard_map/ppermute | solution.py:51
  36.6 0.2 collective-permute-done.6.t2
  36.7 0.0 collective-permute-start.10
  36.7 0.5 %collective-permute-start.9 = (bf16[256,512]{1,0:T(8,128)(2,1)S(1)}, bf16[256,512]{1,0:T(8,128)(2,1)S(1)}, u32[]{:S(2)}, u32[]{:S(2)}) collective-permute-start(bf16[256,512]{1,0:T(8,128)(2,1)S(1)} %shard_map.50.t1), channel_id=1, source_target_pairs={{0,1},{1,0},{2,3},{3,2},{4,5},{5,4},{6,7},{7,6},{8,9},{9,8},{10,11... | collective-permute-start | bytes 786440 | tf_op jit(solution)/shard_map/ppermute | solution.py:51
  37.2 1.4 %collective-permute-start.14 = (bf16[256,512]{1,0:T(8,128)(2,1)S(1)}, bf16[256,512]{1,0:T(8,128)(2,1)S(1)}, u32[]{:S(2)}, u32[]{:S(2)}) collective-permute-start(bf16[256,512]{1,0:T(8,128)(2,1)S(1)} %shard_map.50.t1), channel_id=1, source_target_pairs={{0,2},{1,3},{2,0},{3,1},{4,6},{5,7},{6,4},{7,5},{8,10},{9,11},{10,... | collective-permute-start | bytes 786440 | tf_op jit(solution)/shard_map/ppermute | solution.py:51
  38.7 0.0 collective-permute-done.8.s0
  38.7 0.0 collective-permute-done.10.s2
  38.7 0.0 collective-permute-done.9.s1
  38.7 0.8 %collective-permute-done.13.g3 = bf16[512,512]{1,0:T(8,128)(2,1)S(1)} collective-permute-done((bf16[512,512]{1,0:T(8,128)(2,1)S(1)}, bf16[512,512]{1,0:T(8,128)(2,1)S(1)}, u32[]{:S(2)}, u32[]{:S(2)}) %collective-permute-start.13) | collective-permute-done | bytes 524320 | tf_op jit(solution)/shard_map/ppermute | solution.py:300
  39.5 4.6 %shard_map.52 = (bf16[1024,1024]{1,0:T(8,128)(2,1)}, f32[256,1024]{1,0:T(8,128)S(1)}, f32[256,1024]{1,0:T(8,128)S(1)}, bf16[512,1024]{1,0:T(8,128)(2,1)}, bf16[1024,1024]{1,0:T(8,128)(2,1)S(1)}) custom-call(bf16[256,512]{1,0:T(8,128)(2,1)S(1)} %shard_map.49.t0, bf16[256,512]{1,0:T(8,128)(2,1)S(1)} %collective-permute-done.6.t2, ...), custom_call_target="tpu_custom_call" | custom-call | tf_op jit(solution)/shard_map/pallas_call | solution.py:238
  44.1 1.3 %collective-permute-done.14.a_ref = bf16[256,512]{1,0:T(8,128)(2,1)S(1)} collective-permute-done((bf16[256,512]{1,0:T(8,128)(2,1)S(1)}, bf16[256,512]{1,0:T(8,128)(2,1)S(1)}, u32[]{:S(2)}, u32[]{:S(2)}) %collective-permute-start.14) | collective-permute-done | bytes 262176 | tf_op jit(solution)/shard_map/ppermute | solution.py:51
  45.5 0.1 collective-permute-start.15
  45.5 1.3 %shard_map.54.first = bf16[256,1024]{1,0:T(8,128)(2,1)S(1)} custom-call(bf16[1024,1024]{1,0:T(8,128)(2,1)S(1)} %get-tuple-element.28.right, bf16[256,512]{1,0:T(8,128)(2,1)S(1)} %shard_map.50.t1, bf16[256,512]{1,0:T(8,128)(2,1)S(1)} %shard_map.53.t3), custom_call_target="tpu_custom_call" | custom-call | flops 500000000 | tf_op jit(solution)/shard_map/pallas_call | solution.py:238
  46.8 0.2 collective-permute-done.15.s
  47.1 1.6 %shard_map.55 = bf16[1024,1024]{1,0:T(8,128)(2,1)} custom-call(bf16[1024,1024]{1,0:T(8,128)(2,1)} %get-tuple-element.27.out_in, bf16[256,1024]{1,0:T(8,128)(2,1)S(1)} %shard_map.54.first, f32[256,1024]{1,0:T(8,128)S(1)} %get-tuple-element.31.grad, f32[256,1024]{1,0:T(8,128)S(1)} %get-tuple-element.32.fisher, ...), custom_call_target="tpu_custom_call", output_to_operand_aliasing={{}: (0, {})} | custom-call | tf_op jit(solution)/shard_map/pallas_call | solution.py:329
  (3 shorter events, 0.1 us)
Async XLA Ops:
  0.0 15.1 %collective-permute-start.2 = (bf16[2,128,1024]{2,1,0:T(8,128)(2,1)}, bf16[2,128,1024]{2,1,0:T(8,128)(2,1)S(1)}, u32[]{:S(2)}, u32[]{:S(2)}) collective-permute-start(bf16[2,128,1024]{2,1,0:T(8,128)(2,1)} %refs_0_.1), channel_id=1, source_target_pairs={{0,16},{8,24},{16,0},{24,8},{1,17},{9,25},{17,1},{25,9},{2,18},{10... | collective-permute-start | bytes 1572872 | tf_op jit(solution)/shard_map/ppermute | solution.py:51
  3.0 13.6 %collective-permute-start.3 = (bf16[1024,256]{1,0:T(8,128)(2,1)}, bf16[1024,256]{1,0:T(8,128)(2,1)S(1)}, u32[]{:S(2)}, u32[]{:S(2)}) collective-permute-start(bf16[1024,256]{1,0:T(8,128)(2,1)} %refs_1_.1), channel_id=1, source_target_pairs={{0,8},{8,0},{16,24},{24,16},{1,9},{9,1},{17,25},{25,17},{2,10},{10... | collective-permute-start | bytes 1572872 | tf_op jit(solution)/shard_map/ppermute | solution.py:51
  4.5 15.0 %collective-permute-start.1 = (bf16[2,64,1024]{2,1,0:T(8,128)(2,1)}, bf16[2,64,1024]{2,1,0:T(8,128)(2,1)S(1)}, u32[]{:S(2)}, u32[]{:S(2)}) collective-permute-start(bf16[2,64,1024]{2,1,0:T(8,128)(2,1)} %refs_2_.1), channel_id=1, source_target_pairs={{0,4},{1,5},{2,6},{3,7},{4,0},{5,1},{6,2},{7,3},{8,12},{9,13},{10,... | collective-permute-start | bytes 786440 | tf_op jit(solution)/shard_map/ppermute | solution.py:51
  7.0 12.4 %collective-permute-start.5 = (bf16[1024,128]{1,0:T(8,128)(2,1)}, bf16[1024,128]{1,0:T(8,128)(2,1)S(1)}, u32[]{:S(2)}, u32[]{:S(2)}) collective-permute-start(bf16[1024,128]{1,0:T(8,128)(2,1)} %refs_3_.1), channel_id=1, source_target_pairs={{0,2},{1,3},{2,0},{3,1},{4,6},{5,7},{6,4},{7,5},{8,10},{9,11},{10,... | collective-permute-start | bytes 786440 | tf_op jit(solution)/shard_map/ppermute | solution.py:51
  8.6 11.0 %collective-permute-start = (bf16[2,64,1024]{2,1,0:T(8,128)(2,1)}, bf16[2,64,1024]{2,1,0:T(8,128)(2,1)S(1)}, u32[]{:S(2)}, u32[]{:S(2)}) collective-permute-start(bf16[2,64,1024]{2,1,0:T(8,128)(2,1)} %refs_2_.1), channel_id=1, source_target_pairs={{0,1},{1,0},{2,3},{3,2},{4,5},{5,4},{6,7},{7,6},{8,9},{9,8},{10,11... | collective-permute-start | bytes 786440 | tf_op jit(solution)/shard_map/ppermute | solution.py:51
  8.6 1.0 %copy-start = (bf16[2,128,1024]{2,1,0:T(8,128)(2,1)S(1)}, bf16[2,128,1024]{2,1,0:T(8,128)(2,1)}, u32[]{:S(2)}) copy-start(bf16[2,128,1024]{2,1,0:T(8,128)(2,1)} %refs_0_.1) | copy-start | bytes 1572868
  9.7 1.0 %copy-start.1 = (bf16[1024,256]{1,0:T(8,128)(2,1)S(1)}, bf16[1024,256]{1,0:T(8,128)(2,1)}, u32[]{:S(2)}) copy-start(bf16[1024,256]{1,0:T(8,128)(2,1)} %refs_1_.1) | copy-start | bytes 1572868
  10.7 0.9 %copy-start.2 = (bf16[1024,128]{1,0:T(8,128)(2,1)S(1)}, bf16[1024,128]{1,0:T(8,128)(2,1)}, u32[]{:S(2)}) copy-start(bf16[1024,128]{1,0:T(8,128)(2,1)} %refs_3_.1) | copy-start | bytes 786436
  11.7 0.9 %copy-start.3 = (bf16[2,64,1024]{2,1,0:T(8,128)(2,1)S(1)}, bf16[2,64,1024]{2,1,0:T(8,128)(2,1)}, u32[]{:S(2)}) copy-start(bf16[2,64,1024]{2,1,0:T(8,128)(2,1)} %refs_2_.1) | copy-start | bytes 786436
  17.4 12.5 %collective-permute-start.11 = (bf16[512,512]{1,0:T(8,128)(2,1)S(1)}, bf16[512,512]{1,0:T(8,128)(2,1)S(1)}, u32[]{:S(2)}, u32[]{:S(2)}) collective-permute-start(bf16[512,512]{1,0:T(8,128)(2,1)S(1)} %shard_map.47.g0), channel_id=1, source_target_pairs={{0,16},{8,24},{16,0},{24,8},{1,17},{9,25},{17,1},{25,9},{2,18},{10... | collective-permute-start | bytes 1572872 | tf_op jit(solution)/shard_map/ppermute | solution.py:51
  17.7 12.5 %collective-permute-start.12 = (bf16[512,512]{1,0:T(8,128)(2,1)S(1)}, bf16[512,512]{1,0:T(8,128)(2,1)S(1)}, u32[]{:S(2)}, u32[]{:S(2)}) collective-permute-start(bf16[512,512]{1,0:T(8,128)(2,1)S(1)} %shard_map.47.g0), channel_id=1, source_target_pairs={{0,8},{8,0},{16,24},{24,16},{1,9},{9,1},{17,25},{25,17},{2,10},{10... | collective-permute-start | bytes 1572872 | tf_op jit(solution)/shard_map/ppermute | solution.py:51
  19.4 1.5 %collective-permute-start.4 = (bf16[2,64,1024]{2,1,0:T(8,128)(2,1)S(1)}, bf16[2,64,1024]{2,1,0:T(8,128)(2,1)S(1)}, u32[]{:S(2)}, u32[]{:S(2)}) collective-permute-start(bf16[2,64,1024]{2,1,0:T(8,128)(2,1)S(1)} %collective-permute-done.1.near_ref), channel_id=1, source_target_pairs={{0,1},{1,0},{2,3},{3,2},{4,5},{5,4},{6,7},{7,6},{8,9},{9,8},{10,11... | collective-permute-start | bytes 786440 | tf_op jit(solution)/shard_map/ppermute | solution.py:51
  21.5 15.0 %collective-permute-start.7 = (bf16[256,512]{1,0:T(8,128)(2,1)S(1)}, bf16[256,512]{1,0:T(8,128)(2,1)S(1)}, u32[]{:S(2)}, u32[]{:S(2)}) collective-permute-start(bf16[256,512]{1,0:T(8,128)(2,1)S(1)} %shard_map.49.t0), channel_id=1, source_target_pairs={{0,4},{1,5},{2,6},{3,7},{4,0},{5,1},{6,2},{7,3},{8,12},{9,13},{10,... | collective-permute-start | bytes 786440 | tf_op jit(solution)/shard_map/ppermute | solution.py:51
  24.1 12.6 %collective-permute-start.6 = (bf16[256,512]{1,0:T(8,128)(2,1)S(1)}, bf16[256,512]{1,0:T(8,128)(2,1)S(1)}, u32[]{:S(2)}, u32[]{:S(2)}) collective-permute-start(bf16[256,512]{1,0:T(8,128)(2,1)S(1)} %shard_map.49.t0), channel_id=1, source_target_pairs={{0,2},{1,3},{2,0},{3,1},{4,6},{5,7},{6,4},{7,5},{8,10},{9,11},{10,... | collective-permute-start | bytes 786440 | tf_op jit(solution)/shard_map/ppermute | solution.py:51
  25.7 13.0 %collective-permute-start.8 = (bf16[256,512]{1,0:T(8,128)(2,1)S(1)}, bf16[256,512]{1,0:T(8,128)(2,1)S(1)}, u32[]{:S(2)}, u32[]{:S(2)}) collective-permute-start(bf16[256,512]{1,0:T(8,128)(2,1)S(1)} %shard_map.49.t0), channel_id=1, source_target_pairs={{0,1},{1,0},{2,3},{3,2},{4,5},{5,4},{6,7},{7,6},{8,9},{9,8},{10,11... | collective-permute-start | bytes 786440 | tf_op jit(solution)/shard_map/ppermute | solution.py:51
  30.3 9.2 %collective-permute-start.13 = (bf16[512,512]{1,0:T(8,128)(2,1)S(1)}, bf16[512,512]{1,0:T(8,128)(2,1)S(1)}, u32[]{:S(2)}, u32[]{:S(2)}) collective-permute-start(bf16[512,512]{1,0:T(8,128)(2,1)S(1)} %shard_map.51), channel_id=1, source_target_pairs={{0,8},{8,0},{16,24},{24,16},{1,17},{9,25},{17,1},{25,9},{2,10},{10... | collective-permute-start | bytes 1572872 | tf_op jit(solution)/shard_map/ppermute | solution.py:300
  36.7 2.0 %collective-permute-start.10 = (bf16[256,512]{1,0:T(8,128)(2,1)S(1)}, bf16[256,512]{1,0:T(8,128)(2,1)S(1)}, u32[]{:S(2)}, u32[]{:S(2)}) collective-permute-start(bf16[256,512]{1,0:T(8,128)(2,1)S(1)} %collective-permute-done.6.t2), channel_id=1, source_target_pairs={{0,1},{1,0},{2,3},{3,2},{4,5},{5,4},{6,7},{7,6},{8,9},{9,8},{10,11... | collective-permute-start | bytes 786440 | tf_op jit(solution)/shard_map/ppermute | solution.py:51
  36.7 2.0 %collective-permute-start.9 = (bf16[256,512]{1,0:T(8,128)(2,1)S(1)}, bf16[256,512]{1,0:T(8,128)(2,1)S(1)}, u32[]{:S(2)}, u32[]{:S(2)}) collective-permute-start(bf16[256,512]{1,0:T(8,128)(2,1)S(1)} %shard_map.50.t1), channel_id=1, source_target_pairs={{0,1},{1,0},{2,3},{3,2},{4,5},{5,4},{6,7},{7,6},{8,9},{9,8},{10,11... | collective-permute-start | bytes 786440 | tf_op jit(solution)/shard_map/ppermute | solution.py:51
  37.2 8.2 %collective-permute-start.14 = (bf16[256,512]{1,0:T(8,128)(2,1)S(1)}, bf16[256,512]{1,0:T(8,128)(2,1)S(1)}, u32[]{:S(2)}, u32[]{:S(2)}) collective-permute-start(bf16[256,512]{1,0:T(8,128)(2,1)S(1)} %shard_map.50.t1), channel_id=1, source_target_pairs={{0,2},{1,3},{2,0},{3,1},{4,6},{5,7},{6,4},{7,5},{8,10},{9,11},{10,... | collective-permute-start | bytes 786440 | tf_op jit(solution)/shard_map/ppermute | solution.py:51
  45.5 1.6 %collective-permute-start.15 = (bf16[256,512]{1,0:T(8,128)(2,1)S(1)}, bf16[256,512]{1,0:T(8,128)(2,1)S(1)}, u32[]{:S(2)}, u32[]{:S(2)}) collective-permute-start(bf16[256,512]{1,0:T(8,128)(2,1)S(1)} %shard_map.53.t3), channel_id=1, source_target_pairs={{0,1},{1,0},{2,3},{3,2},{4,5},{5,4},{6,7},{7,6},{8,9},{9,8},{10,11... | collective-permute-start | bytes 786440 | tf_op jit(solution)/shard_map/ppermute | solution.py:51

commit v6 on v5

--- a/solution.py
+++ b/solution.py
@@ -203,11 +203,12 @@
 
 def late_kernel(out_in, first, grad, fisher, right, s, out_ref, done, sems):
     tok, _, core = hid_digits()
-    span, width = s.shape[1], right.shape[1] // 2
+    pieces = 4
+    span, width = s.shape[1], right.shape[1] // pieces
     copies = send_rows(first, out_ref, 1 - tok, core, 0, slice(0, done.shape[1]), sems)
     rows = s[...]
     rows_squared = squared(rows)
-    for c in range(2):
+    for c in range(pieces):
         columns = slice(c * width, (c + 1) * width)
         beside = right[span:, columns]
         g = grad[:, columns] + dot(rows, beside)
@@ -331,7 +332,7 @@
         out_shape=shape(out.shape, bf16),
         in_specs=[anywhere] + [vmem] * 5,
         out_specs=anywhere,
-        scratch_shapes=[pltpu.VMEM(part_rows, bf16), pltpu.SemaphoreType.DMA((6,))],
+        scratch_shapes=[pltpu.VMEM(part_rows, bf16), pltpu.SemaphoreType.DMA((10,))],
         input_output_aliases={0: 0},
         compiler_params=params,
     )(out, first, grad, fisher, right, s3)

time: 48.9 us -> 48.8 us (level)
  transfers between devices with their start and end apart: 16 -> 16, of which waited for: 10 -> 10; matrix products, arithmetic and copies ran while one was open for 0% -> 0% of each run, Pallas kernels for 15% -> 16%
where the time goes in v6:
time: 48.8 us; the launch traced here: 48.5 us
  starting transfers between devices  18.5 us (38%)
  waiting for transfers between devices  16.9 us (35%)
  Pallas kernels  9.02 us (18%)
  local copies, waits for them, and re-layouts  3.98 us (8%)
    ppermute x15, starting transfers between devices, swap(): return lax.ppermute(values, axis, [(i, i ^ distance) for i in range(count)])  16.9 us
    ppermute x15, waiting for transfers between devices, swap(): return lax.ppermute(values, axis, [(i, i ^ distance) for i in range(count)])  16.1 us
    pallas_call x9, Pallas kernels, call(): pl.pallas_call(kernel, out_shape=outs, in_specs=[space] * len(operands),...  7.54 us
    unnamed x8, local copies, waits for them, and re-layouts  3.98 us
    ppermute x1, starting transfers between devices, paired(): g3 = lax.ppermute(picked, ('inb', 'hid'), onward)  1.56 us
    pallas_call x1, Pallas kernels, paired(): pl.pallas_call(late_kernel, out_shape=shape(out.shape, bf16), in_specs=[a...  1.48 us
  transfers between devices with their start and end apart: 16, of which 10 were waited for; matrix products, arithmetic and copies ran while one was open for 0% of the time, Pallas kernels for 16%

profile of v6, /device:TPU:0, one launch (start us, length us, event | category | flops | bytes accessed | tf_op | source)
XLA Modules:
  0.0 48.5 jit_solution(15819856766899251781)
XLA Ops:
  0.0 3.0 %collective-permute-start.2 = (bf16[2,128,1024]{2,1,0:T(8,128)(2,1)}, bf16[2,128,1024]{2,1,0:T(8,128)(2,1)S(1)}, u32[]{:S(2)}, u32[]{:S(2)}) collective-permute-start(bf16[2,128,1024]{2,1,0:T(8,128)(2,1)} %refs_0_.1), channel_id=1, source_target_pairs={{0,16},{8,24},{16,0},{24,8},{1,17},{9,25},{17,1},{25,9},{2,18},{10... | collective-permute-start | bytes 1572872 | tf_op jit(solution)/shard_map/ppermute | solution.py:51
  3.0 1.5 %collective-permute-start.3 = (bf16[1024,256]{1,0:T(8,128)(2,1)}, bf16[1024,256]{1,0:T(8,128)(2,1)S(1)}, u32[]{:S(2)}, u32[]{:S(2)}) collective-permute-start(bf16[1024,256]{1,0:T(8,128)(2,1)} %refs_1_.1), channel_id=1, source_target_pairs={{0,8},{8,0},{16,24},{24,16},{1,9},{9,1},{17,25},{25,17},{2,10},{10... | collective-permute-start | bytes 1572872 | tf_op jit(solution)/shard_map/ppermute | solution.py:51
  4.5 2.6 %collective-permute-start.1 = (bf16[2,64,1024]{2,1,0:T(8,128)(2,1)}, bf16[2,64,1024]{2,1,0:T(8,128)(2,1)S(1)}, u32[]{:S(2)}, u32[]{:S(2)}) collective-permute-start(bf16[2,64,1024]{2,1,0:T(8,128)(2,1)} %refs_2_.1), channel_id=1, source_target_pairs={{0,4},{1,5},{2,6},{3,7},{4,0},{5,1},{6,2},{7,3},{8,12},{9,13},{10,... | collective-permute-start | bytes 786440 | tf_op jit(solution)/shard_map/ppermute | solution.py:51
  7.0 1.6 %collective-permute-start.5 = (bf16[1024,128]{1,0:T(8,128)(2,1)}, bf16[1024,128]{1,0:T(8,128)(2,1)S(1)}, u32[]{:S(2)}, u32[]{:S(2)}) collective-permute-start(bf16[1024,128]{1,0:T(8,128)(2,1)} %refs_3_.1), channel_id=1, source_target_pairs={{0,2},{1,3},{2,0},{3,1},{4,6},{5,7},{6,4},{7,5},{8,10},{9,11},{10,... | collective-permute-start | bytes 786440 | tf_op jit(solution)/shard_map/ppermute | solution.py:51
  8.6 0.0 collective-permute-start
  8.6 0.0 copy-start
  8.6 1.0 %copy-done = bf16[2,128,1024]{2,1,0:T(8,128)(2,1)S(1)} copy-done((bf16[2,128,1024]{2,1,0:T(8,128)(2,1)S(1)}, bf16[2,128,1024]{2,1,0:T(8,128)(2,1)}, u32[]{:S(2)}) %copy-start) | copy-done | bytes 524312
  9.7 0.0 copy-start.1
  9.7 1.0 %copy-done.1 = bf16[1024,256]{1,0:T(8,128)(2,1)S(1)} copy-done((bf16[1024,256]{1,0:T(8,128)(2,1)S(1)}, bf16[1024,256]{1,0:T(8,128)(2,1)}, u32[]{:S(2)}) %copy-start.1) | copy-done | bytes 524312
  10.7 0.0 copy-start.2
  10.7 0.9 %copy-done.2 = bf16[1024,128]{1,0:T(8,128)(2,1)S(1)} copy-done((bf16[1024,128]{1,0:T(8,128)(2,1)S(1)}, bf16[1024,128]{1,0:T(8,128)(2,1)}, u32[]{:S(2)}) %copy-start.2) | copy-done | bytes 262168
  11.7 0.0 copy-start.3
  11.7 0.9 %copy-done.3 = bf16[2,64,1024]{2,1,0:T(8,128)(2,1)S(1)} copy-done((bf16[2,64,1024]{2,1,0:T(8,128)(2,1)S(1)}, bf16[2,64,1024]{2,1,0:T(8,128)(2,1)}, u32[]{:S(2)}) %copy-start.3) | copy-done | bytes 262168
  12.6 0.1 shard_map.46
  12.8 2.3 %collective-permute-done.2.refs_1_ = bf16[2,128,1024]{2,1,0:T(8,128)(2,1)S(1)} collective-permute-done((bf16[2,128,1024]{2,1,0:T(8,128)(2,1)}, bf16[2,128,1024]{2,1,0:T(8,128)(2,1)S(1)}, u32[]{:S(2)}, u32[]{:S(2)}) %collective-permute-start.2) | collective-permute-done | bytes 524320 | tf_op jit(solution)/shard_map/ppermute | solution.py:51
  15.1 1.5 %collective-permute-done.3.refs_3_ = bf16[1024,256]{1,0:T(8,128)(2,1)S(1)} collective-permute-done((bf16[1024,256]{1,0:T(8,128)(2,1)}, bf16[1024,256]{1,0:T(8,128)(2,1)S(1)}, u32[]{:S(2)}, u32[]{:S(2)}) %collective-permute-start.3) | collective-permute-done | bytes 524320 | tf_op jit(solution)/shard_map/ppermute | solution.py:51
  16.6 0.8 %shard_map.47.g0 = bf16[512,512]{1,0:T(8,128)(2,1)S(1)} custom-call(bf16[2,128,1024]{2,1,0:T(8,128)(2,1)S(1)} %get-tuple-element.20.refs_0_, bf16[2,128,1024]{2,1,0:T(8,128)(2,1)S(1)} %collective-permute-done.2.refs_1_, bf16[1024,256]{1,0:T(8,128)(2,1)S(1)} %get-tuple-element.21.refs_2_, bf16[1024,256]{1,0:T(8,128)(2,1)S(1)} %collective-permute-done.3.refs_3_), custom_call_target="tpu_custom_call" | custom-call | flops 536870912 | tf_op jit(solution)/shard_map/pallas_call | solution.py:239
  17.4 0.3 collective-permute-start.11
  17.7 1.7 %collective-permute-start.12 = (bf16[512,512]{1,0:T(8,128)(2,1)S(1)}, bf16[512,512]{1,0:T(8,128)(2,1)S(1)}, u32[]{:S(2)}, u32[]{:S(2)}) collective-permute-start(bf16[512,512]{1,0:T(8,128)(2,1)S(1)} %shard_map.47.g0), channel_id=1, source_target_pairs={{0,8},{8,0},{16,24},{24,16},{1,9},{9,1},{17,25},{25,17},{2,10},{10... | collective-permute-start | bytes 1572872 | tf_op jit(solution)/shard_map/ppermute | solution.py:51
  19.4 0.0 collective-permute-done.1.near_ref
  19.4 0.0 collective-permute-start.4
  19.4 0.0 collective-permute-done.5.far_ref
  19.4 0.2 shard_map.48.weights
  19.6 0.0 collective-permute-done.core_ref
  19.6 1.4 %collective-permute-done.4.near_core_ref = bf16[2,64,1024]{2,1,0:T(8,128)(2,1)S(1)} collective-permute-done((bf16[2,64,1024]{2,1,0:T(8,128)(2,1)S(1)}, bf16[2,64,1024]{2,1,0:T(8,128)(2,1)S(1)}, u32[]{:S(2)}, u32[]{:S(2)}) %collective-permute-start.4) | collective-permute-done | bytes 262176 | tf_op jit(solution)/shard_map/ppermute | solution.py:51
  21.0 0.5 %shard_map.49.t0 = bf16[256,512]{1,0:T(8,128)(2,1)S(1)} custom-call(bf16[2,64,1024]{2,1,0:T(8,128)(2,1)S(1)} %get-tuple-element.19.own_ref, bf16[2,64,1024]{2,1,0:T(8,128)(2,1)S(1)} %collective-permute-done.core_ref, bf16[2,64,1024]{2,1,0:T(8,128)(2,1)S(1)} %collective-permute-done.1.near_ref, bf16[2,64,1024]{2,1,0:T(8,128)(2,1)S(1)} %collective-permute-done.4.near_core_ref, ...), custom_call_target="tpu_custom_call" | custom-call | flops 2268435456 | tf_op jit(solution)/shard_map/pallas_call | solution.py:239
  21.5 2.7 %collective-permute-start.7 = (bf16[256,512]{1,0:T(8,128)(2,1)S(1)}, bf16[256,512]{1,0:T(8,128)(2,1)S(1)}, u32[]{:S(2)}, u32[]{:S(2)}) collective-permute-start(bf16[256,512]{1,0:T(8,128)(2,1)S(1)} %shard_map.49.t0), channel_id=1, source_target_pairs={{0,4},{1,5},{2,6},{3,7},{4,0},{5,1},{6,2},{7,3},{8,12},{9,13},{10,... | collective-permute-start | bytes 786440 | tf_op jit(solution)/shard_map/ppermute | solution.py:51
  24.1 1.6 %collective-permute-start.6 = (bf16[256,512]{1,0:T(8,128)(2,1)S(1)}, bf16[256,512]{1,0:T(8,128)(2,1)S(1)}, u32[]{:S(2)}, u32[]{:S(2)}) collective-permute-start(bf16[256,512]{1,0:T(8,128)(2,1)S(1)} %shard_map.49.t0), channel_id=1, source_target_pairs={{0,2},{1,3},{2,0},{3,1},{4,6},{5,7},{6,4},{7,5},{8,10},{9,11},{10,... | collective-permute-start | bytes 786440 | tf_op jit(solution)/shard_map/ppermute | solution.py:51
  25.7 0.0 collective-permute-start.8
  25.7 4.2 %collective-permute-done.11.refs_0_.g1 = bf16[512,512]{1,0:T(8,128)(2,1)S(1)} collective-permute-done((bf16[512,512]{1,0:T(8,128)(2,1)S(1)}, bf16[512,512]{1,0:T(8,128)(2,1)S(1)}, u32[]{:S(2)}, u32[]{:S(2)}) %collective-permute-start.11) | collective-permute-done | bytes 524320 | tf_op jit(solution)/shard_map/ppermute | solution.py:51
  29.9 0.3 collective-permute-done.12.refs_1_.g2
  30.3 1.6 %collective-permute-start.13 = (bf16[512,512]{1,0:T(8,128)(2,1)S(1)}, bf16[512,512]{1,0:T(8,128)(2,1)S(1)}, u32[]{:S(2)}, u32[]{:S(2)}) collective-permute-start(bf16[512,512]{1,0:T(8,128)(2,1)S(1)} %shard_map.51), channel_id=1, source_target_pairs={{0,8},{8,0},{16,24},{24,16},{1,17},{9,25},{17,1},{25,9},{2,10},{10... | collective-permute-start | bytes 1572872 | tf_op jit(solution)/shard_map/ppermute | solution.py:301
  31.8 4.7 %collective-permute-done.7.a_ref = bf16[256,512]{1,0:T(8,128)(2,1)S(1)} collective-permute-done((bf16[256,512]{1,0:T(8,128)(2,1)S(1)}, bf16[256,512]{1,0:T(8,128)(2,1)S(1)}, u32[]{:S(2)}, u32[]{:S(2)}) %collective-permute-start.7) | collective-permute-done | bytes 262176 | tf_op jit(solution)/shard_map/ppermute | solution.py:51
  36.6 0.2 collective-permute-done.6.t2
  36.7 0.0 collective-permute-start.10
  36.7 0.5 %collective-permute-start.9 = (bf16[256,512]{1,0:T(8,128)(2,1)S(1)}, bf16[256,512]{1,0:T(8,128)(2,1)S(1)}, u32[]{:S(2)}, u32[]{:S(2)}) collective-permute-start(bf16[256,512]{1,0:T(8,128)(2,1)S(1)} %shard_map.50.t1), channel_id=1, source_target_pairs={{0,1},{1,0},{2,3},{3,2},{4,5},{5,4},{6,7},{7,6},{8,9},{9,8},{10,11... | collective-permute-start | bytes 786440 | tf_op jit(solution)/shard_map/ppermute | solution.py:51
  37.2 1.4 %collective-permute-start.14 = (bf16[256,512]{1,0:T(8,128)(2,1)S(1)}, bf16[256,512]{1,0:T(8,128)(2,1)S(1)}, u32[]{:S(2)}, u32[]{:S(2)}) collective-permute-start(bf16[256,512]{1,0:T(8,128)(2,1)S(1)} %shard_map.50.t1), channel_id=1, source_target_pairs={{0,2},{1,3},{2,0},{3,1},{4,6},{5,7},{6,4},{7,5},{8,10},{9,11},{10,... | collective-permute-start | bytes 786440 | tf_op jit(solution)/shard_map/ppermute | solution.py:51
  38.7 0.0 collective-permute-done.8.s0
  38.7 0.0 collective-permute-done.10.s2
  38.7 0.0 collective-permute-done.9.s1
  38.7 0.8 %collective-permute-done.13.g3 = bf16[512,512]{1,0:T(8,128)(2,1)S(1)} collective-permute-done((bf16[512,512]{1,0:T(8,128)(2,1)S(1)}, bf16[512,512]{1,0:T(8,128)(2,1)S(1)}, u32[]{:S(2)}, u32[]{:S(2)}) %collective-permute-start.13) | collective-permute-done | bytes 524320 | tf_op jit(solution)/shard_map/ppermute | solution.py:301
  39.5 4.6 %shard_map.52 = (bf16[1024,1024]{1,0:T(8,128)(2,1)}, f32[256,1024]{1,0:T(8,128)S(1)}, f32[256,1024]{1,0:T(8,128)S(1)}, bf16[512,1024]{1,0:T(8,128)(2,1)}, bf16[1024,1024]{1,0:T(8,128)(2,1)S(1)}) custom-call(bf16[256,512]{1,0:T(8,128)(2,1)S(1)} %shard_map.49.t0, bf16[256,512]{1,0:T(8,128)(2,1)S(1)} %collective-permute-done.6.t2, ...), custom_call_target="tpu_custom_call" | custom-call | tf_op jit(solution)/shard_map/pallas_call | solution.py:239
  44.1 1.3 %collective-permute-done.14.a_ref = bf16[256,512]{1,0:T(8,128)(2,1)S(1)} collective-permute-done((bf16[256,512]{1,0:T(8,128)(2,1)S(1)}, bf16[256,512]{1,0:T(8,128)(2,1)S(1)}, u32[]{:S(2)}, u32[]{:S(2)}) %collective-permute-start.14) | collective-permute-done | bytes 262176 | tf_op jit(solution)/shard_map/ppermute | solution.py:51
  45.5 0.1 collective-permute-start.15
  45.5 1.3 %shard_map.54.first = bf16[256,1024]{1,0:T(8,128)(2,1)S(1)} custom-call(bf16[1024,1024]{1,0:T(8,128)(2,1)S(1)} %get-tuple-element.28.right, bf16[256,512]{1,0:T(8,128)(2,1)S(1)} %shard_map.50.t1, bf16[256,512]{1,0:T(8,128)(2,1)S(1)} %shard_map.53.t3), custom_call_target="tpu_custom_call" | custom-call | flops 500000000 | tf_op jit(solution)/shard_map/pallas_call | solution.py:239
  46.8 0.2 collective-permute-done.15.s
  47.1 1.5 %shard_map.55 = bf16[1024,1024]{1,0:T(8,128)(2,1)} custom-call(bf16[1024,1024]{1,0:T(8,128)(2,1)} %get-tuple-element.27.out_in, bf16[256,1024]{1,0:T(8,128)(2,1)S(1)} %shard_map.54.first, f32[256,1024]{1,0:T(8,128)S(1)} %get-tuple-element.31.grad, f32[256,1024]{1,0:T(8,128)S(1)} %get-tuple-element.32.fisher, ...), custom_call_target="tpu_custom_call", output_to_operand_aliasing={{}: (0, {})} | custom-call | tf_op jit(solution)/shard_map/pallas_call | solution.py:330
  (3 shorter events, 0.1 us)
Async XLA Ops:
  0.0 15.1 %collective-permute-start.2 = (bf16[2,128,1024]{2,1,0:T(8,128)(2,1)}, bf16[2,128,1024]{2,1,0:T(8,128)(2,1)S(1)}, u32[]{:S(2)}, u32[]{:S(2)}) collective-permute-start(bf16[2,128,1024]{2,1,0:T(8,128)(2,1)} %refs_0_.1), channel_id=1, source_target_pairs={{0,16},{8,24},{16,0},{24,8},{1,17},{9,25},{17,1},{25,9},{2,18},{10... | collective-permute-start | bytes 1572872 | tf_op jit(solution)/shard_map/ppermute | solution.py:51
  3.0 13.6 %collective-permute-start.3 = (bf16[1024,256]{1,0:T(8,128)(2,1)}, bf16[1024,256]{1,0:T(8,128)(2,1)S(1)}, u32[]{:S(2)}, u32[]{:S(2)}) collective-permute-start(bf16[1024,256]{1,0:T(8,128)(2,1)} %refs_1_.1), channel_id=1, source_target_pairs={{0,8},{8,0},{16,24},{24,16},{1,9},{9,1},{17,25},{25,17},{2,10},{10... | collective-permute-start | bytes 1572872 | tf_op jit(solution)/shard_map/ppermute | solution.py:51
  4.5 15.0 %collective-permute-start.1 = (bf16[2,64,1024]{2,1,0:T(8,128)(2,1)}, bf16[2,64,1024]{2,1,0:T(8,128)(2,1)S(1)}, u32[]{:S(2)}, u32[]{:S(2)}) collective-permute-start(bf16[2,64,1024]{2,1,0:T(8,128)(2,1)} %refs_2_.1), channel_id=1, source_target_pairs={{0,4},{1,5},{2,6},{3,7},{4,0},{5,1},{6,2},{7,3},{8,12},{9,13},{10,... | collective-permute-start | bytes 786440 | tf_op jit(solution)/shard_map/ppermute | solution.py:51
  7.0 12.4 %collective-permute-start.5 = (bf16[1024,128]{1,0:T(8,128)(2,1)}, bf16[1024,128]{1,0:T(8,128)(2,1)S(1)}, u32[]{:S(2)}, u32[]{:S(2)}) collective-permute-start(bf16[1024,128]{1,0:T(8,128)(2,1)} %refs_3_.1), channel_id=1, source_target_pairs={{0,2},{1,3},{2,0},{3,1},{4,6},{5,7},{6,4},{7,5},{8,10},{9,11},{10,... | collective-permute-start | bytes 786440 | tf_op jit(solution)/shard_map/ppermute | solution.py:51
  8.6 11.0 %collective-permute-start = (bf16[2,64,1024]{2,1,0:T(8,128)(2,1)}, bf16[2,64,1024]{2,1,0:T(8,128)(2,1)S(1)}, u32[]{:S(2)}, u32[]{:S(2)}) collective-permute-start(bf16[2,64,1024]{2,1,0:T(8,128)(2,1)} %refs_2_.1), channel_id=1, source_target_pairs={{0,1},{1,0},{2,3},{3,2},{4,5},{5,4},{6,7},{7,6},{8,9},{9,8},{10,11... | collective-permute-start | bytes 786440 | tf_op jit(solution)/shard_map/ppermute | solution.py:51
  8.6 1.0 %copy-start = (bf16[2,128,1024]{2,1,0:T(8,128)(2,1)S(1)}, bf16[2,128,1024]{2,1,0:T(8,128)(2,1)}, u32[]{:S(2)}) copy-start(bf16[2,128,1024]{2,1,0:T(8,128)(2,1)} %refs_0_.1) | copy-start | bytes 1572868
  9.7 1.0 %copy-start.1 = (bf16[1024,256]{1,0:T(8,128)(2,1)S(1)}, bf16[1024,256]{1,0:T(8,128)(2,1)}, u32[]{:S(2)}) copy-start(bf16[1024,256]{1,0:T(8,128)(2,1)} %refs_1_.1) | copy-start | bytes 1572868
  10.7 0.9 %copy-start.2 = (bf16[1024,128]{1,0:T(8,128)(2,1)S(1)}, bf16[1024,128]{1,0:T(8,128)(2,1)}, u32[]{:S(2)}) copy-start(bf16[1024,128]{1,0:T(8,128)(2,1)} %refs_3_.1) | copy-start | bytes 786436
  11.7 0.9 %copy-start.3 = (bf16[2,64,1024]{2,1,0:T(8,128)(2,1)S(1)}, bf16[2,64,1024]{2,1,0:T(8,128)(2,1)}, u32[]{:S(2)}) copy-start(bf16[2,64,1024]{2,1,0:T(8,128)(2,1)} %refs_2_.1) | copy-start | bytes 786436
  17.4 12.5 %collective-permute-start.11 = (bf16[512,512]{1,0:T(8,128)(2,1)S(1)}, bf16[512,512]{1,0:T(8,128)(2,1)S(1)}, u32[]{:S(2)}, u32[]{:S(2)}) collective-permute-start(bf16[512,512]{1,0:T(8,128)(2,1)S(1)} %shard_map.47.g0), channel_id=1, source_target_pairs={{0,16},{8,24},{16,0},{24,8},{1,17},{9,25},{17,1},{25,9},{2,18},{10... | collective-permute-start | bytes 1572872 | tf_op jit(solution)/shard_map/ppermute | solution.py:51
  17.7 12.5 %collective-permute-start.12 = (bf16[512,512]{1,0:T(8,128)(2,1)S(1)}, bf16[512,512]{1,0:T(8,128)(2,1)S(1)}, u32[]{:S(2)}, u32[]{:S(2)}) collective-permute-start(bf16[512,512]{1,0:T(8,128)(2,1)S(1)} %shard_map.47.g0), channel_id=1, source_target_pairs={{0,8},{8,0},{16,24},{24,16},{1,9},{9,1},{17,25},{25,17},{2,10},{10... | collective-permute-start | bytes 1572872 | tf_op jit(solution)/shard_map/ppermute | solution.py:51
  19.4 1.5 %collective-permute-start.4 = (bf16[2,64,1024]{2,1,0:T(8,128)(2,1)S(1)}, bf16[2,64,1024]{2,1,0:T(8,128)(2,1)S(1)}, u32[]{:S(2)}, u32[]{:S(2)}) collective-permute-start(bf16[2,64,1024]{2,1,0:T(8,128)(2,1)S(1)} %collective-permute-done.1.near_ref), channel_id=1, source_target_pairs={{0,1},{1,0},{2,3},{3,2},{4,5},{5,4},{6,7},{7,6},{8,9},{9,8},{10,11... | collective-permute-start | bytes 786440 | tf_op jit(solution)/shard_map/ppermute | solution.py:51
  21.5 15.0 %collective-permute-start.7 = (bf16[256,512]{1,0:T(8,128)(2,1)S(1)}, bf16[256,512]{1,0:T(8,128)(2,1)S(1)}, u32[]{:S(2)}, u32[]{:S(2)}) collective-permute-start(bf16[256,512]{1,0:T(8,128)(2,1)S(1)} %shard_map.49.t0), channel_id=1, source_target_pairs={{0,4},{1,5},{2,6},{3,7},{4,0},{5,1},{6,2},{7,3},{8,12},{9,13},{10,... | collective-permute-start | bytes 786440 | tf_op jit(solution)/shard_map/ppermute | solution.py:51
  24.1 12.6 %collective-permute-start.6 = (bf16[256,512]{1,0:T(8,128)(2,1)S(1)}, bf16[256,512]{1,0:T(8,128)(2,1)S(1)}, u32[]{:S(2)}, u32[]{:S(2)}) collective-permute-start(bf16[256,512]{1,0:T(8,128)(2,1)S(1)} %shard_map.49.t0), channel_id=1, source_target_pairs={{0,2},{1,3},{2,0},{3,1},{4,6},{5,7},{6,4},{7,5},{8,10},{9,11},{10,... | collective-permute-start | bytes 786440 | tf_op jit(solution)/shard_map/ppermute | solution.py:51
  25.7 13.0 %collective-permute-start.8 = (bf16[256,512]{1,0:T(8,128)(2,1)S(1)}, bf16[256,512]{1,0:T(8,128)(2,1)S(1)}, u32[]{:S(2)}, u32[]{:S(2)}) collective-permute-start(bf16[256,512]{1,0:T(8,128)(2,1)S(1)} %shard_map.49.t0), channel_id=1, source_target_pairs={{0,1},{1,0},{2,3},{3,2},{4,5},{5,4},{6,7},{7,6},{8,9},{9,8},{10,11... | collective-permute-start | bytes 786440 | tf_op jit(solution)/shard_map/ppermute | solution.py:51
  30.3 9.2 %collective-permute-start.13 = (bf16[512,512]{1,0:T(8,128)(2,1)S(1)}, bf16[512,512]{1,0:T(8,128)(2,1)S(1)}, u32[]{:S(2)}, u32[]{:S(2)}) collective-permute-start(bf16[512,512]{1,0:T(8,128)(2,1)S(1)} %shard_map.51), channel_id=1, source_target_pairs={{0,8},{8,0},{16,24},{24,16},{1,17},{9,25},{17,1},{25,9},{2,10},{10... | collective-permute-start | bytes 1572872 | tf_op jit(solution)/shard_map/ppermute | solution.py:301
  36.7 2.0 %collective-permute-start.10 = (bf16[256,512]{1,0:T(8,128)(2,1)S(1)}, bf16[256,512]{1,0:T(8,128)(2,1)S(1)}, u32[]{:S(2)}, u32[]{:S(2)}) collective-permute-start(bf16[256,512]{1,0:T(8,128)(2,1)S(1)} %collective-permute-done.6.t2), channel_id=1, source_target_pairs={{0,1},{1,0},{2,3},{3,2},{4,5},{5,4},{6,7},{7,6},{8,9},{9,8},{10,11... | collective-permute-start | bytes 786440 | tf_op jit(solution)/shard_map/ppermute | solution.py:51
  36.7 2.0 %collective-permute-start.9 = (bf16[256,512]{1,0:T(8,128)(2,1)S(1)}, bf16[256,512]{1,0:T(8,128)(2,1)S(1)}, u32[]{:S(2)}, u32[]{:S(2)}) collective-permute-start(bf16[256,512]{1,0:T(8,128)(2,1)S(1)} %shard_map.50.t1), channel_id=1, source_target_pairs={{0,1},{1,0},{2,3},{3,2},{4,5},{5,4},{6,7},{7,6},{8,9},{9,8},{10,11... | collective-permute-start | bytes 786440 | tf_op jit(solution)/shard_map/ppermute | solution.py:51
  37.2 8.2 %collective-permute-start.14 = (bf16[256,512]{1,0:T(8,128)(2,1)S(1)}, bf16[256,512]{1,0:T(8,128)(2,1)S(1)}, u32[]{:S(2)}, u32[]{:S(2)}) collective-permute-start(bf16[256,512]{1,0:T(8,128)(2,1)S(1)} %shard_map.50.t1), channel_id=1, source_target_pairs={{0,2},{1,3},{2,0},{3,1},{4,6},{5,7},{6,4},{7,5},{8,10},{9,11},{10,... | collective-permute-start | bytes 786440 | tf_op jit(solution)/shard_map/ppermute | solution.py:51
  45.5 1.6 %collective-permute-start.15 = (bf16[256,512]{1,0:T(8,128)(2,1)S(1)}, bf16[256,512]{1,0:T(8,128)(2,1)S(1)}, u32[]{:S(2)}, u32[]{:S(2)}) collective-permute-start(bf16[256,512]{1,0:T(8,128)(2,1)S(1)} %shard_map.53.t3), channel_id=1, source_target_pairs={{0,1},{1,0},{2,3},{3,2},{4,5},{5,4},{6,7},{7,6},{8,9},{9,8},{10,11... | collective-permute-start | bytes 786440 | tf_op jit(solution)/shard_map/ppermute | solution.py:51
